TPU v7x, 32 devices: a whole 2x2x4 slice. The times are simulated.
32 devices in a mesh: lon: 4 (over z), lat: 4 (over y, core), lev: 2 (over x).
Axes of the slice: x: 2, y: 2, z: 4, core: 2. Of those that a mesh axis runs over, the one named last changes fastest.
Arguments:
- state: float32 [5, 16, 64, 2048], P(None, 'lev', 'lat', 'lon'), may hold values from -6 to 6
- mask: int32 [16, 64, 2048], P('lev', 'lat', 'lon'), may hold values 0 or 1
- coriolis: float32 [64], P('lat'), may hold values from 0.05 to 0.3
- penetration: float32 [16], P('lev'), may hold values from 0.05 to 1
- flux_tiles: float32 [2048, 3, 512], P(('lon', 'lat')), may hold values from -4 to 4
- flux_owner: int32 [2048, 1], P(('lon', 'lat')), may hold values from 0 to 15; in each aligned block of 128 rows (0 to 127, 128 to 255, ...) at most 16 rows name the same one
- flux_row: int32 [2048], P(('lon', 'lat')), may hold values from 0 to 15
- fold_partner: int32 [2048], replicated, may hold values from 0 to 2047, as said below
Outputs:
- new_state: float32 [5, 16, 64, 2048], P(None, 'lev', 'lat', 'lon')
Inputs may be any that keep to these rules, and one draw needn't show every extreme that they name: `flux_owner`: among the 128 tiles of one device at most 16 name the same owner, and some owner receives exactly 16 from some device. fold_partner[i] = (h - i) mod 2048 for one hinge column h.
All inputs are finite; a program needn't handle non-finite values. No bound on the sum of `mask` on one device may be relied on, other than what follows from the above.
Results may differ from a plain program's by a relative error of at most 0.0003.
Values sent between devices are 32-bit elements; how exact they have to be, the bound alone decides.
No kernel may reach another device: no remote copies, remote signals or barrier semaphores. Data moves between devices by JAX's collectives and lax.ppermute only.
A program may use at most 192 MiB of HBM per device.

v0:
```python
import functools

import jax
import jax.numpy as jnp
from jax import lax
from jax.experimental import pallas as pl
from jax.experimental.pallas import tpu as pltpu
from jax.sharding import PartitionSpec as P

ALPHA = 0.2
BETA = 0.15
PRESS = 0.1
VISCOUS = 0.1
DIFFUSE = 0.1
ADVECT = 0.1

F32 = jnp.float32
I32 = jnp.int32
LANES = 128
DEEP = 8
FAR = 64
WET = 48
ABOVE = 56
SLABS = 11
CORNERS = SLABS
VMEM_BYTES = 24 * 1024 * 1024

VMEM = pl.BlockSpec(memory_space=pltpu.VMEM)
SMEM = pl.BlockSpec(memory_space=pltpu.SMEM)
ANY = pl.BlockSpec(memory_space=pl.ANY)
HBM = pl.BlockSpec(memory_space=pltpu.HBM)


def iota(shape, dim):
    return lax.broadcasted_iota(I32, shape, dim)


def roll(value, shift, axis):
    return pltpu.roll(value, shift % value.shape[axis], axis)


def call(kernel, out_shape, in_specs, args, scratch=(), name=None, out_specs=None, aliases=None):
    return pl.pallas_call(
        kernel,
        out_shape=out_shape,
        in_specs=in_specs,
        out_specs=out_specs or jax.tree.map(lambda _: VMEM, out_shape),
        input_output_aliases=aliases or {},
        scratch_shapes=list(scratch),
        compiler_params=pltpu.CompilerParams(vmem_limit_bytes=VMEM_BYTES),
        name=name,
    )(*args)


def after(values, *others):
    return lax.optimization_barrier((values, others))[0]


def shape(*dims):
    return pltpu.VMEM(dims, F32)


def in_hbm(*arrays):
    return tuple(pltpu.with_memory_space_constraint(array, pltpu.HBM) for array in arrays)


def prepare_kernel(
    n_lon, n_lat, state_hbm, mask_hbm, tiles_hbm, owner_hbm, row_hbm, partner_hbm, keep_ref, send_ref, west_ref, east_ref,
    total_ref, state_ref, mask_ref, x_ref, owners_ref, rows_ref, hinge_ref, sem,
):
    tiles, cols = tiles_hbm.shape[1], tiles_hbm.shape[2]
    half_cols = cols // 2
    rows = 2 * DEEP
    n_y = n_lat // 2
    half = lax.axis_index("lev")
    lat = lax.axis_index("lat")
    core = lax.rem(lat, 2)
    begin = pl.multiple_of(half * half_cols, LANES)
    indices = [
        pltpu.make_async_copy(owner_hbm, owners_ref, sem.at[0]),
        pltpu.make_async_copy(row_hbm, rows_ref, sem.at[1]),
        pltpu.make_async_copy(partner_hbm, hinge_ref, sem.at[2]),
    ]
    fluxes = [
        pltpu.make_async_copy(
            tiles_hbm.at[c, :, pl.ds(begin, half_cols)], x_ref.at[:, pl.ds(c * half_cols, half_cols)], sem.at[3 + c]
        )
        for c in range(3)
    ]
    fields = [
        pltpu.make_async_copy(state_hbm, state_ref, sem.at[6]),
        pltpu.make_async_copy(mask_hbm, mask_ref, sem.at[7]),
    ]
    for copy in indices + fluxes + fields:
        copy.start()
    for copy in indices:
        copy.wait()

    key = owners_ref[...] * rows + rows_ref[...]
    hinge_block = hinge_ref[0] // cols
    slots = keep_ref.shape[0]
    slot = iota((slots, tiles), 0)
    group, sub = slot >> 3, slot & 7
    at_y = (group >> (n_lon.bit_length() - 1)) ^ (lat // 2)
    at_lon = (group & (n_lon - 1)) ^ lax.axis_index("lon")

    def wrapped(lon):
        return jnp.where(lon < 0, lon + n_lon, jnp.where(lon >= n_lon, lon - n_lon, lon))

    def one_hot(hit):
        return jnp.where(hit, 1.0, 0.0).astype(jnp.bfloat16)

    def weights(to_core):
        lat = 2 * at_y + to_core
        owner = at_lon * n_lat + lat
        last = lat == n_lat - 1
        top = n_lat * rows - 1
        south = jnp.where(lat == 0, owner * rows, owner * rows - 1)
        north = jnp.where(last, wrapped(hinge_block - at_lon) * (n_lat * rows) + top, (owner + 1) * rows)
        third = jnp.where(last, wrapped(hinge_block - at_lon - 1) * (n_lat * rows) + top, -1)
        kind = sub >> 1
        extra_key = jnp.where(kind == 0, south, jnp.where(kind == 1, north, jnp.where(kind == 2, third, -1)))
        extra = key == extra_key
        beside = wrapped(at_lon + 1 - 2 * half) * n_lat + lat
        return (
            one_hot(key == owner * rows + sub),
            one_hot(key == owner * rows + DEEP + sub),
            one_hot(extra & ((sub & 1) == 0)),
            one_hot(extra & ((sub & 1) == 1)),
            one_hot(((key >> 4) == beside) & (sub == 6)),
        )

    def split(x):
        first = x.astype(jnp.bfloat16)
        rest = x - first.astype(F32)
        second = rest.astype(jnp.bfloat16)
        third = (rest - second.astype(F32)).astype(jnp.bfloat16)
        return first, second, third

    square = iota((tiles, tiles), 0) == iota((tiles, tiles), 1)
    row_of = jnp.sum(jnp.where(square, (key & (rows - 1)).astype(F32), 0.0), axis=1, keepdims=True).astype(I32)

    for copy in fluxes:
        copy.wait()
    x = x_ref[...]
    lane = iota((tiles, LANES), 1)
    edge = jnp.zeros((tiles, LANES), F32)
    for c in range(3):
        begin = c * half_cols
        value = jnp.where(half == 0, x[:, begin : begin + 1], x[:, begin + half_cols - 1 : begin + half_cols])
        edge = jnp.where(((lane >> 4) == c) & ((lane & 15) == row_of), value, edge)
    parts, edges = split(x), split(edge)
    wide = 3 * half_cols
    quarter = wide // 2

    def dot(hot, terms, begin, end):
        products = [
            jnp.dot(hot, term[:, begin:end], preferred_element_type=F32) for term in reversed(terms)
        ]
        return products[0] + products[1] + products[2]

    for out_ref, to_core in ((keep_ref, core), (send_ref, 1 - core)):
        low, high, even, odd, ring = weights(to_core)
        out_ref[:, 0:wide] = dot(low, parts, 0, wide)
        out_ref[:, wide : 2 * wide] = dot(high, parts, 0, wide)
        rest = dot(even, parts, 0, quarter) + dot(odd, parts, quarter, wide)
        beside = dot(ring, edges, 0, LANES)
        out_ref[:, 2 * wide : 2 * wide + LANES] = rest[:, 0:LANES] + beside
        out_ref[:, 2 * wide + LANES :] = rest[:, LANES:]

    for copy in fields:
        copy.wait()
    total = jnp.zeros(total_ref.shape, F32)
    for k in range(DEEP):
        at = slice(k * rows, (k + 1) * rows)
        total = total + buoyancy_of(state_ref[2, at, :], state_ref[3, at, :])
    total_ref[...] = total
    edge_columns(state_ref, mask_ref, west_ref, east_ref)


def merge_kernel(kept_ref, got_ref, keep_ref, send_ref):
    half = keep_ref.shape[0]
    send_ref[...] = kept_ref[half:, :] + got_ref[half:, :]
    keep_ref[...] = kept_ref[0:half, :] + got_ref[0:half, :]


def prepare(state, mask, flux_tiles, flux_owner, flux_row, fold_partner, n_lon, n_lat):
    tiles, _, cols = flux_tiles.shape
    wide = 3 * (cols // 2)
    slots = shape(n_lon * n_lat // 2 * DEEP, 2 * wide + wide // 2)
    side = shape(2 * DEEP, LANES)
    return call(
        functools.partial(prepare_kernel, n_lon, n_lat),
        (slots, slots, side, side, shape(2 * DEEP, cols)),
        [HBM] * 6,
        in_hbm(
            state,
            mask,
            flux_tiles.transpose(1, 0, 2),
            flux_owner.reshape(1, tiles),
            flux_row.reshape(1, tiles),
            fold_partner,
        ),
        [
            pltpu.VMEM(state.shape, F32),
            pltpu.VMEM(mask.shape, I32),
            pltpu.VMEM((tiles, wide), F32),
            pltpu.VMEM((1, tiles), I32),
            pltpu.VMEM((1, tiles), I32),
            pltpu.SMEM(fold_partner.shape, I32),
            pltpu.SemaphoreType.DMA((8,)),
        ],
        name="prepare",
    )


def level_rows(ref, row, rows):
    return jnp.concatenate([ref[k * rows + row : k * rows + row + 1, :] for k in range(DEEP)], axis=0)


def buoyancy_of(temper, saline):
    return ALPHA * temper - BETA * saline


def edge_rows(state_ref, mask_ref, out_ref, rows, near, far):
    for f in range(5):
        out_ref[2 * f] = level_rows(state_ref.at[f], near, rows)
        out_ref[2 * f + 1] = level_rows(state_ref.at[f], far, rows)
    out_ref[10] = level_rows(mask_ref, near, rows).astype(F32)


def edge_columns(state_ref, mask_ref, west_ref, east_ref):
    rows, cols = west_ref.shape[0], state_ref.shape[2]
    lane = iota((rows, LANES), 1)
    last = slice(cols - LANES, cols)
    west = jnp.zeros((rows, LANES), F32)
    east = jnp.zeros((rows, LANES), F32)
    for k in range(DEEP):
        at = slice(k * rows, (k + 1) * rows)
        for f in range(5):
            to = f * DEEP + k
            left, right = state_ref[f, at, 0:LANES], state_ref[f, at, last]
            west = jnp.where(lane == to, roll(left, to, 1), west)
            west = jnp.where(lane == FAR + to, roll(left, FAR + to - 1, 1), west)
            east = jnp.where(lane == to, roll(right, to + 1, 1), east)
            east = jnp.where(lane == FAR + to, roll(right, FAR + to + 2, 1), east)
        west = jnp.where(lane == WET + k, roll(mask_ref[at, 0:LANES].astype(F32), WET + k, 1), west)
        east = jnp.where(lane == WET + k, roll(mask_ref[at, last].astype(F32), WET + k + 1, 1), east)
    west_ref[...] = west
    east_ref[...] = east


def top_kernel(state_ref, mask_ref, prefix_ref, top_ref):
    rows, cols = prefix_ref.shape
    for slab in range(SLABS):
        if slab < 10:
            line = level_rows(state_ref.at[slab // 2], rows - 1 - slab % 2, rows)
        else:
            line = level_rows(mask_ref, rows - 1, rows).astype(F32)
        for piece in range(cols // LANES):
            top_ref[piece, slab] = line[:, piece * LANES : (piece + 1) * LANES]
    top_ref[:, CORNERS] = jnp.zeros((cols // LANES, DEEP, LANES), F32)
    for n in (1, 2):
        for piece in range(cols // LANES):
            top_ref[piece, CORNERS, 2 + n : 3 + n, :] = prefix_ref[rows - n : rows - n + 1, piece * LANES : (piece + 1) * LANES]


def columns_kernel(n_lat, west_ref, east_ref, prefix_ref, fold_ref, partner_ref, west_out_ref, east_out_ref):
    rows, cols = prefix_ref.shape
    lane = iota((rows, LANES), 1)
    for side, in_ref, out_ref in ((0, west_ref, west_out_ref), (1, east_ref, east_out_ref)):
        near, far = (0, 1) if side == 0 else (cols - 1, cols - 2)
        value = jnp.where(lane == ABOVE, prefix_ref[:, near : near + 1], in_ref[...])
        out_ref[0:rows, :] = jnp.where(lane == FAR + ABOVE, prefix_ref[:, far : far + 1], value)
        out_ref[rows:, :] = jnp.zeros((DEEP, LANES), F32)

    @pl.when(lax.axis_index("lat") == n_lat - 1)
    def _():
        within = partner_ref[0] & (LANES - 1)
        sub8, lane8 = iota((DEEP, LANES), 0), iota((DEEP, LANES), 1)
        col = iota((DEEP, cols + LANES), 1)
        for place, out_ref in ((cols + within, west_out_ref), (within + 1, east_out_ref)):
            line = jnp.zeros((DEEP, LANES), F32)
            for slab in (0, 2, 4, 6, 8, CORNERS):
                line_there = jnp.concatenate([fold_ref[piece, slab] for piece in range(fold_ref.shape[0])], axis=1)
                cell = jnp.sum(jnp.where(col == place, line_there, 0.0), axis=1, keepdims=True)
                here = (lane8 == ABOVE) & (sub8 == 3) if slab == CORNERS else lane8 == (slab // 2) * DEEP + sub8
                line = jnp.where(here, -cell if slab < 4 else cell, line)
            out_ref[rows : rows + 1, :] = jnp.sum(line, axis=0, keepdims=True)


def corner_slab(out_ref, prefix_ref, turn_ref, from_west_ref, from_east_ref, near, far):
    out_ref[CORNERS] = jnp.full(out_ref.shape[1:], turn_ref[near], F32)
    out_ref[CORNERS, 0:1, 0:LANES] = from_west_ref[near : near + 1, :]
    out_ref[CORNERS, 1:2, 0:LANES] = from_east_ref[near : near + 1, :]
    out_ref[CORNERS, 3:4, :] = prefix_ref[near : near + 1, :]
    out_ref[CORNERS, 4:5, :] = prefix_ref[far : far + 1, :]


def rows_kernel(state_ref, mask_ref, prefix_ref, turn_ref, from_west_ref, from_east_ref, pair_ref, cross_ref):
    rows = prefix_ref.shape[0]
    odd = lax.rem(lax.axis_index("lat"), 2) == 1

    def fill(out_ref, near, far):
        edge_rows(state_ref, mask_ref, out_ref, rows, near, far)
        corner_slab(out_ref, prefix_ref, turn_ref, from_west_ref, from_east_ref, near, far)

    @pl.when(odd)
    def _():
        fill(pair_ref, 0, 1)
        fill(cross_ref, rows - 1, rows - 2)

    @pl.when(jnp.logical_not(odd))
    def _():
        fill(pair_ref, rows - 1, rows - 2)
        fill(cross_ref, 0, 1)


def around(value, west, east, south, north):
    rows, cols = value.shape
    row, col = iota((rows, cols), 0), iota((rows, cols), 1)
    return (
        jnp.where(col == cols - 1, east, roll(value, -1, 1)),
        jnp.where(col == 0, west, roll(value, 1, 1)),
        jnp.where(row == rows - 1, north, roll(value, -1, 0)),
        jnp.where(row == 0, south, roll(value, 1, 0)),
    )


def advanced(values, sides, wet, turn, pressed, heat=None):
    zonal, merid = values[0], values[1]
    sums = [(e + w) + (n + s) for e, w, n, s in sides]
    across = [(e - w, n - s) for e, w, n, s in sides]
    press_x, press_y = pressed(
        0.5 * buoyancy_of(across[2][0], across[3][0]), 0.5 * buoyancy_of(across[2][1], across[3][1])
    )
    out = []
    carry_x, carry_y = (0.5 * ADVECT) * zonal, (0.5 * ADVECT) * merid
    for f in range(5):
        spread = (VISCOUS if f < 2 else DIFFUSE) * (sums[f] - 4.0 * values[f])
        if f == 0:
            trend = spread + (turn * merid - press_x)
        elif f == 1:
            trend = spread - (turn * zonal + press_y)
        else:
            trend = spread - (carry_x * across[f][0] + carry_y * across[f][1])
        new = values[f] + wet * trend
        out.append(new if heat is None or f < 2 else new + heat[f - 2])
    return out


class Tiles:
    def __init__(self, grid, west=None, east=None, south=None, north=None):
        self.grid, self.ghosts, self.turned = grid, (west, east, south, north), {}
        self.lane, self.sub = iota((DEEP, LANES), 1), iota((DEEP, LANES), 0)

    def rolled(self, r, j, shift, axis):
        at = (r, j, shift, axis)
        if at not in self.turned:
            self.turned[at] = roll(self.grid[r][j], shift, axis)
        return self.turned[at]

    def side(self, r, j, shift, axis):
        here = self.rolled(r, j, shift, axis)
        r_from, j_from = (r, j - shift) if axis else (r - shift, j)
        edge = (0 if shift == 1 else LANES - 1) if axis else (0 if shift == 1 else DEEP - 1)
        if 0 <= r_from < len(self.grid) and 0 <= j_from < len(self.grid[0]):
            other = self.rolled(r_from, j_from, shift, axis)
        else:
            ghost = self.ghosts[(0 if shift == 1 else 1) + (0 if axis else 2)]
            if ghost is None:
                return here
            other = ghost[r if axis else j]
        return jnp.where((self.lane if axis else self.sub) == edge, other, here)

    def around(self, r, j):
        return self.side(r, j, -1, 1), self.side(r, j, 1, 1), self.side(r, j, -1, 0), self.side(r, j, 1, 0)


def tile(r, j, k, rows):
    return slice(k * rows + r * DEEP, k * rows + (r + 1) * DEEP), slice(j * LANES, (j + 1) * LANES)


def turn_column(turn_ref, rows):
    row = iota((rows, LANES), 0)
    column = jnp.zeros((rows, LANES), F32)
    for j in range(rows):
        column = jnp.where(row == j, turn_ref[j], column)
    return column


def mirrored(value, width):
    back = LANES - 1 - iota((value.shape[0], LANES), 1)
    blocks = [
        jnp.take_along_axis(value[:, begin : begin + LANES], back, axis=1)
        for begin in range(width - LANES, -1, -LANES)
    ]
    return jnp.concatenate(blocks, axis=1)


def scan_down(value):
    row = iota(value.shape, 0)
    for step in (1, 2, 4):
        value = value + jnp.where(row >= step, roll(value, step, 0), 0.0)
    return value


def scan_lanes(value):
    lane = iota(value.shape, 1) & 7
    for step in (1, 2, 4):
        value = value + jnp.where(lane >= step, roll(value, step, 1), 0.0)
    return value


def lanes_between(value, begin, end):
    lane = iota(value.shape, 1)
    return jnp.where((lane >= begin) & (lane < end), value, 0.0)


def buoyancy_sum(column):
    here = lanes_between(buoyancy_of(roll(column, -16, 1), roll(column, -24, 1)), 0, 8)
    return jnp.sum(here, axis=1, keepdims=True)


def inside_kernel(state_ref, mask_ref, prefix_ref, turn_ref, share_ref, new_ref, sums_ref):
    rows, cols = prefix_ref.shape
    n_r, n_j = rows // DEEP, cols // LANES
    turn = turn_column(turn_ref, rows)
    grid = [(r, j) for r in range(n_r) for j in range(n_j)]
    zero = jnp.zeros((DEEP, LANES), F32)
    prefix = Tiles([[prefix_ref[tile(r, j, 0, rows)] for j in range(n_j)] for r in range(n_r)])
    run = {}
    for at in grid:
        east, west, north, south = prefix.around(*at)
        run[at] = [0.5 * (east - west), 0.5 * (north - south), zero, zero]
    for k in range(DEEP):
        fields = [Tiles([[state_ref[(f, *tile(r, j, k, rows))] for j in range(n_j)] for r in range(n_r)]) for f in range(5)]
        for r, j in grid:
            at = tile(r, j, k, rows)
            above_x, above_y, total, absorbed = run[r, j]
            slopes = []

            def pressed(x, y):
                slopes.extend((x, y))
                return PRESS * (above_x + 0.5 * x), PRESS * (above_y + 0.5 * y)

            values = [field.grid[r][j] for field in fields]
            wet = mask_ref[at].astype(F32)
            new = advanced(
                values, [field.around(r, j) for field in fields], wet, turn[r * DEEP : (r + 1) * DEEP, 0:1], pressed
            )
            for f in range(5):
                new_ref[(f, *at)] = new[f]
            run[r, j] = [
                above_x + slopes[0],
                above_y + slopes[1],
                total + buoyancy_of(new[2], new[3]),
                absorbed + wet * share_ref[k],
            ]
    for r, j in grid:
        for kind in range(2):
            at = slice(kind * cols + j * LANES, kind * cols + (j + 1) * LANES)
            sums_ref[r * DEEP : (r + 1) * DEEP, at] = run[r, j][2 + kind]


def rim_kernel(
    n_lat, state_ref, mask_ref, prefix_ref, turn_ref, share_ref, partner_ref, own_west_ref, own_east_ref,
    from_west_ref, from_east_ref, pair_ref, cross_ref, fold_ref, inside_ref, ring_rows_ref, ring_cols_ref,
    edge_rows_ref, edge_cols_ref, sums_ref, south_ref, north_ref,
):
    rows, cols = prefix_ref.shape
    lat = lax.axis_index("lat")
    odd = lax.rem(lat, 2) == 1
    within = partner_ref[0] & (LANES - 1)
    at_top = lat == n_lat - 1

    @pl.when(odd)
    def _():
        south_ref[...] = pair_ref[...]

    @pl.when(jnp.logical_not(odd))
    def _():
        north_ref[...] = pair_ref[...]

    @pl.when(jnp.logical_not(odd) & (lat > 0))
    def _():
        south_ref[...] = cross_ref[...]

    @pl.when(odd & (lat < n_lat - 1))
    def _():
        north_ref[...] = cross_ref[...]

    @pl.when(lat == 0)
    def _():
        edge_rows(state_ref, mask_ref, south_ref, rows, 0, 0)
        corner_slab(south_ref, prefix_ref, turn_ref, from_west_ref, from_east_ref, 0, 0)

    sub8, lane8 = iota((DEEP, LANES), 0), iota((DEEP, LANES), 1)

    @pl.when(at_top)
    def _():
        for slab in range(SLABS + 1):
            row = jnp.concatenate([fold_ref[piece, slab] for piece in range(fold_ref.shape[0])], axis=1)
            row = pltpu.roll(row, cols + LANES - 1 - within, 1)
            if slab < 4:
                row = -row
            north_ref[slab] = mirrored(row, cols)
        north_ref[CORNERS, 0:1, 0:LANES] = from_west_ref[rows : rows + 1, :]
        north_ref[CORNERS, 1:2, 0:LANES] = from_east_ref[rows : rows + 1, :]
        north_ref[CORNERS, 2:3, :] = jnp.full((1, cols), turn_ref[rows - 1], F32)

    wide = cols + LANES
    sums_ref[rows:, :] = jnp.zeros((DEEP, 2 * wide), F32)
    for kind in range(2):
        sums_ref[0:rows, kind * wide : kind * wide + cols] = inside_ref[:, kind * cols : (kind + 1) * cols]

    share_down = jnp.zeros((DEEP, LANES), F32)
    for k in range(DEEP):
        share_down = jnp.where(sub8 == k, share_ref[k], share_down)

    def down(line, f):
        return jnp.sum(jnp.where(lane8 == f * DEEP + sub8, line, 0.0), axis=1, keepdims=True)

    def row_step(near, south, north, west_line, east_line, wet, turn, above, above_south, above_north):
        col = iota((DEEP, cols), 1)
        sides = [
            (
                jnp.where(col == cols - 1, down(east_line, f), roll(near[f], -1, 1)),
                jnp.where(col == 0, down(west_line, f), roll(near[f], 1, 1)),
                north[f],
                south[f],
            )
            for f in range(5)
        ]
        east = jnp.where(col[0:1] == cols - 1, east_line[:, ABOVE : ABOVE + 1], roll(above, -1, 1))
        west = jnp.where(col[0:1] == 0, west_line[:, ABOVE : ABOVE + 1], roll(above, 1, 1))
        above_x, above_y = 0.5 * (east - west), 0.5 * (above_north - above_south)

        def pressed(x, y):
            return PRESS * (above_x + scan_down(x) - 0.5 * x), PRESS * (above_y + scan_down(y) - 0.5 * y)

        return advanced(near, sides, wet, turn, pressed)

    for side, ghost_ref, edge, inner in ((0, south_ref, 0, 1), (1, north_ref, rows - 1, rows - 2)):
        near = [ghost_ref[2 * f] for f in range(5)]
        far = [ghost_ref[2 * f + 1] for f in range(5)]
        own = [level_rows(state_ref.at[f], edge, rows) for f in range(5)]
        own_next = [level_rows(state_ref.at[f], inner, rows) for f in range(5)]
        ring_wet = ghost_ref[10]
        corners = ghost_ref[CORNERS, :, 0:LANES]
        above_near, above_far = ghost_ref[CORNERS, 3:4, :], ghost_ref[CORNERS, 4:5, :]
        above_own, above_next = prefix_ref[edge : edge + 1, :], prefix_ref[inner : inner + 1, :]
        outward, inward = (far, above_far), (own, above_own)
        (south, above_south), (north, above_north) = (outward, inward) if side == 0 else (inward, outward)
        ring = row_step(
            near, south, north, corners[0:1, :], corners[1:2, :], ring_wet, corners[2:3, 0:1], above_near, above_south, above_north
        )
        outward, inward = (near, above_near), (own_next, above_next)
        (south, above_south), (north, above_north) = (outward, inward) if side == 0 else (inward, outward)
        wet = level_rows(mask_ref, edge, rows).astype(F32)
        edge_line = slice(edge, edge + 1)
        new = row_step(
            own, south, north, from_west_ref[edge_line, :], from_east_ref[edge_line, :], wet, turn_ref[edge],
            above_own, above_south, above_north,
        )
        for f in range(5):
            edge_rows_ref[side, f] = new[f]
            ring_rows_ref[side, f] = jnp.where(lat == 0, new[f], ring[f]) if side == 0 else ring[f]
        ring_rows_ref[side, 5] = ring_wet
        at = slice(rows + side, rows + side + 1)
        here = buoyancy_of(ring_rows_ref[side, 2], ring_rows_ref[side, 3])
        sums_ref[at, 0:cols] = jnp.sum(here, axis=0, keepdims=True)
        sums_ref[at, wide : wide + cols] = jnp.sum(ring_wet * share_down[:, 0:1], axis=0, keepdims=True)

    row, lane = iota((rows, LANES), 0), iota((rows, LANES), 1)
    turn = turn_column(turn_ref, rows)
    share_lanes = jnp.zeros((rows, LANES), F32)
    for k in range(DEEP):
        share_lanes = jnp.where((lane & 7) == k, share_ref[k], share_lanes)

    def column_step(near, east, west, north, south):
        dx, dy = 0.5 * (east - west), 0.5 * (north - south)
        lap = (east + west) + (north + south) - 4.0 * near
        zonal, merid = lanes_between(near, 0, 8), lanes_between(near, 8, 16)
        wet = lanes_between(near, WET, WET + 8)
        wet_all = sum(roll(wet, -8 * n, 1) for n in range(2, 7))
        zonal_all = sum(roll(zonal, 8 * n, 1) for n in (2, 3, 4))
        merid_all = sum(roll(merid, 8 * n, 1) for n in (1, 2, 3))
        bx = lanes_between(buoyancy_of(roll(dx, -16, 1), roll(dx, -24, 1)), 0, 8)
        by = lanes_between(buoyancy_of(roll(dy, -8, 1), roll(dy, -16, 1)), 8, 16)
        press_x = lanes_between(PRESS * (dx[:, ABOVE : ABOVE + 1] + scan_lanes(bx) - 0.5 * bx), 0, 8)
        press_y = lanes_between(PRESS * (dy[:, ABOVE : ABOVE + 1] + scan_lanes(by) - 0.5 * by), 8, 16)
        trend = VISCOUS * lap - ADVECT * (zonal_all * dx + merid_all * dy) - press_x - press_y
        trend = trend + lanes_between(turn * roll(near, -8, 1), 0, 8) - lanes_between(turn * roll(near, 8, 1), 8, 16)
        return near + wet_all * trend, wet

    blocks = [jnp.zeros((rows, LANES), F32)] * 2
    sides = ((0, from_west_ref, own_west_ref), (1, from_east_ref, own_east_ref))
    for side, ghost_ref, own_ref in sides:
        near, own = ghost_ref[0:rows, :], own_ref[0:rows, :]
        far, own_next = roll(near, -FAR, 1), roll(own, -FAR, 1)
        north = jnp.where(row == rows - 1, north_ref[CORNERS, side : side + 1, 0:LANES], roll(near, -1, 0))
        south = jnp.where(row == 0, south_ref[CORNERS, side : side + 1, 0:LANES], roll(near, 1, 0))
        east, west = (own, far) if side == 0 else (far, own)
        new, wet = column_step(near, east, west, north, south)
        ring_cols_ref[side] = new
        blocks[0] = jnp.where(lane == side, buoyancy_sum(new), blocks[0])
        blocks[1] = jnp.where(lane == side, jnp.sum(wet * share_lanes, axis=1, keepdims=True), blocks[1])
        east, west = (own_next, near) if side == 0 else (near, own_next)
        new, _ = column_step(own, east, west, roll(own, -1, 0), roll(own, 1, 0))
        edge_cols_ref[side] = new
        column = 0 if side == 0 else cols - 1
        sums_ref[0:rows, column : column + 1] = buoyancy_sum(new)
    for kind in range(2):
        sums_ref[0:rows, kind * wide + cols : (kind + 1) * wide] = blocks[kind]
    for side, edge in ((0, 0), (1, rows - 1)):
        here = buoyancy_of(edge_rows_ref[side, 2], edge_rows_ref[side, 3])
        sums_ref[edge : edge + 1, 0:cols] = jnp.sum(here, axis=0, keepdims=True)


def flux_kernel(n_lat, sums_ref, mine_ref, theirs_ref, partner_ref, flux_ref, flux_rows_ref, flux_cols_ref, above_ref):
    rows, cols = flux_ref.shape[1:]
    half_cols = cols // 2
    wide = 3 * half_cols
    mine, theirs = mine_ref[...], theirs_ref[...]
    first = lax.axis_index("lev") == 0
    halves = (jnp.where(first, mine, theirs), jnp.where(first, theirs, mine))
    at_top = lax.axis_index("lat") == n_lat - 1
    hinge = partner_ref[0]
    within = hinge - (hinge // cols) * cols

    def extra(kind, c):
        found = []
        for part in halves:
            line = jnp.concatenate(
                [part[2 * kind : 2 * kind + 1, 2 * wide :], part[2 * kind + 1 : 2 * kind + 2, 2 * wide :]], axis=1
            )
            found.append(line[:, c * half_cols : (c + 1) * half_cols])
        return jnp.concatenate(found, axis=1)

    flux, flux_south, flux_north, flux_west, flux_east = [], [], [], [], []
    crossed = jnp.zeros((DEEP, 2 * cols), F32)
    for c in range(3):
        pair = jnp.concatenate([extra(2, c), extra(1, c)], axis=1)
        crossed = jnp.where(iota(crossed.shape, 0) == c, pair, crossed)
    crossed = mirrored(pltpu.roll(crossed, 2 * cols - 1 - within, 1), cols)
    row, lane = iota((rows, LANES), 0), iota((rows, LANES), 1)
    for c in range(3):
        bands = [
            jnp.concatenate([part[:, b * wide + c * half_cols : b * wide + (c + 1) * half_cols] for part in halves], axis=1)
            for b in range(2)
        ]
        flux.append(jnp.concatenate(bands, axis=0))
        flux_south.append(extra(0, c))
        flux_north.append(jnp.where(at_top, crossed[c : c + 1, :], extra(1, c)))
        here = lane == c * 16 + row
        for side, part in ((flux_west, halves[1]), (flux_east, halves[0])):
            line = part[6:7, 2 * wide : 2 * wide + LANES]
            side.append(jnp.sum(jnp.where(here, line, 0.0), axis=1, keepdims=True))

    flux_cols = jnp.zeros((rows, LANES), F32)
    for c in range(3):
        flux_ref[c] = flux[c]
        flux_rows_ref[c : c + 1, :] = flux_south[c]
        flux_rows_ref[3 + c : 4 + c, :] = flux_north[c]
        flux_cols = jnp.where(lane == c, flux_west[c], jnp.where(lane == 3 + c, flux_east[c], flux_cols))
    flux_rows_ref[6:8, :] = jnp.zeros((2, cols), F32)
    flux_cols_ref[...] = flux_cols
    reach = cols + LANES
    above_ref[rows:, :] = jnp.zeros((DEEP, reach), F32)
    above_ref[0:rows, 0:cols] = sums_ref[0:rows, 0:cols] + sums_ref[0:rows, reach : reach + cols] * buoyancy_of(flux[0], flux[1])
    ends = jnp.zeros((rows, LANES), F32)
    for side, column, line in ((0, (flux_west[0], flux_west[1]), flux_south), (1, (flux_east[0], flux_east[1]), flux_north)):
        at = slice(rows + side, rows + side + 1)
        above_ref[at, 0:cols] = sums_ref[at, 0:cols] + sums_ref[at, reach : reach + cols] * buoyancy_of(line[0], line[1])
        before, taken = sums_ref[0:rows, cols:reach], sums_ref[0:rows, reach + cols :]
        ends = jnp.where(lane == side, before + taken * buoyancy_of(*column), ends)
    above_ref[0:rows, cols:reach] = ends


def second_kernel(
    state_ref, mask_ref, ring_rows_ref, ring_cols_ref, edge_rows_ref, edge_cols_ref, flux_ref, flux_rows_ref,
    flux_cols_ref, turn_ref, share_ref, out_hbm, flow_ref, tracers_ref, sem,
):
    rows, cols = flux_ref.shape[1:]
    n_r, n_j = rows // DEEP, cols // LANES
    sub8, lane8 = iota((DEEP, LANES), 0), iota((DEEP, LANES), 1)
    lane = iota((rows, LANES), 1)
    turn = turn_column(turn_ref, rows)
    share_down = jnp.zeros((DEEP, LANES), F32)
    share_lanes = jnp.zeros((rows, LANES), F32)
    for k in range(DEEP):
        share_down = jnp.where(sub8 == k, share_ref[k], share_down)
        share_lanes = jnp.where((lane & 7) == k, share_ref[k], share_lanes)

    ring_rows, ring_cols = [], []
    for side in range(2):
        taken = ring_rows_ref[side, 5] * share_down[:, 0:1]
        values = [ring_rows_ref[side, f] for f in range(2)]
        values += [ring_rows_ref[side, 2 + c] + taken * flux_rows_ref[3 * side + c : 3 * side + c + 1, :] for c in range(3)]
        ring_rows.append(values)
        found = ring_cols_ref[side]
        taken = lanes_between(found, WET, WET + 8) * share_lanes
        for c in range(3):
            found = found + roll(taken, 8 * (2 + c) - WET, 1) * flux_cols_ref[:, 3 * side + c : 3 * side + c + 1]
        ring_cols.append(found)

    grid = [(r, j) for r in range(n_r) for j in range(n_j)]

    def cut(value, r, j):
        return value[r * DEEP : (r + 1) * DEEP, j * LANES : (j + 1) * LANES]

    zero = jnp.zeros((DEEP, LANES), F32)
    run = {at: (zero, zero) for at in grid}
    edge_cols = [edge_cols_ref[side] for side in range(2)]
    copies = []

    def column(value, r, n):
        return jnp.broadcast_to(value[r * DEEP : (r + 1) * DEEP, n : n + 1], (DEEP, LANES))

    for k in range(DEEP):
        wets, heats, grids = {}, {}, [[[None] * n_j for _ in range(n_r)] for _ in range(5)]
        for r, j in grid:
            at = tile(r, j, k, rows)
            wet = mask_ref[at].astype(F32)
            taken = wet * share_ref[k]
            wets[r, j] = wet
            heats[r, j] = [taken * cut(flux_ref[c], r, j) for c in range(3)]
            for f in range(5):
                value = state_ref[(f, *at)]
                if j == 0:
                    value = jnp.where(lane8 == 0, column(edge_cols[0], r, f * DEEP + k), value)
                if j == n_j - 1:
                    value = jnp.where(lane8 == LANES - 1, column(edge_cols[1], r, f * DEEP + k), value)
                if r == 0:
                    value = jnp.where(sub8 == 0, edge_rows_ref[0, f, k : k + 1, at[1]], value)
                if r == n_r - 1:
                    value = jnp.where(sub8 == DEEP - 1, edge_rows_ref[1, f, k : k + 1, at[1]], value)
                if f >= 2:
                    value = value + heats[r, j][f - 2]
                grids[f][r][j] = value
        fields = [
            Tiles(
                grids[f],
                [column(ring_cols[0], r, f * DEEP + k) for r in range(n_r)],
                [column(ring_cols[1], r, f * DEEP + k) for r in range(n_r)],
                [ring_rows[0][f][k : k + 1, j * LANES : (j + 1) * LANES] for j in range(n_j)],
                [ring_rows[1][f][k : k + 1, j * LANES : (j + 1) * LANES] for j in range(n_j)],
            )
            for f in range(5)
        ]
        for r, j in grid:
            at = tile(r, j, k, rows)
            over_x, over_y = run[r, j]

            def pressed(x, y):
                run[r, j] = (over_x + x, over_y + y)
                return PRESS * (over_x + 0.5 * x), PRESS * (over_y + 0.5 * y)

            new = advanced(
                [field.grid[r][j] for field in fields],
                [field.around(r, j) for field in fields],
                wets[r, j],
                turn[r * DEEP : (r + 1) * DEEP, 0:1],
                pressed,
                heats[r, j],
            )
            for f in range(5):
                if f < 2:
                    flow_ref[(f, *at)] = new[f]
                else:
                    tracers_ref[(f - 2, *at)] = new[f]
        whole = pl.ds(k * rows, rows)
        copies.append(
            pltpu.make_async_copy(tracers_ref.at[:, whole, :], out_hbm.at[pl.ds(2, 3), whole, :], sem.at[k])
        )
        copies[-1].start()
    for copy in copies:
        copy.wait()


def last_kernel(out_in_hbm, flow_ref, mask_ref, above_ref, out_hbm, moved_ref, sem):
    del out_in_hbm
    rows, cols = mask_ref.shape[0] // DEEP, mask_ref.shape[1]
    above = above_ref[...]
    east, west, north, south = around(
        above[0:rows, 0:cols],
        above[0:rows, cols : cols + 1],
        above[0:rows, cols + 1 : cols + 2],
        above[rows : rows + 1, 0:cols],
        above[rows + 1 : rows + 2, 0:cols],
    )
    push_x, push_y = (0.5 * PRESS) * (east - west), (0.5 * PRESS) * (north - south)
    copies = []
    for k in range(DEEP):
        whole = pl.ds(k * rows, rows)
        wet = mask_ref[whole, :].astype(F32)
        moved_ref[0, whole, :] = flow_ref[0, whole, :] - wet * push_x
        moved_ref[1, whole, :] = flow_ref[1, whole, :] - wet * push_y
        copies.append(pltpu.make_async_copy(moved_ref.at[:, whole, :], out_hbm.at[pl.ds(0, 2), whole, :], sem.at[k]))
        copies[-1].start()
    for copy in copies:
        copy.wait()


def body(n_lon, n_lat, state, mask, coriolis, penetration, flux_tiles, flux_owner, flux_row, fold_partner):
    fields, levels, rows, cols = state.shape
    flat_state = state.reshape(fields, levels * rows, cols)
    flat_mask = mask.reshape(levels * rows, cols)
    last = n_lat - 1

    keep, send, west, east, total = prepare(
        flat_state, flat_mask, flux_tiles, flux_owner, flux_row, fold_partner, n_lon, n_lat
    )

    stages = []
    for axis, size, least in (("lat", n_lat, 2), ("lon", n_lon, 1)):
        bit = size // 2
        while bit >= least:
            stages.append((axis, size, bit))
            bit //= 2
    got = lax.ppermute(send, "lat", [(i, i ^ 1) for i in range(n_lat)])
    prefix = lax.ppermute(total, "lev", [(0, 1)])

    def merged(keep, got):
        half = shape(keep.shape[0] // 2, keep.shape[1])
        return call(merge_kernel, (half, half), [VMEM] * 2, (keep, got), name="merge_flux")

    def passed_on(send, stage):
        axis, size, bit = stage
        return lax.ppermute(send, axis, [(i, i ^ bit) for i in range(size)])

    pieces = cols // LANES
    hinge_piece = fold_partner[0] >> (LANES.bit_length() - 1)
    keep = after(keep, (prefix, hinge_piece))
    keep, send = merged(keep, got)
    got = passed_on(send, stages[0])

    message = shape(SLABS + 1, DEEP, cols)
    top_shape = shape(pieces, SLABS + 1, DEEP, LANES)
    top = call(top_kernel, top_shape, [VMEM] * 3, (flat_state, flat_mask, prefix), name="top_rows")
    top = after(top, send)

    def folded(hinge_piece):
        block, piece = divmod(hinge_piece, pieces)

        def swap(rows_out):
            def across(part, other):
                pairs = [(a * n_lat + last, (other - a) % n_lon * n_lat + last) for a in range(n_lon)]
                return lax.ppermute(part, ("lon", "lat"), pairs)

            return jnp.concatenate([across(rows_out[piece:], block - 1), across(rows_out[: piece + 1], block)], axis=0)

        return swap

    fold = lax.switch(hinge_piece, [folded(n) for n in range(n_lon * pieces)], top)
    keep = after(keep, fold)
    keep, send = merged(keep, got)
    got = passed_on(send, stages[1])

    west, east = after((west, east), send)
    side = shape(rows + DEEP, LANES)
    west, east = call(
        functools.partial(columns_kernel, n_lat),
        (side, side),
        [VMEM] * 4 + [SMEM],
        (west, east, prefix, fold, fold_partner),
        name="edge_columns",
    )
    from_west = lax.ppermute(east, "lon", [(i, (i + 1) % n_lon) for i in range(n_lon)])
    from_east = lax.ppermute(west, "lon", [((i + 1) % n_lon, i) for i in range(n_lon)])
    pair, cross = call(
        rows_kernel,
        (message, message),
        [VMEM, VMEM, VMEM, SMEM, VMEM, VMEM],
        (flat_state, flat_mask, prefix, coriolis, from_west, from_east),
        name="edge_rows",
    )
    from_pair = lax.ppermute(pair, "lat", [(i, i ^ 1) for i in range(n_lat)])
    from_cross = lax.ppermute(cross, "lat", [(i, i + 1 if i % 2 else i - 1) for i in range(1, last)])
    keep = after(keep, (pair, cross))
    for stage in stages[2:]:
        keep, send = merged(keep, got)
        got = passed_on(send, stage)

    near_state, near_mask = after((flat_state, flat_mask), send)
    new_state, inside = call(
        inside_kernel,
        (shape(fields, levels * rows, cols), shape(rows, 2 * cols)),
        [VMEM, VMEM, VMEM, SMEM, SMEM],
        (near_state, near_mask, prefix, coriolis, penetration),
        name="first_inside",
    )
    keep = after(keep, inside)
    mine = keep + got
    theirs = lax.ppermute(mine, "lev", [(0, 1), (1, 0)])

    inside = after(inside, mine)
    wide = cols + LANES
    *ring, sums = call(
        functools.partial(rim_kernel, n_lat),
        (
            shape(2, 6, DEEP, cols),
            shape(2, rows, LANES),
            shape(2, 5, DEEP, cols),
            shape(2, rows, LANES),
            shape(rows + DEEP, 2 * wide),
        ),
        [VMEM, VMEM, VMEM, SMEM, SMEM, SMEM] + [VMEM] * 8,
        (
            flat_state, flat_mask, prefix, coriolis, penetration, fold_partner, west, east, from_west, from_east, from_pair,
            from_cross, fold, inside,
        ),
        [pltpu.VMEM((SLABS + 1, DEEP, cols), F32), pltpu.VMEM((SLABS + 1, DEEP, cols), F32)],
        name="first_rim",
    )
    *flux, above = call(
        functools.partial(flux_kernel, n_lat),
        (shape(3, rows, cols), shape(DEEP, cols), shape(rows, LANES), shape(rows + DEEP, wide)),
        [VMEM] * 3 + [SMEM],
        (sums, mine, theirs, fold_partner),
        name="flux_parts",
    )
    above = lax.ppermute(above, "lev", [(0, 1)])

    out = jax.ShapeDtypeStruct(flat_state.shape, F32)
    result, flow = call(
        second_kernel,
        (out, shape(2, levels * rows, cols)),
        [VMEM] * 9 + [SMEM] * 2,
        (new_state, flat_mask, *ring, *flux, coriolis, penetration),
        [pltpu.VMEM((3, levels * rows, cols), F32), pltpu.SemaphoreType.DMA((DEEP,))],
        name="second_substep",
        out_specs=(ANY, VMEM),
    )
    result = call(
        last_kernel,
        out,
        [ANY] + [VMEM] * 3,
        (result, flow, flat_mask, above),
        [pltpu.VMEM((2, levels * rows, cols), F32), pltpu.SemaphoreType.DMA((DEEP,))],
        name="deeper_pressure",
        out_specs=ANY,
        aliases={0: 0},
    )
    return result.reshape(fields, levels, rows, cols)


def solution(mesh):
    n_lon, n_lat = mesh.shape["lon"], mesh.shape["lat"]
    assert mesh.shape["lev"] == 2 and n_lat % 2 == 0 and n_lon > 2
    return jax.shard_map(
        functools.partial(body, n_lon, n_lat),
        mesh=mesh,
        in_specs=(
            P(None, "lev", "lat", "lon"),
            P("lev", "lat", "lon"),
            P("lat"),
            P("lev"),
            P(("lon", "lat"), None, None),
            P(("lon", "lat"), None),
            P(("lon", "lat")),
            P(),
        ),
        out_specs=P(None, "lev", "lat", "lon"),
        check_vma=False,
    )
```

profile of v0, /device:TPU:6, one launch (start us, length us, event | category | flops | bytes accessed | tf_op | source)
XLA Modules:
  0.0 45.4 jit_solution(1938646268222085125)
XLA Ops:
  0.0 2.5 %prepare.1 = (f32[64,1920]{1,0:T(8,128)S(1)}, f32[64,1920]{1,0:T(8,128)S(1)}, f32[16,128]{1,0:T(8,128)S(1)}, f32[16,128]{1,0:T(8,128)S(1)}, f32[16,512]{1,0:T(8,128)S(1)}) custom-call(f32[5,128,512]{2,1,0:T(8,128)} %bitcast.7, s32[128,512]{1,0:T(8,128)} %bitcast.12, f32[3,128,512]{2,1,0:T(8,128)} %bitcast.19, s32[1,128]{1,0:T(1,128)} %bitcast.20, ...), custom_call_target="tpu_custom_call" | custom-call | tf_op jit(solution)/shard_map/prepare/pallas_call | solution.py:43
  2.6 1.3 %collective-permute-start.32 = (f32[16,512]{1,0:T(8,128)S(1)}, f32[16,512]{1,0:T(8,128)S(1)}, u32[]{:S(2)}, u32[]{:S(2)}) collective-permute-start(f32[16,512]{1,0:T(8,128)S(1)} %get-tuple-element.77), channel_id=1, source_target_pairs={{0,1},{2,3},{4,5},{6,7},{8,9},{10,11},{12,13},{14,15},{16,17},{18,... | collective-permute-start | bytes 98312 | tf_op jit(solution)/shard_map/ppermute | solution.py:823
  5.1 3.3 %collective-permute-done.32.prefix_ref = f32[16,512]{1,0:T(8,128)S(1)} collective-permute-done((f32[16,512]{1,0:T(8,128)S(1)}, f32[16,512]{1,0:T(8,128)S(1)}, u32[]{:S(2)}, u32[]{:S(2)}) %collective-permute-start.32) | collective-permute-done | bytes 32800 | tf_op jit(solution)/shard_map/ppermute | solution.py:823
  9.1 1.5 %conditional.1 = (f32[5,12,8,128]{3,2,1,0:T(8,128)S(1)}) conditional(s32[]{:T(128)} %clamp.3, f32[4,12,8,128]{3,2,1,0:T(8,128)S(1)} %top_rows.1, f32[4,12,8,128]{3,2,1,0:T(8,128)S(1)} %top_rows.1, f32[4,12,8,128]{3,2,1,0:T(8,128)S(1)} %top_rows.1, f32[4,12,8,128]{3,2,1,0:T(8,128)S(1)} %top_rows.1, ...), branch_computations={%region_0.0_spmd, %region_1.0_spmd, %region_2.0_spmd, %region_3.0_... | conditional | flops 61440 | bytes 1966168 | solution.py:856
  9.1 0.7 %collective-permute-start = (f32[4,12,8,128]{3,2,1,0:T(8,128)S(1)}, f32[4,12,8,128]{3,2,1,0:T(8,128)S(1)}, u32[]{:S(2)}, u32[]{:S(2)}) collective-permute-start(f32[4,12,8,128]{3,2,1,0:T(8,128)S(1)} %param), channel_id=1, source_target_pairs={{6,30},{14,22},{22,14},{30,6},{7,31},{15,23},{23,15},{31,7}} | collective-permute-start | bytes 589832 | tf_op jit(solution)/shard_map/cond/branch_0_fun/ppermute | solution.py:850
  10.6 5.1 %collective-permute-done.34.got_ref = f32[32,1920]{1,0:T(8,128)S(1)} collective-permute-done((f32[32,1920]{1,0:T(8,128)S(1)}, f32[32,1920]{1,0:T(8,128)S(1)}, u32[]{:S(2)}, u32[]{:S(2)}) %collective-permute-start.34) | collective-permute-done | bytes 245792 | tf_op jit(solution)/shard_map/ppermute | solution.py:831
  15.7 2.7 %collective-permute-start.37 = (f32[16,1920]{1,0:T(8,128)S(1)}, f32[16,1920]{1,0:T(8,128)S(1)}, u32[]{:S(2)}, u32[]{:S(2)}) collective-permute-start(f32[16,1920]{1,0:T(8,128)S(1)} %get-tuple-element.87), channel_id=1, source_target_pairs={{0,16},{8,24},{16,0},{24,8},{1,17},{9,25},{17,1},{25,9},{2,18},{10... | collective-permute-start | bytes 368648 | tf_op jit(solution)/shard_map/ppermute | solution.py:831
  18.4 0.7 %edge_columns.1 = (f32[24,128]{1,0:T(8,128)S(1)}, f32[24,128]{1,0:T(8,128)S(1)}) custom-call(f32[16,128]{1,0:T(8,128)S(1)} %get-tuple-element.88.west_ref, f32[16,128]{1,0:T(8,128)S(1)} %get-tuple-element.89.east_ref, f32[16,512]{1,0:T(8,128)S(1)} %collective-permute-done.32.prefix_ref, f32[5,12,8,128]{3,2,1,0:T(8,128)S(1)} %get-tuple-element.114.fold_ref, ...), custom_call_target="tpu_custom_call" | custom-call | tf_op jit(solution)/shard_map/edge_columns/pallas_call | solution.py:43
  19.1 1.6 %collective-permute-start.35 = (f32[24,128]{1,0:T(8,128)S(1)}, f32[24,128]{1,0:T(8,128)S(1)}, u32[]{:S(2)}, u32[]{:S(2)}) collective-permute-start(f32[24,128]{1,0:T(8,128)S(1)} %get-tuple-element.90.own_east_ref), channel_id=1, source_target_pairs={{0,8},{8,16},{16,24},{24,0},{1,9},{9,17},{17,25},{25,1},{2,10},{10... | collective-permute-start | bytes 36872 | tf_op jit(solution)/shard_map/ppermute | solution.py:870
  20.7 2.2 %collective-permute-start.36 = (f32[24,128]{1,0:T(8,128)S(1)}, f32[24,128]{1,0:T(8,128)S(1)}, u32[]{:S(2)}, u32[]{:S(2)}) collective-permute-start(f32[24,128]{1,0:T(8,128)S(1)} %get-tuple-element.91.own_west_ref), channel_id=1, source_target_pairs={{8,0},{16,8},{24,16},{0,24},{9,1},{17,9},{25,17},{1,25},{10,2},{18... | collective-permute-start | bytes 36872 | tf_op jit(solution)/shard_map/ppermute | solution.py:871
  23.0 1.9 %collective-permute-done.35.from_west_ref = f32[24,128]{1,0:T(8,128)S(1)} collective-permute-done((f32[24,128]{1,0:T(8,128)S(1)}, f32[24,128]{1,0:T(8,128)S(1)}, u32[]{:S(2)}, u32[]{:S(2)}) %collective-permute-start.35) | collective-permute-done | bytes 12320 | tf_op jit(solution)/shard_map/ppermute | solution.py:870
  24.9 1.1 %collective-permute-done.36.from_east_ref = f32[24,128]{1,0:T(8,128)S(1)} collective-permute-done((f32[24,128]{1,0:T(8,128)S(1)}, f32[24,128]{1,0:T(8,128)S(1)}, u32[]{:S(2)}, u32[]{:S(2)}) %collective-permute-start.36) | collective-permute-done | bytes 12320 | tf_op jit(solution)/shard_map/ppermute | solution.py:871
  26.1 0.7 %edge_rows.1 = (f32[12,8,512]{2,1,0:T(8,128)S(1)}, f32[12,8,512]{2,1,0:T(8,128)S(1)}) custom-call(f32[5,128,512]{2,1,0:T(8,128)S(1)} %bitcast.9, s32[128,512]{1,0:T(8,128)S(1)} %bitcast.14, f32[16,512]{1,0:T(8,128)S(1)} %collective-permute-done.32.prefix_ref, f32[16]{0:T(128)S(1)} %copy-done.3, f32[24,128]{1,0:T(8,128)S(1)} %collective-permute-done.35.from_west_ref, ...), custom_call_target="tpu_custom_call" | custom-call | tf_op jit(solution)/shard_map/edge_rows/pallas_call | solution.py:43
  27.0 1.9 %collective-permute-start.39 = (f32[12,8,512]{2,1,0:T(8,128)S(1)}, f32[12,8,512]{2,1,0:T(8,128)S(1)}, u32[]{:S(2)}, u32[]{:S(2)}) collective-permute-start(f32[12,8,512]{2,1,0:T(8,128)S(1)} %get-tuple-element.93), channel_id=1, source_target_pairs={{2,4},{4,2},{3,5},{5,3},{10,12},{12,10},{11,13},{13,11},{18,20},{2... | collective-permute-start | bytes 589832 | tf_op jit(solution)/shard_map/ppermute | solution.py:880
  28.9 0.8 %collective-permute-start.40 = (f32[8,1920]{1,0:T(8,128)S(1)}, f32[8,1920]{1,0:T(8,128)S(1)}, u32[]{:S(2)}, u32[]{:S(2)}) collective-permute-start(f32[8,1920]{1,0:T(8,128)S(1)} %get-tuple-element.95), channel_id=1, source_target_pairs={{0,8},{8,0},{16,24},{24,16},{1,9},{9,1},{17,25},{25,17},{2,10},{10... | collective-permute-start | bytes 184328 | tf_op jit(solution)/shard_map/ppermute | solution.py:831
  29.7 1.6 %first_inside.1 = (f32[5,128,512]{2,1,0:T(8,128)S(1)}, f32[16,1024]{1,0:T(8,128)S(1)}) custom-call(f32[5,128,512]{2,1,0:T(8,128)S(1)} %bitcast.10, s32[128,512]{1,0:T(8,128)S(1)} %bitcast.15, f32[16,512]{1,0:T(8,128)S(1)} %collective-permute-done.32.prefix_ref, f32[16]{0:T(128)S(1)} %copy-done.3, f32[8]{0:T(128)S(1)} %copy-done.4), custom_call_target="tpu_custom_call" | custom-call | tf_op jit(solution)/shard_map/first_inside/pallas_call | solution.py:43
  31.3 1.9 %collective-permute-done.40 = f32[8,1920]{1,0:T(8,128)S(1)} collective-permute-done((f32[8,1920]{1,0:T(8,128)S(1)}, f32[8,1920]{1,0:T(8,128)S(1)}, u32[]{:S(2)}, u32[]{:S(2)}) %collective-permute-start.40) | collective-permute-done | bytes 61472 | tf_op jit(solution)/shard_map/ppermute | solution.py:831
  33.9 2.5 %first_rim.1 = (f32[2,6,8,512]{3,2,1,0:T(8,128)S(1)}, f32[2,16,128]{2,1,0:T(8,128)S(1)}, f32[2,5,8,512]{3,2,1,0:T(8,128)S(1)}, f32[2,16,128]{2,1,0:T(8,128)S(1)}, f32[24,1280]{1,0:T(8,128)S(1)}) custom-call(f32[5,128,512]{2,1,0:T(8,128)S(1)} %bitcast.11, s32[128,512]{1,0:T(8,128)S(1)} %bitcast.16, f32[16,512]{1,0:T(8,128)S(1)} %collective-permute-done.32.prefix_ref, ...), custom_call_target="tpu_custom_call" | custom-call | tf_op jit(solution)/shard_map/first_rim/pallas_call | solution.py:43
  36.4 1.0 %collective-permute-done.41.theirs_ref = f32[8,1920]{1,0:T(8,128)S(1)} collective-permute-done((f32[8,1920]{1,0:T(8,128)S(1)}, f32[8,1920]{1,0:T(8,128)S(1)}, u32[]{:S(2)}, u32[]{:S(2)}) %collective-permute-start.41) | collective-permute-done | bytes 61472 | tf_op jit(solution)/shard_map/ppermute | solution.py:896
  37.5 0.9 %flux_parts.1 = (f32[3,16,512]{2,1,0:T(8,128)S(1)}, f32[8,512]{1,0:T(8,128)S(1)}, f32[16,128]{1,0:T(8,128)S(1)}, f32[24,640]{1,0:T(8,128)S(1)}) custom-call(f32[24,1280]{1,0:T(8,128)S(1)} %get-tuple-element.107.sums_ref, f32[8,1920]{1,0:T(8,128)S(1)} %add.3.mine_ref, f32[8,1920]{1,0:T(8,128)S(1)} %collective-permute-done.41.theirs_ref, s32[2048]{0:T(1024)S(1)} %copy-done.2), custom_call_target="tpu_custom_call" | custom-call | tf_op jit(solution)/shard_map/flux_parts/pallas_call | solution.py:43
  38.4 1.3 %collective-permute-start.42 = (f32[24,640]{1,0:T(8,128)S(1)}, f32[24,640]{1,0:T(8,128)S(1)}, u32[]{:S(2)}, u32[]{:S(2)}) collective-permute-start(f32[24,640]{1,0:T(8,128)S(1)} %get-tuple-element.113), channel_id=1, source_target_pairs={{0,1},{2,3},{4,5},{6,7},{8,9},{10,11},{12,13},{14,15},{16,17},{18,... | collective-permute-start | bytes 184328 | tf_op jit(solution)/shard_map/ppermute | solution.py:924
  39.6 2.8 %second_substep.1 = (f32[5,128,512]{2,1,0:T(8,128)}, f32[2,128,512]{2,1,0:T(8,128)S(1)}) custom-call(f32[5,128,512]{2,1,0:T(8,128)S(1)} %get-tuple-element.98.state_ref, s32[128,512]{1,0:T(8,128)S(1)} %bitcast.17, f32[2,6,8,512]{3,2,1,0:T(8,128)S(1)} %get-tuple-element.103.ring_rows_ref, f32[2,16,128]{2,1,0:T(8,128)S(1)} %get-tuple-element.104.ring_cols_ref, ...), custom_call_target="tpu_custom_call" | custom-call | tf_op jit(solution)/shard_map/second_substep/pallas_call | solution.py:43
  42.5 2.0 %collective-permute-done.42.above_ref = f32[24,640]{1,0:T(8,128)S(1)} collective-permute-done((f32[24,640]{1,0:T(8,128)S(1)}, f32[24,640]{1,0:T(8,128)S(1)}, u32[]{:S(2)}, u32[]{:S(2)}) %collective-permute-start.42) | collective-permute-done | bytes 61472 | tf_op jit(solution)/shard_map/ppermute | solution.py:924
  44.5 1.0 %deeper_pressure.1 = f32[5,128,512]{2,1,0:T(8,128)} custom-call(f32[5,128,512]{2,1,0:T(8,128)} %get-tuple-element.111.out_in_hbm, f32[2,128,512]{2,1,0:T(8,128)S(1)} %get-tuple-element.112.flow_ref, s32[128,512]{1,0:T(8,128)S(1)} %bitcast.18, f32[24,640]{1,0:T(8,128)S(1)} %collective-permute-done.42.above_ref), custom_call_target="tpu_custom_call", output_to_operand_aliasing={{}: (0, {})} | custom-call | tf_op jit(solution)/shard_map/deeper_pressure/pallas_call | solution.py:43
  (29 shorter events, 3.0 us)
Async XLA Ops:
  0.0 3.9 %copy-start.2 = (s32[2048]{0:T(1024)S(1)}, s32[2048]{0:T(1024)}, u32[]{:S(2)}) copy-start(s32[2048]{0:T(1024)} %partner_ref.5) | copy-start | bytes 24580
  0.0 9.0 %copy-start = (f32[5,8,16,512]{3,2,1,0:T(8,128)S(1)}, f32[5,8,16,512]{3,2,1,0:T(8,128)}, u32[]{:S(2)}) copy-start(f32[5,8,16,512]{3,2,1,0:T(8,128)} %param.24) | copy-start | bytes 3932164
  0.0 9.0 %copy-start.1 = (s32[8,16,512]{2,1,0:T(8,128)S(1)}, s32[8,16,512]{2,1,0:T(8,128)}, u32[]{:S(2)}) copy-start(s32[8,16,512]{2,1,0:T(8,128)} %param.25) | copy-start | bytes 786436
  2.5 5.9 %collective-permute-start.33 = (f32[64,1920]{1,0:T(8,128)S(1)}, f32[64,1920]{1,0:T(8,128)S(1)}, u32[]{:S(2)}, u32[]{:S(2)}) collective-permute-start(f32[64,1920]{1,0:T(8,128)S(1)} %get-tuple-element.79), channel_id=1, source_target_pairs={{0,2},{2,0},{4,6},{6,4},{1,3},{3,1},{5,7},{7,5},{8,10},{10,8},{12,... | collective-permute-start | bytes 1474568 | tf_op jit(solution)/shard_map/ppermute | solution.py:822
  2.6 5.8 %collective-permute-start.32 = (f32[16,512]{1,0:T(8,128)S(1)}, f32[16,512]{1,0:T(8,128)S(1)}, u32[]{:S(2)}, u32[]{:S(2)}) collective-permute-start(f32[16,512]{1,0:T(8,128)S(1)} %get-tuple-element.77), channel_id=1, source_target_pairs={{0,1},{2,3},{4,5},{6,7},{8,9},{10,11},{12,13},{14,15},{16,17},{18,... | collective-permute-start | bytes 98312 | tf_op jit(solution)/shard_map/ppermute | solution.py:823
  8.5 7.3 %collective-permute-start.34 = (f32[32,1920]{1,0:T(8,128)S(1)}, f32[32,1920]{1,0:T(8,128)S(1)}, u32[]{:S(2)}, u32[]{:S(2)}) collective-permute-start(f32[32,1920]{1,0:T(8,128)S(1)} %get-tuple-element.81), channel_id=1, source_target_pairs={{0,4},{2,6},{4,0},{6,2},{1,5},{3,7},{5,1},{7,3},{8,12},{10,14},{12... | collective-permute-start | bytes 737288 | tf_op jit(solution)/shard_map/ppermute | solution.py:831
  9.1 17.0 %copy-start.3 = (f32[16]{0:T(128)S(1)}, f32[16]{0:T(128)}, u32[]{:S(2)}) copy-start(f32[16]{0:T(128)} %turn_ref.7) | copy-start | bytes 196
  9.1 1.4 %collective-permute-start = (f32[4,12,8,128]{3,2,1,0:T(8,128)S(1)}, f32[4,12,8,128]{3,2,1,0:T(8,128)S(1)}, u32[]{:S(2)}, u32[]{:S(2)}) collective-permute-start(f32[4,12,8,128]{3,2,1,0:T(8,128)S(1)} %param), channel_id=1, source_target_pairs={{6,30},{14,22},{22,14},{30,6},{7,31},{15,23},{23,15},{31,7}} | collective-permute-start | bytes 589832 | tf_op jit(solution)/shard_map/cond/branch_0_fun/ppermute | solution.py:850
  9.8 0.7 %collective-permute-start.1 = (f32[1,12,8,128]{3,2,1,0:T(8,128)S(1)}, f32[1,12,8,128]{3,2,1,0:T(8,128)S(1)}, u32[]{:S(2)}, u32[]{:S(2)}) collective-permute-start(f32[1,12,8,128]{3,2,1,0:T(8,128)S(1)} %slice.50), channel_id=1, source_target_pairs={{6,6},{14,30},{22,22},{30,14},{7,7},{15,31},{23,23},{31,15}} | collective-permute-start | bytes 147464 | tf_op jit(solution)/shard_map/cond/branch_0_fun/ppermute | solution.py:850
  10.6 19.1 %copy-start.4 = (f32[8]{0:T(128)S(1)}, f32[8]{0:T(128)}, u32[]{:S(2)}) copy-start(f32[8]{0:T(128)} %share_ref.5) | copy-start | bytes 100
  15.7 13.1 %collective-permute-start.37 = (f32[16,1920]{1,0:T(8,128)S(1)}, f32[16,1920]{1,0:T(8,128)S(1)}, u32[]{:S(2)}, u32[]{:S(2)}) collective-permute-start(f32[16,1920]{1,0:T(8,128)S(1)} %get-tuple-element.87), channel_id=1, source_target_pairs={{0,16},{8,24},{16,0},{24,8},{1,17},{9,25},{17,1},{25,9},{2,18},{10... | collective-permute-start | bytes 368648 | tf_op jit(solution)/shard_map/ppermute | solution.py:831
  19.1 5.8 %collective-permute-start.35 = (f32[24,128]{1,0:T(8,128)S(1)}, f32[24,128]{1,0:T(8,128)S(1)}, u32[]{:S(2)}, u32[]{:S(2)}) collective-permute-start(f32[24,128]{1,0:T(8,128)S(1)} %get-tuple-element.90.own_east_ref), channel_id=1, source_target_pairs={{0,8},{8,16},{16,24},{24,0},{1,9},{9,17},{17,25},{25,1},{2,10},{10... | collective-permute-start | bytes 36872 | tf_op jit(solution)/shard_map/ppermute | solution.py:870
  20.7 5.3 %collective-permute-start.36 = (f32[24,128]{1,0:T(8,128)S(1)}, f32[24,128]{1,0:T(8,128)S(1)}, u32[]{:S(2)}, u32[]{:S(2)}) collective-permute-start(f32[24,128]{1,0:T(8,128)S(1)} %get-tuple-element.91.own_west_ref), channel_id=1, source_target_pairs={{8,0},{16,8},{24,16},{0,24},{9,1},{17,9},{25,17},{1,25},{10,2},{18... | collective-permute-start | bytes 36872 | tf_op jit(solution)/shard_map/ppermute | solution.py:871
  26.8 6.7 %collective-permute-start.38 = (f32[12,8,512]{2,1,0:T(8,128)S(1)}, f32[12,8,512]{2,1,0:T(8,128)S(1)}, u32[]{:S(2)}, u32[]{:S(2)}) collective-permute-start(f32[12,8,512]{2,1,0:T(8,128)S(1)} %get-tuple-element.92), channel_id=1, source_target_pairs={{0,2},{2,0},{4,6},{6,4},{1,3},{3,1},{5,7},{7,5},{8,10},{10,8},{12,... | collective-permute-start | bytes 589832 | tf_op jit(solution)/shard_map/ppermute | solution.py:879
  27.0 7.0 %collective-permute-start.39 = (f32[12,8,512]{2,1,0:T(8,128)S(1)}, f32[12,8,512]{2,1,0:T(8,128)S(1)}, u32[]{:S(2)}, u32[]{:S(2)}) collective-permute-start(f32[12,8,512]{2,1,0:T(8,128)S(1)} %get-tuple-element.93), channel_id=1, source_target_pairs={{2,4},{4,2},{3,5},{5,3},{10,12},{12,10},{11,13},{13,11},{18,20},{2... | collective-permute-start | bytes 589832 | tf_op jit(solution)/shard_map/ppermute | solution.py:880
  28.9 4.3 %collective-permute-start.40 = (f32[8,1920]{1,0:T(8,128)S(1)}, f32[8,1920]{1,0:T(8,128)S(1)}, u32[]{:S(2)}, u32[]{:S(2)}) collective-permute-start(f32[8,1920]{1,0:T(8,128)S(1)} %get-tuple-element.95), channel_id=1, source_target_pairs={{0,8},{8,0},{16,24},{24,16},{1,9},{9,1},{17,25},{25,17},{2,10},{10... | collective-permute-start | bytes 184328 | tf_op jit(solution)/shard_map/ppermute | solution.py:831
  33.2 4.3 %collective-permute-start.41 = (f32[8,1920]{1,0:T(8,128)S(1)}, f32[8,1920]{1,0:T(8,128)S(1)}, u32[]{:S(2)}, u32[]{:S(2)}) collective-permute-start(f32[8,1920]{1,0:T(8,128)S(1)} %add.3.mine_ref), channel_id=1, source_target_pairs={{0,1},{1,0},{2,3},{3,2},{4,5},{5,4},{6,7},{7,6},{8,9},{9,8},{10,11... | collective-permute-start | bytes 184328 | tf_op jit(solution)/shard_map/ppermute | solution.py:896
  38.4 6.1 %collective-permute-start.42 = (f32[24,640]{1,0:T(8,128)S(1)}, f32[24,640]{1,0:T(8,128)S(1)}, u32[]{:S(2)}, u32[]{:S(2)}) collective-permute-start(f32[24,640]{1,0:T(8,128)S(1)} %get-tuple-element.113), channel_id=1, source_target_pairs={{0,1},{2,3},{4,5},{6,7},{8,9},{10,11},{12,13},{14,15},{16,17},{18,... | collective-permute-start | bytes 184328 | tf_op jit(solution)/shard_map/ppermute | solution.py:924
where the time goes:
time: 45.5 us; the launch traced here: 45.4 us
  waiting for transfers between devices  16.9 us (37%)
  starting transfers between devices  14.2 us (31%)
  Pallas kernels  12.9 us (28%)
  between operations  0.79 us (2%)
  local copies, waits for them, and re-layouts  0.54 us (1%)
    pallas_call x12, Pallas kernels, call(): pl.pallas_call(kernel, out_shape=out_shape, in_specs=in_specs, out_specs=...  12.9 us
    ppermute x3, waiting for transfers between devices, passed_on(): return lax.ppermute(send, axis, [(i, i ^ bit) for i in range(size)])  6.99 us
    ppermute x3, starting transfers between devices, passed_on(): return lax.ppermute(send, axis, [(i, i ^ bit) for i in range(size)])  4.02 us
    ppermute x1, waiting for transfers between devices, body(): prefix = lax.ppermute(total, 'lev', [(0, 1)])  3.33 us
    ppermute x1, starting transfers between devices, body(): lax.ppermute(west, 'lon', [((i + 1) % n_lon, i) for i in range(n_lon)])  2.25 us
    ppermute x1, waiting for transfers between devices, body(): above = lax.ppermute(above, 'lev', [(0, 1)])  1.99 us
    ppermute x1, waiting for transfers between devices, body(): lax.ppermute(east, 'lon', [(i, (i + 1) % n_lon) for i in range(n_lon)])  1.94 us
    ppermute x1, starting transfers between devices, body(): lax.ppermute(cross, 'lat', [(i, i + 1 if i % 2 else i - 1) for i in range...  1.91 us
  transfers between devices with their start and end apart: 13, of which 8 were waited for; matrix products, arithmetic and copies ran while one was open for 1% of the time, Pallas kernels for 19%

commit v1 on v0

--- a/solution.py
+++ b/solution.py
@@ -422,17 +422,13 @@
     return jnp.sum(here, axis=1, keepdims=True)
 
 
-def inside_kernel(state_ref, mask_ref, prefix_ref, turn_ref, share_ref, new_ref, sums_ref):
-    rows, cols = prefix_ref.shape
+def inside_kernel(state_ref, mask_ref, turn_ref, share_ref, new_ref, sums_ref):
+    rows, cols = sums_ref.shape[0], state_ref.shape[2]
     n_r, n_j = rows // DEEP, cols // LANES
     turn = turn_column(turn_ref, rows)
     grid = [(r, j) for r in range(n_r) for j in range(n_j)]
     zero = jnp.zeros((DEEP, LANES), F32)
-    prefix = Tiles([[prefix_ref[tile(r, j, 0, rows)] for j in range(n_j)] for r in range(n_r)])
-    run = {}
-    for at in grid:
-        east, west, north, south = prefix.around(*at)
-        run[at] = [0.5 * (east - west), 0.5 * (north - south), zero, zero]
+    run = {at: [zero] * 4 for at in grid}
     for k in range(DEEP):
         fields = [Tiles([[state_ref[(f, *tile(r, j, k, rows))] for j in range(n_j)] for r in range(n_r)]) for f in range(5)]
         for r, j in grid:
@@ -618,7 +614,7 @@
         sums_ref[edge : edge + 1, 0:cols] = jnp.sum(here, axis=0, keepdims=True)
 
 
-def flux_kernel(n_lat, sums_ref, mine_ref, theirs_ref, partner_ref, flux_ref, flux_rows_ref, flux_cols_ref, above_ref):
+def flux_kernel(n_lat, mine_ref, theirs_ref, partner_ref, flux_ref, flux_rows_ref, flux_cols_ref, drive_ref):
     rows, cols = flux_ref.shape[1:]
     half_cols = cols // 2
     wide = 3 * half_cols
@@ -666,20 +662,17 @@
         flux_cols = jnp.where(lane == c, flux_west[c], jnp.where(lane == 3 + c, flux_east[c], flux_cols))
     flux_rows_ref[6:8, :] = jnp.zeros((2, cols), F32)
     flux_cols_ref[...] = flux_cols
-    reach = cols + LANES
-    above_ref[rows:, :] = jnp.zeros((DEEP, reach), F32)
-    above_ref[0:rows, 0:cols] = sums_ref[0:rows, 0:cols] + sums_ref[0:rows, reach : reach + cols] * buoyancy_of(flux[0], flux[1])
+    drive_ref[rows:, :] = jnp.zeros((DEEP, cols + LANES), F32)
+    drive_ref[0:rows, 0:cols] = buoyancy_of(flux[0], flux[1])
     ends = jnp.zeros((rows, LANES), F32)
-    for side, column, line in ((0, (flux_west[0], flux_west[1]), flux_south), (1, (flux_east[0], flux_east[1]), flux_north)):
-        at = slice(rows + side, rows + side + 1)
-        above_ref[at, 0:cols] = sums_ref[at, 0:cols] + sums_ref[at, reach : reach + cols] * buoyancy_of(line[0], line[1])
-        before, taken = sums_ref[0:rows, cols:reach], sums_ref[0:rows, reach + cols :]
-        ends = jnp.where(lane == side, before + taken * buoyancy_of(*column), ends)
-    above_ref[0:rows, cols:reach] = ends
+    for side, column, line in ((0, flux_west, flux_south), (1, flux_east, flux_north)):
+        drive_ref[rows + side : rows + side + 1, 0:cols] = buoyancy_of(line[0], line[1])
+        ends = jnp.where(lane == side, buoyancy_of(column[0], column[1]), ends)
+    drive_ref[0:rows, cols:] = ends
 
 
 def second_kernel(
-    state_ref, mask_ref, ring_rows_ref, ring_cols_ref, edge_rows_ref, edge_cols_ref, flux_ref, flux_rows_ref,
+    state_ref, mask_ref, prefix_ref, ring_rows_ref, ring_cols_ref, edge_rows_ref, edge_cols_ref, flux_ref, flux_rows_ref,
     flux_cols_ref, turn_ref, share_ref, out_hbm, flow_ref, tracers_ref, sem,
 ):
     rows, cols = flux_ref.shape[1:]
@@ -712,6 +705,11 @@
 
     zero = jnp.zeros((DEEP, LANES), F32)
     run = {at: (zero, zero) for at in grid}
+    prefix = Tiles([[prefix_ref[tile(r, j, 0, rows)] for j in range(n_j)] for r in range(n_r)])
+    push = {}
+    for at in grid:
+        east, west, north, south = prefix.around(*at)
+        push[at] = (0.5 * PRESS) * (east - west), (0.5 * PRESS) * (north - south)
     edge_cols = [edge_cols_ref[side] for side in range(2)]
     copies = []
 
@@ -728,6 +726,8 @@
             heats[r, j] = [taken * cut(flux_ref[c], r, j) for c in range(3)]
             for f in range(5):
                 value = state_ref[(f, *at)]
+                if f < 2:
+                    value = value - wet * push[r, j][f]
                 if j == 0:
                     value = jnp.where(lane8 == 0, column(edge_cols[0], r, f * DEEP + k), value)
                 if j == n_j - 1:
@@ -779,10 +779,11 @@
         copy.wait()
 
 
-def last_kernel(out_in_hbm, flow_ref, mask_ref, above_ref, out_hbm, moved_ref, sem):
+def last_kernel(out_in_hbm, flow_ref, mask_ref, sums_ref, drive_ref, out_hbm, moved_ref, sem):
     del out_in_hbm
     rows, cols = mask_ref.shape[0] // DEEP, mask_ref.shape[1]
-    above = above_ref[...]
+    wide = cols + LANES
+    above = sums_ref[:, 0:wide] + sums_ref[:, wide : 2 * wide] * drive_ref[...]
     east, west, north, south = around(
         above[0:rows, 0:cols],
         above[0:rows, cols : cols + 1],
@@ -830,13 +831,20 @@
         axis, size, bit = stage
         return lax.ppermute(send, axis, [(i, i ^ bit) for i in range(size)])
 
+    near_state, near_mask = after((flat_state, flat_mask), send)
+    new_state, inside = call(
+        inside_kernel,
+        (shape(fields, levels * rows, cols), shape(rows, 2 * cols)),
+        [VMEM, VMEM, SMEM, SMEM],
+        (near_state, near_mask, coriolis, penetration),
+        name="first_inside",
+    )
     pieces = cols // LANES
     hinge_piece = fold_partner[0] >> (LANES.bit_length() - 1)
-    keep = after(keep, (prefix, hinge_piece))
+    keep = after(keep, (prefix, hinge_piece, inside))
     keep, send = merged(keep, got)
     got = passed_on(send, stages[0])
 
-    message = shape(SLABS + 1, DEEP, cols)
     top_shape = shape(pieces, SLABS + 1, DEEP, LANES)
     top = call(top_kernel, top_shape, [VMEM] * 3, (flat_state, flat_mask, prefix), name="top_rows")
     top = after(top, send)
@@ -869,6 +877,13 @@
     )
     from_west = lax.ppermute(east, "lon", [(i, (i + 1) % n_lon) for i in range(n_lon)])
     from_east = lax.ppermute(west, "lon", [((i + 1) % n_lon, i) for i in range(n_lon)])
+    keep = after(keep, (from_west, from_east))
+    for stage in stages[2:]:
+        keep, send = merged(keep, got)
+        got = passed_on(send, stage)
+
+    message = shape(SLABS + 1, DEEP, cols)
+    from_west, from_east = after((from_west, from_east), send)
     pair, cross = call(
         rows_kernel,
         (message, message),
@@ -878,20 +893,7 @@
     )
     from_pair = lax.ppermute(pair, "lat", [(i, i ^ 1) for i in range(n_lat)])
     from_cross = lax.ppermute(cross, "lat", [(i, i + 1 if i % 2 else i - 1) for i in range(1, last)])
-    keep = after(keep, (pair, cross))
-    for stage in stages[2:]:
-        keep, send = merged(keep, got)
-        got = passed_on(send, stage)
-
-    near_state, near_mask = after((flat_state, flat_mask), send)
-    new_state, inside = call(
-        inside_kernel,
-        (shape(fields, levels * rows, cols), shape(rows, 2 * cols)),
-        [VMEM, VMEM, VMEM, SMEM, SMEM],
-        (near_state, near_mask, prefix, coriolis, penetration),
-        name="first_inside",
-    )
-    keep = after(keep, inside)
+    keep = after(keep, (from_pair, from_cross))
     mine = keep + got
     theirs = lax.ppermute(mine, "lev", [(0, 1), (1, 0)])
 
@@ -914,21 +916,21 @@
         [pltpu.VMEM((SLABS + 1, DEEP, cols), F32), pltpu.VMEM((SLABS + 1, DEEP, cols), F32)],
         name="first_rim",
     )
-    *flux, above = call(
+    sums = lax.ppermute(after(sums, theirs), "lev", [(0, 1)])
+    *flux, drive = call(
         functools.partial(flux_kernel, n_lat),
         (shape(3, rows, cols), shape(DEEP, cols), shape(rows, LANES), shape(rows + DEEP, wide)),
-        [VMEM] * 3 + [SMEM],
-        (sums, mine, theirs, fold_partner),
+        [VMEM] * 2 + [SMEM],
+        (mine, theirs, fold_partner),
         name="flux_parts",
     )
-    above = lax.ppermute(above, "lev", [(0, 1)])
 
     out = jax.ShapeDtypeStruct(flat_state.shape, F32)
     result, flow = call(
         second_kernel,
         (out, shape(2, levels * rows, cols)),
-        [VMEM] * 9 + [SMEM] * 2,
-        (new_state, flat_mask, *ring, *flux, coriolis, penetration),
+        [VMEM] * 10 + [SMEM] * 2,
+        (new_state, flat_mask, prefix, *ring, *flux, coriolis, penetration),
         [pltpu.VMEM((3, levels * rows, cols), F32), pltpu.SemaphoreType.DMA((DEEP,))],
         name="second_substep",
         out_specs=(ANY, VMEM),
@@ -936,8 +938,8 @@
     result = call(
         last_kernel,
         out,
-        [ANY] + [VMEM] * 3,
-        (result, flow, flat_mask, above),
+        [ANY] + [VMEM] * 4,
+        (result, flow, flat_mask, sums, drive),
         [pltpu.VMEM((2, levels * rows, cols), F32), pltpu.SemaphoreType.DMA((DEEP,))],
         name="deeper_pressure",
         out_specs=ANY,

time: 45.5 us -> 49.7 us (1.092)
  the two profiles are of different devices: /device:TPU:6 before, /device:TPU:1 now
where the time goes in v1:
time: 49.7 us; the launch traced here: 49.5 us
  starting transfers between devices  19.8 us (40%)
  Pallas kernels  14.8 us (30%)
  waiting for transfers between devices  12.6 us (25%)
  between operations  0.85 us (2%)
  other arithmetic  0.72 us (1%)
  local copies, waits for them, and re-layouts  0.54 us (1%)
    pallas_call x12, Pallas kernels, call(): pl.pallas_call(kernel, out_shape=out_shape, in_specs=in_specs, out_specs=...  14.8 us
    ppermute x1, starting transfers between devices, body(): prefix = lax.ppermute(total, 'lev', [(0, 1)])  4.56 us
    ppermute x3, waiting for transfers between devices, passed_on(): return lax.ppermute(send, axis, [(i, i ^ bit) for i in range(size)])  4.09 us
    ppermute x1, waiting for transfers between devices, body(): lax.ppermute(cross, 'lat', [(i, i + 1 if i % 2 else i - 1) for i in range...  3.83 us
    ppermute x3, starting transfers between devices, passed_on(): return lax.ppermute(send, axis, [(i, i ^ bit) for i in range(size)])  3.69 us
    ppermute x1, starting transfers between devices, body(): lax.ppermute(cross, 'lat', [(i, i + 1 if i % 2 else i - 1) for i in range...  3.05 us
    ppermute x1, starting transfers between devices, body(): sums = lax.ppermute(after(sums, theirs), 'lev', [(0, 1)])  2.83 us
    ppermute x1, starting transfers between devices, body(): from_pair = lax.ppermute(pair, 'lat', [(i, i ^ 1) for i in range(n_lat)])  2.71 us
  transfers between devices with their start and end apart: 13, of which 5 were waited for; matrix products, arithmetic and copies ran while one was open for 2% of the time, Pallas kernels for 18%

profile of v1, /device:TPU:1, one launch (start us, length us, event | category | flops | bytes accessed | tf_op | source)
XLA Modules:
  0.0 49.5 jit_solution(14968334886912397166)
XLA Ops:
  0.0 2.5 %prepare.1 = (f32[64,1920]{1,0:T(8,128)S(1)}, f32[64,1920]{1,0:T(8,128)S(1)}, f32[16,128]{1,0:T(8,128)S(1)}, f32[16,128]{1,0:T(8,128)S(1)}, f32[16,512]{1,0:T(8,128)S(1)}) custom-call(f32[5,128,512]{2,1,0:T(8,128)} %bitcast.7, s32[128,512]{1,0:T(8,128)} %bitcast.12, f32[3,128,512]{2,1,0:T(8,128)} %bitcast.19, s32[1,128]{1,0:T(1,128)} %bitcast.20, ...), custom_call_target="tpu_custom_call" | custom-call | tf_op jit(solution)/shard_map/prepare/pallas_call | solution.py:43
  2.6 4.6 %collective-permute-start.32 = (f32[16,512]{1,0:T(8,128)S(1)}, f32[16,512]{1,0:T(8,128)S(1)}, u32[]{:S(2)}, u32[]{:S(2)}) collective-permute-start(f32[16,512]{1,0:T(8,128)S(1)} %get-tuple-element.83), channel_id=1, source_target_pairs={{0,1},{2,3},{4,5},{6,7},{8,9},{10,11},{12,13},{14,15},{16,17},{18,... | collective-permute-start | bytes 98312 | tf_op jit(solution)/shard_map/ppermute | solution.py:824
  8.4 1.6 %first_inside.1 = (f32[5,128,512]{2,1,0:T(8,128)S(1)}, f32[16,1024]{1,0:T(8,128)S(1)}) custom-call(f32[5,128,512]{2,1,0:T(8,128)S(1)} %bitcast.8, s32[128,512]{1,0:T(8,128)S(1)} %bitcast.13, f32[16]{0:T(128)S(1)} %copy-done.3, f32[8]{0:T(128)S(1)} %copy-done.4), custom_call_target="tpu_custom_call" | custom-call | tf_op jit(solution)/shard_map/first_inside/pallas_call | solution.py:43
  10.0 0.7 %merge_flux.3 = (f32[32,1920]{1,0:T(8,128)S(1)}, f32[32,1920]{1,0:T(8,128)}) custom-call(f32[64,1920]{1,0:T(8,128)S(1)} %get-tuple-element.88.kept_ref, f32[64,1920]{1,0:T(8,128)S(1)} %collective-permute-done.33.got_ref), custom_call_target="tpu_custom_call" | custom-call | tf_op jit(solution)/shard_map/merge_flux/pallas_call | solution.py:43
  10.8 1.2 %collective-permute-start.34 = (f32[32,1920]{1,0:T(8,128)}, f32[32,1920]{1,0:T(8,128)}, u32[]{:S(2)}, u32[]{:S(2)}) collective-permute-start(f32[32,1920]{1,0:T(8,128)} %get-tuple-element.90), channel_id=1, source_target_pairs={{0,4},{2,6},{4,0},{6,2},{1,5},{3,7},{5,1},{7,3},{8,12},{10,14},{12... | collective-permute-start | bytes 737288 | tf_op jit(solution)/shard_map/ppermute | solution.py:832
  12.1 2.2 %conditional.1 = (f32[5,12,8,128]{3,2,1,0:T(8,128)}) conditional(s32[]{:T(128)} %clamp.3, f32[4,12,8,128]{3,2,1,0:T(8,128)S(1)} %top_rows.1, f32[4,12,8,128]{3,2,1,0:T(8,128)S(1)} %top_rows.1, f32[4,12,8,128]{3,2,1,0:T(8,128)S(1)} %top_rows.1, f32[4,12,8,128]{3,2,1,0:T(8,128)S(1)} %top_rows.1, ...), branch_computations={%region_0.0_spmd, %region_1.0_spmd, %region_2.0_spmd, %region_3.0_... | conditional | flops 61440 | bytes 1966168 | solution.py:864
  12.2 0.7 %collective-permute-start.23 = (f32[4,12,8,128]{3,2,1,0:T(8,128)S(1)}, f32[4,12,8,128]{3,2,1,0:T(8,128)S(1)}, u32[]{:S(2)}, u32[]{:S(2)}) collective-permute-start(f32[4,12,8,128]{3,2,1,0:T(8,128)S(1)} %param.11), channel_id=1, source_target_pairs={{6,22},{14,14},{22,6},{30,30},{7,23},{15,15},{23,7},{31,31}} | collective-permute-start | bytes 589832 | tf_op jit(solution)/shard_map/cond/branch_11_fun/ppermute | solution.py:858
  13.5 0.7 %pad_maximum_fusion.11 = f32[5,12,8,128]{3,2,1,0:T(8,128)} fusion(f32[4,12,8,128]{3,2,1,0:T(8,128)S(1)} %collective-permute-done.23, f32[1,12,8,128]{3,2,1,0:T(8,128)S(1)} %collective-permute-done.22), kind=kLoop, calls=%fused_computation.11 | loop fusion | flops 61440 | bytes 491520 | tf_op jit(solution)/shard_map/cond/branch_11_fun/concatenate | solution.py:860
  14.3 4.1 %collective-permute-done.34.got_ref = f32[32,1920]{1,0:T(8,128)} collective-permute-done((f32[32,1920]{1,0:T(8,128)}, f32[32,1920]{1,0:T(8,128)}, u32[]{:S(2)}, u32[]{:S(2)}) %collective-permute-start.34) | collective-permute-done | bytes 245792 | tf_op jit(solution)/shard_map/ppermute | solution.py:832
  18.3 1.0 %merge_flux.4 = (f32[16,1920]{1,0:T(8,128)S(1)}, f32[16,1920]{1,0:T(8,128)S(1)}) custom-call(f32[32,1920]{1,0:T(8,128)S(1)} %get-tuple-element.92.kept_ref, f32[32,1920]{1,0:T(8,128)} %collective-permute-done.34.got_ref), custom_call_target="tpu_custom_call" | custom-call | tf_op jit(solution)/shard_map/merge_flux/pallas_call | solution.py:43
  19.3 2.4 %collective-permute-start.37 = (f32[16,1920]{1,0:T(8,128)S(1)}, f32[16,1920]{1,0:T(8,128)S(1)}, u32[]{:S(2)}, u32[]{:S(2)}) collective-permute-start(f32[16,1920]{1,0:T(8,128)S(1)} %get-tuple-element.93), channel_id=1, source_target_pairs={{0,16},{8,24},{16,0},{24,8},{1,17},{9,25},{17,1},{25,9},{2,18},{10... | collective-permute-start | bytes 368648 | tf_op jit(solution)/shard_map/ppermute | solution.py:832
  21.7 1.0 %edge_columns.1 = (f32[24,128]{1,0:T(8,128)S(1)}, f32[24,128]{1,0:T(8,128)S(1)}) custom-call(f32[16,128]{1,0:T(8,128)S(1)} %get-tuple-element.94.west_ref, f32[16,128]{1,0:T(8,128)S(1)} %get-tuple-element.95.east_ref, f32[16,512]{1,0:T(8,128)S(1)} %collective-permute-done.32.prefix_ref, f32[5,12,8,128]{3,2,1,0:T(8,128)} %get-tuple-element.120.fold_ref, ...), custom_call_target="tpu_custom_call" | custom-call | tf_op jit(solution)/shard_map/edge_columns/pallas_call | solution.py:43
  22.7 1.1 %collective-permute-start.36 = (f32[24,128]{1,0:T(8,128)S(1)}, f32[24,128]{1,0:T(8,128)S(1)}, u32[]{:S(2)}, u32[]{:S(2)}) collective-permute-start(f32[24,128]{1,0:T(8,128)S(1)} %get-tuple-element.96.own_west_ref), channel_id=1, source_target_pairs={{8,0},{16,8},{24,16},{0,24},{9,1},{17,9},{25,17},{1,25},{10,2},{18... | collective-permute-start | bytes 36872 | tf_op jit(solution)/shard_map/ppermute | solution.py:879
  24.2 1.5 %collective-permute-done.36.from_east_ref = f32[24,128]{1,0:T(8,128)S(1)} collective-permute-done((f32[24,128]{1,0:T(8,128)S(1)}, f32[24,128]{1,0:T(8,128)S(1)}, u32[]{:S(2)}, u32[]{:S(2)}) %collective-permute-start.36) | collective-permute-done | bytes 12320 | tf_op jit(solution)/shard_map/ppermute | solution.py:879
  25.7 2.6 %collective-permute-done.35.from_west_ref = f32[24,128]{1,0:T(8,128)S(1)} collective-permute-done((f32[24,128]{1,0:T(8,128)S(1)}, f32[24,128]{1,0:T(8,128)S(1)}, u32[]{:S(2)}, u32[]{:S(2)}) %collective-permute-start.35) | collective-permute-done | bytes 12320 | tf_op jit(solution)/shard_map/ppermute | solution.py:878
  28.4 0.7 %edge_rows.1 = (f32[12,8,512]{2,1,0:T(8,128)S(1)}, f32[12,8,512]{2,1,0:T(8,128)S(1)}) custom-call(f32[5,128,512]{2,1,0:T(8,128)S(1)} %bitcast.10, s32[128,512]{1,0:T(8,128)S(1)} %bitcast.15, f32[16,512]{1,0:T(8,128)S(1)} %collective-permute-done.32.prefix_ref, f32[16]{0:T(128)S(1)} %copy-done.3, f32[24,128]{1,0:T(8,128)S(1)} %collective-permute-done.35.from_west_ref, ...), custom_call_target="tpu_custom_call" | custom-call | tf_op jit(solution)/shard_map/edge_rows/pallas_call | solution.py:43
  29.1 2.7 %collective-permute-start.38 = (f32[12,8,512]{2,1,0:T(8,128)S(1)}, f32[12,8,512]{2,1,0:T(8,128)S(1)}, u32[]{:S(2)}, u32[]{:S(2)}) collective-permute-start(f32[12,8,512]{2,1,0:T(8,128)S(1)} %get-tuple-element.103), channel_id=1, source_target_pairs={{0,2},{2,0},{4,6},{6,4},{1,3},{3,1},{5,7},{7,5},{8,10},{10,8},{12,... | collective-permute-start | bytes 589832 | tf_op jit(solution)/shard_map/ppermute | solution.py:894
  31.8 3.0 %collective-permute-start.39 = (f32[12,8,512]{2,1,0:T(8,128)S(1)}, f32[12,8,512]{2,1,0:T(8,128)S(1)}, u32[]{:S(2)}, u32[]{:S(2)}) collective-permute-start(f32[12,8,512]{2,1,0:T(8,128)S(1)} %get-tuple-element.104), channel_id=1, source_target_pairs={{2,4},{4,2},{3,5},{5,3},{10,12},{12,10},{11,13},{13,11},{18,20},{2... | collective-permute-start | bytes 589832 | tf_op jit(solution)/shard_map/ppermute | solution.py:895
  34.9 3.8 %collective-permute-done.39.cross_ref = f32[12,8,512]{2,1,0:T(8,128)S(1)} collective-permute-done((f32[12,8,512]{2,1,0:T(8,128)S(1)}, f32[12,8,512]{2,1,0:T(8,128)S(1)}, u32[]{:S(2)}, u32[]{:S(2)}) %collective-permute-start.39) | collective-permute-done | bytes 196640 | tf_op jit(solution)/shard_map/ppermute | solution.py:895
  38.9 2.5 %first_rim.1 = (f32[2,6,8,512]{3,2,1,0:T(8,128)S(1)}, f32[2,16,128]{2,1,0:T(8,128)S(1)}, f32[2,5,8,512]{3,2,1,0:T(8,128)S(1)}, f32[2,16,128]{2,1,0:T(8,128)S(1)}, f32[24,1280]{1,0:T(8,128)S(1)}) custom-call(f32[5,128,512]{2,1,0:T(8,128)S(1)} %bitcast.11, s32[128,512]{1,0:T(8,128)S(1)} %bitcast.16, f32[16,512]{1,0:T(8,128)S(1)} %collective-permute-done.32.prefix_ref, ...), custom_call_target="tpu_custom_call" | custom-call | tf_op jit(solution)/shard_map/first_rim/pallas_call | solution.py:43
  41.9 2.8 %collective-permute-start.42 = (f32[24,1280]{1,0:T(8,128)S(1)}, f32[24,1280]{1,0:T(8,128)S(1)}, u32[]{:S(2)}, u32[]{:S(2)}) collective-permute-start(f32[24,1280]{1,0:T(8,128)S(1)} %get-tuple-element.118), channel_id=1, source_target_pairs={{0,1},{2,3},{4,5},{6,7},{8,9},{10,11},{12,13},{14,15},{16,17},{18,... | collective-permute-start | bytes 368648 | tf_op jit(solution)/shard_map/ppermute | solution.py:919
  44.8 0.9 %flux_parts.1 = (f32[3,16,512]{2,1,0:T(8,128)S(1)}, f32[8,512]{1,0:T(8,128)S(1)}, f32[16,128]{1,0:T(8,128)S(1)}, f32[24,640]{1,0:T(8,128)S(1)}) custom-call(f32[8,1920]{1,0:T(8,128)S(1)} %add.3.mine_ref, f32[8,1920]{1,0:T(8,128)S(1)} %collective-permute-done.41.theirs_ref, s32[2048]{0:T(1024)S(1)} %copy-done.2), custom_call_target="tpu_custom_call" | custom-call | tf_op jit(solution)/shard_map/flux_parts/pallas_call | solution.py:43
  45.6 2.8 %second_substep.1 = (f32[5,128,512]{2,1,0:T(8,128)}, f32[2,128,512]{2,1,0:T(8,128)S(1)}) custom-call(f32[5,128,512]{2,1,0:T(8,128)S(1)} %get-tuple-element.82.state_ref, s32[128,512]{1,0:T(8,128)S(1)} %bitcast.17, f32[16,512]{1,0:T(8,128)S(1)} %collective-permute-done.32.prefix_ref, f32[2,6,8,512]{3,2,1,0:T(8,128)S(1)} %get-tuple-element.108.ring_rows_ref, ...), custom_call_target="tpu_custom_call" | custom-call | tf_op jit(solution)/shard_map/second_substep/pallas_call | solution.py:43
  48.5 1.0 %deeper_pressure.1 = f32[5,128,512]{2,1,0:T(8,128)} custom-call(f32[5,128,512]{2,1,0:T(8,128)} %get-tuple-element.115.out_in_hbm, f32[2,128,512]{2,1,0:T(8,128)S(1)} %get-tuple-element.116.flow_ref, s32[128,512]{1,0:T(8,128)S(1)} %bitcast.18, f32[24,1280]{1,0:T(8,128)S(1)} %collective-permute-done.42.sums_ref, ...), custom_call_target="tpu_custom_call", output_to_operand_aliasing={{}: (0, {})} | custom-call | tf_op jit(solution)/shard_map/deeper_pressure/pallas_call | solution.py:43
  (31 shorter events, 2.5 us)
Async XLA Ops:
  0.0 7.2 %copy-start.2 = (s32[2048]{0:T(1024)S(1)}, s32[2048]{0:T(1024)}, u32[]{:S(2)}) copy-start(s32[2048]{0:T(1024)} %partner_ref.5) | copy-start | bytes 24580
  0.0 8.4 %copy-start.1 = (s32[8,16,512]{2,1,0:T(8,128)S(1)}, s32[8,16,512]{2,1,0:T(8,128)}, u32[]{:S(2)}) copy-start(s32[8,16,512]{2,1,0:T(8,128)} %param.25) | copy-start | bytes 786436
  0.0 8.4 %copy-start = (f32[5,8,16,512]{3,2,1,0:T(8,128)S(1)}, f32[5,8,16,512]{3,2,1,0:T(8,128)}, u32[]{:S(2)}) copy-start(f32[5,8,16,512]{3,2,1,0:T(8,128)} %param.24) | copy-start | bytes 3932164
  0.0 8.4 %copy-start.3 = (f32[16]{0:T(128)S(1)}, f32[16]{0:T(128)}, u32[]{:S(2)}) copy-start(f32[16]{0:T(128)} %turn_ref.7) | copy-start | bytes 196
  0.0 8.4 %copy-start.4 = (f32[8]{0:T(128)S(1)}, f32[8]{0:T(128)}, u32[]{:S(2)}) copy-start(f32[8]{0:T(128)} %share_ref.5) | copy-start | bytes 100
  2.5 7.5 %collective-permute-start.33 = (f32[64,1920]{1,0:T(8,128)S(1)}, f32[64,1920]{1,0:T(8,128)S(1)}, u32[]{:S(2)}, u32[]{:S(2)}) collective-permute-start(f32[64,1920]{1,0:T(8,128)S(1)} %get-tuple-element.79), channel_id=1, source_target_pairs={{0,2},{2,0},{4,6},{6,4},{1,3},{3,1},{5,7},{7,5},{8,10},{10,8},{12,... | collective-permute-start | bytes 1474568 | tf_op jit(solution)/shard_map/ppermute | solution.py:823
  2.6 7.4 %collective-permute-start.32 = (f32[16,512]{1,0:T(8,128)S(1)}, f32[16,512]{1,0:T(8,128)S(1)}, u32[]{:S(2)}, u32[]{:S(2)}) collective-permute-start(f32[16,512]{1,0:T(8,128)S(1)} %get-tuple-element.83), channel_id=1, source_target_pairs={{0,1},{2,3},{4,5},{6,7},{8,9},{10,11},{12,13},{14,15},{16,17},{18,... | collective-permute-start | bytes 98312 | tf_op jit(solution)/shard_map/ppermute | solution.py:824
  10.8 7.6 %collective-permute-start.34 = (f32[32,1920]{1,0:T(8,128)}, f32[32,1920]{1,0:T(8,128)}, u32[]{:S(2)}, u32[]{:S(2)}) collective-permute-start(f32[32,1920]{1,0:T(8,128)} %get-tuple-element.90), channel_id=1, source_target_pairs={{0,4},{2,6},{4,0},{6,2},{1,5},{3,7},{5,1},{7,3},{8,12},{10,14},{12... | collective-permute-start | bytes 737288 | tf_op jit(solution)/shard_map/ppermute | solution.py:832
  12.2 1.4 %collective-permute-start.23 = (f32[4,12,8,128]{3,2,1,0:T(8,128)S(1)}, f32[4,12,8,128]{3,2,1,0:T(8,128)S(1)}, u32[]{:S(2)}, u32[]{:S(2)}) collective-permute-start(f32[4,12,8,128]{3,2,1,0:T(8,128)S(1)} %param.11), channel_id=1, source_target_pairs={{6,22},{14,14},{22,6},{30,30},{7,23},{15,15},{23,7},{31,31}} | collective-permute-start | bytes 589832 | tf_op jit(solution)/shard_map/cond/branch_11_fun/ppermute | solution.py:858
  12.8 0.7 %collective-permute-start.22 = (f32[1,12,8,128]{3,2,1,0:T(8,128)S(1)}, f32[1,12,8,128]{3,2,1,0:T(8,128)S(1)}, u32[]{:S(2)}, u32[]{:S(2)}) collective-permute-start(f32[1,12,8,128]{3,2,1,0:T(8,128)S(1)} %slice.67), channel_id=1, source_target_pairs={{6,14},{14,6},{22,30},{30,22},{7,15},{15,7},{23,31},{31,23}} | collective-permute-start | bytes 147464 | tf_op jit(solution)/shard_map/cond/branch_11_fun/ppermute | solution.py:858
  19.3 19.6 %copy-start.5 = (f32[5,12,8,128]{3,2,1,0:T(8,128)S(1)}, f32[5,12,8,128]{3,2,1,0:T(8,128)}, u32[]{:S(2)}) copy-start(f32[5,12,8,128]{3,2,1,0:T(8,128)} %get-tuple-element.120.fold_ref) | copy-start | bytes 737284
  19.3 9.0 %collective-permute-start.37 = (f32[16,1920]{1,0:T(8,128)S(1)}, f32[16,1920]{1,0:T(8,128)S(1)}, u32[]{:S(2)}, u32[]{:S(2)}) collective-permute-start(f32[16,1920]{1,0:T(8,128)S(1)} %get-tuple-element.93), channel_id=1, source_target_pairs={{0,16},{8,24},{16,0},{24,8},{1,17},{9,25},{17,1},{25,9},{2,18},{10... | collective-permute-start | bytes 368648 | tf_op jit(solution)/shard_map/ppermute | solution.py:832
  22.7 3.0 %collective-permute-start.36 = (f32[24,128]{1,0:T(8,128)S(1)}, f32[24,128]{1,0:T(8,128)S(1)}, u32[]{:S(2)}, u32[]{:S(2)}) collective-permute-start(f32[24,128]{1,0:T(8,128)S(1)} %get-tuple-element.96.own_west_ref), channel_id=1, source_target_pairs={{8,0},{16,8},{24,16},{0,24},{9,1},{17,9},{25,17},{1,25},{10,2},{18... | collective-permute-start | bytes 36872 | tf_op jit(solution)/shard_map/ppermute | solution.py:879
  23.8 4.5 %collective-permute-start.35 = (f32[24,128]{1,0:T(8,128)S(1)}, f32[24,128]{1,0:T(8,128)S(1)}, u32[]{:S(2)}, u32[]{:S(2)}) collective-permute-start(f32[24,128]{1,0:T(8,128)S(1)} %get-tuple-element.97.own_east_ref), channel_id=1, source_target_pairs={{0,8},{8,16},{16,24},{24,0},{1,9},{9,17},{17,25},{25,1},{2,10},{10... | collective-permute-start | bytes 36872 | tf_op jit(solution)/shard_map/ppermute | solution.py:878
  29.1 5.8 %collective-permute-start.38 = (f32[12,8,512]{2,1,0:T(8,128)S(1)}, f32[12,8,512]{2,1,0:T(8,128)S(1)}, u32[]{:S(2)}, u32[]{:S(2)}) collective-permute-start(f32[12,8,512]{2,1,0:T(8,128)S(1)} %get-tuple-element.103), channel_id=1, source_target_pairs={{0,2},{2,0},{4,6},{6,4},{1,3},{3,1},{5,7},{7,5},{8,10},{10,8},{12,... | collective-permute-start | bytes 589832 | tf_op jit(solution)/shard_map/ppermute | solution.py:894
  31.8 7.0 %collective-permute-start.39 = (f32[12,8,512]{2,1,0:T(8,128)S(1)}, f32[12,8,512]{2,1,0:T(8,128)S(1)}, u32[]{:S(2)}, u32[]{:S(2)}) collective-permute-start(f32[12,8,512]{2,1,0:T(8,128)S(1)} %get-tuple-element.104), channel_id=1, source_target_pairs={{2,4},{4,2},{3,5},{5,3},{10,12},{12,10},{11,13},{13,11},{18,20},{2... | collective-permute-start | bytes 589832 | tf_op jit(solution)/shard_map/ppermute | solution.py:895
  34.9 3.9 %collective-permute-start.40 = (f32[8,1920]{1,0:T(8,128)S(1)}, f32[8,1920]{1,0:T(8,128)S(1)}, u32[]{:S(2)}, u32[]{:S(2)}) collective-permute-start(f32[8,1920]{1,0:T(8,128)S(1)} %get-tuple-element.100), channel_id=1, source_target_pairs={{0,8},{8,0},{16,24},{24,16},{1,9},{9,1},{17,25},{25,17},{2,10},{10... | collective-permute-start | bytes 184328 | tf_op jit(solution)/shard_map/ppermute | solution.py:832
  38.8 3.1 %collective-permute-start.41 = (f32[8,1920]{1,0:T(8,128)S(1)}, f32[8,1920]{1,0:T(8,128)S(1)}, u32[]{:S(2)}, u32[]{:S(2)}) collective-permute-start(f32[8,1920]{1,0:T(8,128)S(1)} %add.3.mine_ref), channel_id=1, source_target_pairs={{0,1},{1,0},{2,3},{3,2},{4,5},{5,4},{6,7},{7,6},{8,9},{9,8},{10,11... | collective-permute-start | bytes 184328 | tf_op jit(solution)/shard_map/ppermute | solution.py:898
  41.9 6.6 %collective-permute-start.42 = (f32[24,1280]{1,0:T(8,128)S(1)}, f32[24,1280]{1,0:T(8,128)S(1)}, u32[]{:S(2)}, u32[]{:S(2)}) collective-permute-start(f32[24,1280]{1,0:T(8,128)S(1)} %get-tuple-element.118), channel_id=1, source_target_pairs={{0,1},{2,3},{4,5},{6,7},{8,9},{10,11},{12,13},{14,15},{16,17},{18,... | collective-permute-start | bytes 368648 | tf_op jit(solution)/shard_map/ppermute | solution.py:919

commit v2 on v1

--- a/solution.py
+++ b/solution.py
@@ -23,7 +23,7 @@
 ABOVE = 56
 SLABS = 11
 CORNERS = SLABS
-VMEM_BYTES = 24 * 1024 * 1024
+VMEM_BYTES = 16 * 1024 * 1024
 
 VMEM = pl.BlockSpec(memory_space=pltpu.VMEM)
 SMEM = pl.BlockSpec(memory_space=pltpu.SMEM)
@@ -250,15 +250,10 @@
     east_ref[...] = east
 
 
-def top_kernel(state_ref, mask_ref, prefix_ref, top_ref):
+def top_kernel(own_north_ref, prefix_ref, top_ref):
     rows, cols = prefix_ref.shape
-    for slab in range(SLABS):
-        if slab < 10:
-            line = level_rows(state_ref.at[slab // 2], rows - 1 - slab % 2, rows)
-        else:
-            line = level_rows(mask_ref, rows - 1, rows).astype(F32)
-        for piece in range(cols // LANES):
-            top_ref[piece, slab] = line[:, piece * LANES : (piece + 1) * LANES]
+    for piece in range(cols // LANES):
+        top_ref[piece, 0:SLABS] = own_north_ref[:, :, piece * LANES : (piece + 1) * LANES]
     top_ref[:, CORNERS] = jnp.zeros((cols // LANES, DEEP, LANES), F32)
     for n in (1, 2):
         for piece in range(cols // LANES):
@@ -297,12 +292,12 @@
     out_ref[CORNERS, 4:5, :] = prefix_ref[far : far + 1, :]
 
 
-def rows_kernel(state_ref, mask_ref, prefix_ref, turn_ref, from_west_ref, from_east_ref, pair_ref, cross_ref):
+def rows_kernel(own_south_ref, own_north_ref, prefix_ref, turn_ref, from_west_ref, from_east_ref, pair_ref, cross_ref):
     rows = prefix_ref.shape[0]
     odd = lax.rem(lax.axis_index("lat"), 2) == 1
 
     def fill(out_ref, near, far):
-        edge_rows(state_ref, mask_ref, out_ref, rows, near, far)
+        out_ref[0:SLABS] = (own_south_ref if near == 0 else own_north_ref)[...]
         corner_slab(out_ref, prefix_ref, turn_ref, from_west_ref, from_east_ref, near, far)
 
     @pl.when(odd)
@@ -422,9 +417,11 @@
     return jnp.sum(here, axis=1, keepdims=True)
 
 
-def inside_kernel(state_ref, mask_ref, turn_ref, share_ref, new_ref, sums_ref):
+def inside_kernel(state_ref, mask_ref, turn_ref, share_ref, new_ref, sums_ref, south_ref, north_ref):
     rows, cols = sums_ref.shape[0], state_ref.shape[2]
     n_r, n_j = rows // DEEP, cols // LANES
+    edge_rows(state_ref, mask_ref, south_ref, rows, 0, 1)
+    edge_rows(state_ref, mask_ref, north_ref, rows, rows - 1, rows - 2)
     turn = turn_column(turn_ref, rows)
     grid = [(r, j) for r in range(n_r) for j in range(n_j)]
     zero = jnp.zeros((DEEP, LANES), F32)
@@ -460,7 +457,7 @@
 
 
 def rim_kernel(
-    n_lat, state_ref, mask_ref, prefix_ref, turn_ref, share_ref, partner_ref, own_west_ref, own_east_ref,
+    n_lat, own_south_ref, own_north_ref, prefix_ref, turn_ref, share_ref, partner_ref, own_west_ref, own_east_ref,
     from_west_ref, from_east_ref, pair_ref, cross_ref, fold_ref, inside_ref, ring_rows_ref, ring_cols_ref,
     edge_rows_ref, edge_cols_ref, sums_ref, south_ref, north_ref,
 ):
@@ -488,7 +485,8 @@
 
     @pl.when(lat == 0)
     def _():
-        edge_rows(state_ref, mask_ref, south_ref, rows, 0, 0)
+        for slab in range(SLABS):
+            south_ref[slab] = own_south_ref[slab if slab == 10 else slab - slab % 2]
         corner_slab(south_ref, prefix_ref, turn_ref, from_west_ref, from_east_ref, 0, 0)
 
     sub8, lane8 = iota((DEEP, LANES), 0), iota((DEEP, LANES), 1)
@@ -537,11 +535,12 @@
 
         return advanced(near, sides, wet, turn, pressed)
 
-    for side, ghost_ref, edge, inner in ((0, south_ref, 0, 1), (1, north_ref, rows - 1, rows - 2)):
+    for side, ghost_ref, own_ref in ((0, south_ref, own_south_ref), (1, north_ref, own_north_ref)):
+        edge, inner = (0, 1) if side == 0 else (rows - 1, rows - 2)
         near = [ghost_ref[2 * f] for f in range(5)]
         far = [ghost_ref[2 * f + 1] for f in range(5)]
-        own = [level_rows(state_ref.at[f], edge, rows) for f in range(5)]
-        own_next = [level_rows(state_ref.at[f], inner, rows) for f in range(5)]
+        own = [own_ref[2 * f] for f in range(5)]
+        own_next = [own_ref[2 * f + 1] for f in range(5)]
         ring_wet = ghost_ref[10]
         corners = ghost_ref[CORNERS, :, 0:LANES]
         above_near, above_far = ghost_ref[CORNERS, 3:4, :], ghost_ref[CORNERS, 4:5, :]
@@ -553,7 +552,7 @@
         )
         outward, inward = (near, above_near), (own_next, above_next)
         (south, above_south), (north, above_north) = (outward, inward) if side == 0 else (inward, outward)
-        wet = level_rows(mask_ref, edge, rows).astype(F32)
+        wet = own_ref[10]
         edge_line = slice(edge, edge + 1)
         new = row_step(
             own, south, north, from_west_ref[edge_line, :], from_east_ref[edge_line, :], wet, turn_ref[edge],
@@ -832,9 +831,10 @@
         return lax.ppermute(send, axis, [(i, i ^ bit) for i in range(size)])
 
     near_state, near_mask = after((flat_state, flat_mask), send)
-    new_state, inside = call(
+    own_rows = shape(SLABS, DEEP, cols)
+    new_state, inside, own_south, own_north = call(
         inside_kernel,
-        (shape(fields, levels * rows, cols), shape(rows, 2 * cols)),
+        (shape(fields, levels * rows, cols), shape(rows, 2 * cols), own_rows, own_rows),
         [VMEM, VMEM, SMEM, SMEM],
         (near_state, near_mask, coriolis, penetration),
         name="first_inside",
@@ -846,7 +846,7 @@
     got = passed_on(send, stages[0])
 
     top_shape = shape(pieces, SLABS + 1, DEEP, LANES)
-    top = call(top_kernel, top_shape, [VMEM] * 3, (flat_state, flat_mask, prefix), name="top_rows")
+    top = call(top_kernel, top_shape, [VMEM] * 2, (own_north, prefix), name="top_rows")
     top = after(top, send)
 
     def folded(hinge_piece):
@@ -882,22 +882,18 @@
         keep, send = merged(keep, got)
         got = passed_on(send, stage)
 
+    from_west, from_east = after((from_west, from_east), send)
     message = shape(SLABS + 1, DEEP, cols)
-    from_west, from_east = after((from_west, from_east), send)
     pair, cross = call(
         rows_kernel,
         (message, message),
         [VMEM, VMEM, VMEM, SMEM, VMEM, VMEM],
-        (flat_state, flat_mask, prefix, coriolis, from_west, from_east),
+        (own_south, own_north, prefix, coriolis, from_west, from_east),
         name="edge_rows",
     )
     from_pair = lax.ppermute(pair, "lat", [(i, i ^ 1) for i in range(n_lat)])
     from_cross = lax.ppermute(cross, "lat", [(i, i + 1 if i % 2 else i - 1) for i in range(1, last)])
-    keep = after(keep, (from_pair, from_cross))
-    mine = keep + got
-    theirs = lax.ppermute(mine, "lev", [(0, 1), (1, 0)])
-
-    inside = after(inside, mine)
+    inside = after(inside, send)
     wide = cols + LANES
     *ring, sums = call(
         functools.partial(rim_kernel, n_lat),
@@ -910,12 +906,15 @@
         ),
         [VMEM, VMEM, VMEM, SMEM, SMEM, SMEM] + [VMEM] * 8,
         (
-            flat_state, flat_mask, prefix, coriolis, penetration, fold_partner, west, east, from_west, from_east, from_pair,
+            own_south, own_north, prefix, coriolis, penetration, fold_partner, west, east, from_west, from_east, from_pair,
             from_cross, fold, inside,
         ),
         [pltpu.VMEM((SLABS + 1, DEEP, cols), F32), pltpu.VMEM((SLABS + 1, DEEP, cols), F32)],
         name="first_rim",
     )
+    keep = after(keep, sums)
+    mine = keep + got
+    theirs = lax.ppermute(mine, "lev", [(0, 1), (1, 0)])
     sums = lax.ppermute(after(sums, theirs), "lev", [(0, 1)])
     *flux, drive = call(
         functools.partial(flux_kernel, n_lat),

time: 49.7 us -> 49.3 us (level)
  the two profiles are of different devices: /device:TPU:1 before, /device:TPU:6 now
where the time goes in v2:
time: 49.3 us; the launch traced here: 48.7 us
  waiting for transfers between devices  20.3 us (41%)
  starting transfers between devices  13.9 us (28%)
  Pallas kernels  12.9 us (26%)
  between operations  0.83 us (2%)
  local copies, waits for them, and re-layouts  0.54 us (1%)
    pallas_call x12, Pallas kernels, call(): pl.pallas_call(kernel, out_shape=out_shape, in_specs=in_specs, out_specs=...  12.9 us
    ppermute x3, waiting for transfers between devices, passed_on(): return lax.ppermute(send, axis, [(i, i ^ bit) for i in range(size)])  5.2 us
    ppermute x1, waiting for transfers between devices, body(): lax.ppermute(cross, 'lat', [(i, i + 1 if i % 2 else i - 1) for i in range...  4.48 us
    ppermute x3, starting transfers between devices, passed_on(): return lax.ppermute(send, axis, [(i, i ^ bit) for i in range(size)])  3.3 us
    ppermute x1, waiting for transfers between devices, body(): lax.ppermute(east, 'lon', [(i, (i + 1) % n_lon) for i in range(n_lon)])  3.15 us
    ppermute x1, waiting for transfers between devices, body(): theirs = lax.ppermute(mine, 'lev', [(0, 1), (1, 0)])  2.55 us
    ppermute x1, starting transfers between devices, body(): lax.ppermute(cross, 'lat', [(i, i + 1 if i % 2 else i - 1) for i in range...  2.4 us
    ppermute x1, starting transfers between devices, body(): theirs = lax.ppermute(mine, 'lev', [(0, 1), (1, 0)])  2.05 us
  transfers between devices with their start and end apart: 13, of which 7 were waited for; matrix products, arithmetic and copies ran while one was open for 1% of the time, Pallas kernels for 18%

profile of v2, /device:TPU:6, one launch (start us, length us, event | category | flops | bytes accessed | tf_op | source)
XLA Modules:
  0.0 48.7 jit_solution(5080578538681747146)
XLA Ops:
  0.0 2.5 %prepare.1 = (f32[64,1920]{1,0:T(8,128)S(1)}, f32[64,1920]{1,0:T(8,128)S(1)}, f32[16,128]{1,0:T(8,128)S(1)}, f32[16,128]{1,0:T(8,128)S(1)}, f32[16,512]{1,0:T(8,128)S(1)}) custom-call(f32[5,128,512]{2,1,0:T(8,128)} %bitcast.7, s32[128,512]{1,0:T(8,128)} %bitcast.9, f32[3,128,512]{2,1,0:T(8,128)} %bitcast.13, s32[1,128]{1,0:T(1,128)} %bitcast.14, ...), custom_call_target="tpu_custom_call" | custom-call | tf_op jit(solution)/shard_map/prepare/pallas_call | solution.py:43
  2.6 1.3 %collective-permute-start.32 = (f32[16,512]{1,0:T(8,128)S(1)}, f32[16,512]{1,0:T(8,128)S(1)}, u32[]{:S(2)}, u32[]{:S(2)}) collective-permute-start(f32[16,512]{1,0:T(8,128)S(1)} %get-tuple-element.85), channel_id=1, source_target_pairs={{0,1},{2,3},{4,5},{6,7},{8,9},{10,11},{12,13},{14,15},{16,17},{18,... | collective-permute-start | bytes 98312 | tf_op jit(solution)/shard_map/ppermute | solution.py:823
  5.1 1.7 %first_inside.1 = (f32[5,128,512]{2,1,0:T(8,128)S(1)}, f32[16,1024]{1,0:T(8,128)S(1)}, f32[11,8,512]{2,1,0:T(8,128)S(1)}, f32[11,8,512]{2,1,0:T(8,128)S(1)}) custom-call(f32[5,128,512]{2,1,0:T(8,128)S(1)} %bitcast.8, s32[128,512]{1,0:T(8,128)S(1)} %bitcast.10, f32[16]{0:T(128)S(1)} %copy-done.3, f32[8]{0:T(128)S(1)} %copy-done.4), custom_call_target="tpu_custom_call" | custom-call | tf_op jit(solution)/shard_map/first_inside/pallas_call | solution.py:43
  6.9 1.5 %collective-permute-done.32.prefix_ref = f32[16,512]{1,0:T(8,128)S(1)} collective-permute-done((f32[16,512]{1,0:T(8,128)S(1)}, f32[16,512]{1,0:T(8,128)S(1)}, u32[]{:S(2)}, u32[]{:S(2)}) %collective-permute-start.32) | collective-permute-done | bytes 32800 | tf_op jit(solution)/shard_map/ppermute | solution.py:823
  9.1 1.5 %conditional.1 = (f32[5,12,8,128]{3,2,1,0:T(8,128)S(1)}) conditional(s32[]{:T(128)} %clamp.3, f32[4,12,8,128]{3,2,1,0:T(8,128)S(1)} %top_rows.1, f32[4,12,8,128]{3,2,1,0:T(8,128)S(1)} %top_rows.1, f32[4,12,8,128]{3,2,1,0:T(8,128)S(1)} %top_rows.1, f32[4,12,8,128]{3,2,1,0:T(8,128)S(1)} %top_rows.1, ...), branch_computations={%region_0.0_spmd, %region_1.0_spmd, %region_2.0_spmd, %region_3.0_... | conditional | flops 61440 | bytes 1966168 | solution.py:864
  9.1 0.7 %collective-permute-start.8 = (f32[4,12,8,128]{3,2,1,0:T(8,128)S(1)}, f32[4,12,8,128]{3,2,1,0:T(8,128)S(1)}, u32[]{:S(2)}, u32[]{:S(2)}) collective-permute-start(f32[4,12,8,128]{3,2,1,0:T(8,128)S(1)} %param.4), channel_id=1, source_target_pairs={{6,6},{14,30},{22,22},{30,14},{7,7},{15,31},{23,23},{31,15}} | collective-permute-start | bytes 589832 | tf_op jit(solution)/shard_map/cond/branch_4_fun/ppermute | solution.py:858
  9.8 0.7 %collective-permute-start.9 = (f32[1,12,8,128]{3,2,1,0:T(8,128)S(1)}, f32[1,12,8,128]{3,2,1,0:T(8,128)S(1)}, u32[]{:S(2)}, u32[]{:S(2)}) collective-permute-start(f32[1,12,8,128]{3,2,1,0:T(8,128)S(1)} %slice.56), channel_id=1, source_target_pairs={{6,14},{14,6},{22,30},{30,22},{7,15},{15,7},{23,31},{31,23}} | collective-permute-start | bytes 147464 | tf_op jit(solution)/shard_map/cond/branch_4_fun/ppermute | solution.py:858
  10.5 5.2 %collective-permute-done.34.got_ref = f32[32,1920]{1,0:T(8,128)S(1)} collective-permute-done((f32[32,1920]{1,0:T(8,128)S(1)}, f32[32,1920]{1,0:T(8,128)S(1)}, u32[]{:S(2)}, u32[]{:S(2)}) %collective-permute-start.34) | collective-permute-done | bytes 245792 | tf_op jit(solution)/shard_map/ppermute | solution.py:831
  15.8 2.7 %collective-permute-start.37 = (f32[16,1920]{1,0:T(8,128)S(1)}, f32[16,1920]{1,0:T(8,128)S(1)}, u32[]{:S(2)}, u32[]{:S(2)}) collective-permute-start(f32[16,1920]{1,0:T(8,128)S(1)} %get-tuple-element.97), channel_id=1, source_target_pairs={{0,16},{8,24},{16,0},{24,8},{1,17},{9,25},{17,1},{25,9},{2,18},{10... | collective-permute-start | bytes 368648 | tf_op jit(solution)/shard_map/ppermute | solution.py:831
  18.4 0.7 %edge_columns.1 = (f32[24,128]{1,0:T(8,128)S(1)}, f32[24,128]{1,0:T(8,128)S(1)}) custom-call(f32[16,128]{1,0:T(8,128)S(1)} %get-tuple-element.98.west_ref, f32[16,128]{1,0:T(8,128)S(1)} %get-tuple-element.99.east_ref, f32[16,512]{1,0:T(8,128)S(1)} %collective-permute-done.32.prefix_ref, f32[5,12,8,128]{3,2,1,0:T(8,128)S(1)} %get-tuple-element.124.fold_ref, ...), custom_call_target="tpu_custom_call" | custom-call | tf_op jit(solution)/shard_map/edge_columns/pallas_call | solution.py:43
  19.2 1.4 %collective-permute-start.36 = (f32[24,128]{1,0:T(8,128)S(1)}, f32[24,128]{1,0:T(8,128)S(1)}, u32[]{:S(2)}, u32[]{:S(2)}) collective-permute-start(f32[24,128]{1,0:T(8,128)S(1)} %get-tuple-element.100.own_west_ref), channel_id=1, source_target_pairs={{8,0},{16,8},{24,16},{0,24},{9,1},{17,9},{25,17},{1,25},{10,2},{18... | collective-permute-start | bytes 36872 | tf_op jit(solution)/shard_map/ppermute | solution.py:879
  20.5 0.7 %collective-permute-start.35 = (f32[24,128]{1,0:T(8,128)S(1)}, f32[24,128]{1,0:T(8,128)S(1)}, u32[]{:S(2)}, u32[]{:S(2)}) collective-permute-start(f32[24,128]{1,0:T(8,128)S(1)} %get-tuple-element.101.own_east_ref), channel_id=1, source_target_pairs={{0,8},{8,16},{16,24},{24,0},{1,9},{9,17},{17,25},{25,1},{2,10},{10... | collective-permute-start | bytes 36872 | tf_op jit(solution)/shard_map/ppermute | solution.py:878
  21.2 1.7 %collective-permute-done.36.from_east_ref = f32[24,128]{1,0:T(8,128)S(1)} collective-permute-done((f32[24,128]{1,0:T(8,128)S(1)}, f32[24,128]{1,0:T(8,128)S(1)}, u32[]{:S(2)}, u32[]{:S(2)}) %collective-permute-start.36) | collective-permute-done | bytes 12320 | tf_op jit(solution)/shard_map/ppermute | solution.py:879
  22.9 3.1 %collective-permute-done.35.from_west_ref = f32[24,128]{1,0:T(8,128)S(1)} collective-permute-done((f32[24,128]{1,0:T(8,128)S(1)}, f32[24,128]{1,0:T(8,128)S(1)}, u32[]{:S(2)}, u32[]{:S(2)}) %collective-permute-start.35) | collective-permute-done | bytes 12320 | tf_op jit(solution)/shard_map/ppermute | solution.py:878
  26.8 2.4 %collective-permute-start.39 = (f32[12,8,512]{2,1,0:T(8,128)S(1)}, f32[12,8,512]{2,1,0:T(8,128)S(1)}, u32[]{:S(2)}, u32[]{:S(2)}) collective-permute-start(f32[12,8,512]{2,1,0:T(8,128)S(1)} %get-tuple-element.108), channel_id=1, source_target_pairs={{2,4},{4,2},{3,5},{5,3},{10,12},{12,10},{11,13},{13,11},{18,20},{2... | collective-permute-start | bytes 589832 | tf_op jit(solution)/shard_map/ppermute | solution.py:895
  29.3 4.5 %collective-permute-done.39.cross_ref = f32[12,8,512]{2,1,0:T(8,128)S(1)} collective-permute-done((f32[12,8,512]{2,1,0:T(8,128)S(1)}, f32[12,8,512]{2,1,0:T(8,128)S(1)}, u32[]{:S(2)}, u32[]{:S(2)}) %collective-permute-start.39) | collective-permute-done | bytes 196640 | tf_op jit(solution)/shard_map/ppermute | solution.py:895
  33.8 2.5 %first_rim.1 = (f32[2,6,8,512]{3,2,1,0:T(8,128)S(1)}, f32[2,16,128]{2,1,0:T(8,128)S(1)}, f32[2,5,8,512]{3,2,1,0:T(8,128)S(1)}, f32[2,16,128]{2,1,0:T(8,128)S(1)}, f32[24,1280]{1,0:T(8,128)S(1)}) custom-call(f32[11,8,512]{2,1,0:T(8,128)S(1)} %get-tuple-element.86.own_south_ref, f32[11,8,512]{2,1,0:T(8,128)S(1)} %get-tuple-element.87.own_north_ref, ...), custom_call_target="tpu_custom_call" | custom-call | tf_op jit(solution)/shard_map/first_rim/pallas_call | solution.py:43
  36.3 2.0 %collective-permute-start.41 = (f32[8,1920]{1,0:T(8,128)S(1)}, f32[8,1920]{1,0:T(8,128)S(1)}, u32[]{:S(2)}, u32[]{:S(2)}) collective-permute-start(f32[8,1920]{1,0:T(8,128)S(1)} %add.3.mine_ref), channel_id=1, source_target_pairs={{0,1},{1,0},{2,3},{3,2},{4,5},{5,4},{6,7},{7,6},{8,9},{9,8},{10,11... | collective-permute-start | bytes 184328 | tf_op jit(solution)/shard_map/ppermute | solution.py:917
  38.4 2.5 %collective-permute-done.41.theirs_ref = f32[8,1920]{1,0:T(8,128)S(1)} collective-permute-done((f32[8,1920]{1,0:T(8,128)S(1)}, f32[8,1920]{1,0:T(8,128)S(1)}, u32[]{:S(2)}, u32[]{:S(2)}) %collective-permute-start.41) | collective-permute-done | bytes 61472 | tf_op jit(solution)/shard_map/ppermute | solution.py:917
  40.9 1.3 %collective-permute-start.42 = (f32[24,1280]{1,0:T(8,128)S(1)}, f32[24,1280]{1,0:T(8,128)S(1)}, u32[]{:S(2)}, u32[]{:S(2)}) collective-permute-start(f32[24,1280]{1,0:T(8,128)S(1)} %get-tuple-element.122), channel_id=1, source_target_pairs={{0,1},{2,3},{4,5},{6,7},{8,9},{10,11},{12,13},{14,15},{16,17},{18,... | collective-permute-start | bytes 368648 | tf_op jit(solution)/shard_map/ppermute | solution.py:918
  42.2 0.9 %flux_parts.1 = (f32[3,16,512]{2,1,0:T(8,128)S(1)}, f32[8,512]{1,0:T(8,128)S(1)}, f32[16,128]{1,0:T(8,128)S(1)}, f32[24,640]{1,0:T(8,128)S(1)}) custom-call(f32[8,1920]{1,0:T(8,128)S(1)} %add.3.mine_ref, f32[8,1920]{1,0:T(8,128)S(1)} %collective-permute-done.41.theirs_ref, s32[2048]{0:T(1024)S(1)} %copy-done.2), custom_call_target="tpu_custom_call" | custom-call | tf_op jit(solution)/shard_map/flux_parts/pallas_call | solution.py:43
  43.1 2.8 %second_substep.1 = (f32[5,128,512]{2,1,0:T(8,128)}, f32[2,128,512]{2,1,0:T(8,128)S(1)}) custom-call(f32[5,128,512]{2,1,0:T(8,128)S(1)} %get-tuple-element.84.state_ref, s32[128,512]{1,0:T(8,128)S(1)} %bitcast.11, f32[16,512]{1,0:T(8,128)S(1)} %collective-permute-done.32.prefix_ref, f32[2,6,8,512]{3,2,1,0:T(8,128)S(1)} %get-tuple-element.110.ring_rows_ref, ...), custom_call_target="tpu_custom_call" | custom-call | tf_op jit(solution)/shard_map/second_substep/pallas_call | solution.py:43
  45.9 1.8 %collective-permute-done.42.sums_ref = f32[24,1280]{1,0:T(8,128)S(1)} collective-permute-done((f32[24,1280]{1,0:T(8,128)S(1)}, f32[24,1280]{1,0:T(8,128)S(1)}, u32[]{:S(2)}, u32[]{:S(2)}) %collective-permute-start.42) | collective-permute-done | bytes 122912 | tf_op jit(solution)/shard_map/ppermute | solution.py:918
  47.7 1.0 %deeper_pressure.1 = f32[5,128,512]{2,1,0:T(8,128)} custom-call(f32[5,128,512]{2,1,0:T(8,128)} %get-tuple-element.120.out_in_hbm, f32[2,128,512]{2,1,0:T(8,128)S(1)} %get-tuple-element.121.flow_ref, s32[128,512]{1,0:T(8,128)S(1)} %bitcast.12, f32[24,1280]{1,0:T(8,128)S(1)} %collective-permute-done.42.sums_ref, ...), custom_call_target="tpu_custom_call", output_to_operand_aliasing={{}: (0, {})} | custom-call | tf_op jit(solution)/shard_map/deeper_pressure/pallas_call | solution.py:43
  (29 shorter events, 2.2 us)
Async XLA Ops:
  0.0 3.9 %copy-start.2 = (s32[2048]{0:T(1024)S(1)}, s32[2048]{0:T(1024)}, u32[]{:S(2)}) copy-start(s32[2048]{0:T(1024)} %partner_ref.5) | copy-start | bytes 24580
  0.0 5.1 %copy-start.1 = (s32[8,16,512]{2,1,0:T(8,128)S(1)}, s32[8,16,512]{2,1,0:T(8,128)}, u32[]{:S(2)}) copy-start(s32[8,16,512]{2,1,0:T(8,128)} %param.25) | copy-start | bytes 786436
  0.0 5.1 %copy-start = (f32[5,8,16,512]{3,2,1,0:T(8,128)S(1)}, f32[5,8,16,512]{3,2,1,0:T(8,128)}, u32[]{:S(2)}) copy-start(f32[5,8,16,512]{3,2,1,0:T(8,128)} %param.24) | copy-start | bytes 3932164
  0.0 5.1 %copy-start.3 = (f32[16]{0:T(128)S(1)}, f32[16]{0:T(128)}, u32[]{:S(2)}) copy-start(f32[16]{0:T(128)} %turn_ref.7) | copy-start | bytes 196
  0.0 5.1 %copy-start.4 = (f32[8]{0:T(128)S(1)}, f32[8]{0:T(128)}, u32[]{:S(2)}) copy-start(f32[8]{0:T(128)} %share_ref.5) | copy-start | bytes 100
  2.5 5.9 %collective-permute-start.33 = (f32[64,1920]{1,0:T(8,128)S(1)}, f32[64,1920]{1,0:T(8,128)S(1)}, u32[]{:S(2)}, u32[]{:S(2)}) collective-permute-start(f32[64,1920]{1,0:T(8,128)S(1)} %get-tuple-element.81), channel_id=1, source_target_pairs={{0,2},{2,0},{4,6},{6,4},{1,3},{3,1},{5,7},{7,5},{8,10},{10,8},{12,... | collective-permute-start | bytes 1474568 | tf_op jit(solution)/shard_map/ppermute | solution.py:822
  2.6 5.8 %collective-permute-start.32 = (f32[16,512]{1,0:T(8,128)S(1)}, f32[16,512]{1,0:T(8,128)S(1)}, u32[]{:S(2)}, u32[]{:S(2)}) collective-permute-start(f32[16,512]{1,0:T(8,128)S(1)} %get-tuple-element.85), channel_id=1, source_target_pairs={{0,1},{2,3},{4,5},{6,7},{8,9},{10,11},{12,13},{14,15},{16,17},{18,... | collective-permute-start | bytes 98312 | tf_op jit(solution)/shard_map/ppermute | solution.py:823
  8.5 7.3 %collective-permute-start.34 = (f32[32,1920]{1,0:T(8,128)S(1)}, f32[32,1920]{1,0:T(8,128)S(1)}, u32[]{:S(2)}, u32[]{:S(2)}) collective-permute-start(f32[32,1920]{1,0:T(8,128)S(1)} %get-tuple-element.94), channel_id=1, source_target_pairs={{0,4},{2,6},{4,0},{6,2},{1,5},{3,7},{5,1},{7,3},{8,12},{10,14},{12... | collective-permute-start | bytes 737288 | tf_op jit(solution)/shard_map/ppermute | solution.py:831
  9.1 1.4 %collective-permute-start.8 = (f32[4,12,8,128]{3,2,1,0:T(8,128)S(1)}, f32[4,12,8,128]{3,2,1,0:T(8,128)S(1)}, u32[]{:S(2)}, u32[]{:S(2)}) collective-permute-start(f32[4,12,8,128]{3,2,1,0:T(8,128)S(1)} %param.4), channel_id=1, source_target_pairs={{6,6},{14,30},{22,22},{30,14},{7,7},{15,31},{23,23},{31,15}} | collective-permute-start | bytes 589832 | tf_op jit(solution)/shard_map/cond/branch_4_fun/ppermute | solution.py:858
  9.8 0.7 %collective-permute-start.9 = (f32[1,12,8,128]{3,2,1,0:T(8,128)S(1)}, f32[1,12,8,128]{3,2,1,0:T(8,128)S(1)}, u32[]{:S(2)}, u32[]{:S(2)}) collective-permute-start(f32[1,12,8,128]{3,2,1,0:T(8,128)S(1)} %slice.56), channel_id=1, source_target_pairs={{6,14},{14,6},{22,30},{30,22},{7,15},{15,7},{23,31},{31,23}} | collective-permute-start | bytes 147464 | tf_op jit(solution)/shard_map/cond/branch_4_fun/ppermute | solution.py:858
  15.8 10.3 %collective-permute-start.37 = (f32[16,1920]{1,0:T(8,128)S(1)}, f32[16,1920]{1,0:T(8,128)S(1)}, u32[]{:S(2)}, u32[]{:S(2)}) collective-permute-start(f32[16,1920]{1,0:T(8,128)S(1)} %get-tuple-element.97), channel_id=1, source_target_pairs={{0,16},{8,24},{16,0},{24,8},{1,17},{9,25},{17,1},{25,9},{2,18},{10... | collective-permute-start | bytes 368648 | tf_op jit(solution)/shard_map/ppermute | solution.py:831
  19.2 3.7 %collective-permute-start.36 = (f32[24,128]{1,0:T(8,128)S(1)}, f32[24,128]{1,0:T(8,128)S(1)}, u32[]{:S(2)}, u32[]{:S(2)}) collective-permute-start(f32[24,128]{1,0:T(8,128)S(1)} %get-tuple-element.100.own_west_ref), channel_id=1, source_target_pairs={{8,0},{16,8},{24,16},{0,24},{9,1},{17,9},{25,17},{1,25},{10,2},{18... | collective-permute-start | bytes 36872 | tf_op jit(solution)/shard_map/ppermute | solution.py:879
  20.5 5.5 %collective-permute-start.35 = (f32[24,128]{1,0:T(8,128)S(1)}, f32[24,128]{1,0:T(8,128)S(1)}, u32[]{:S(2)}, u32[]{:S(2)}) collective-permute-start(f32[24,128]{1,0:T(8,128)S(1)} %get-tuple-element.101.own_east_ref), channel_id=1, source_target_pairs={{0,8},{8,16},{16,24},{24,0},{1,9},{9,17},{17,25},{25,1},{2,10},{10... | collective-permute-start | bytes 36872 | tf_op jit(solution)/shard_map/ppermute | solution.py:878
  26.6 2.7 %collective-permute-start.38 = (f32[12,8,512]{2,1,0:T(8,128)S(1)}, f32[12,8,512]{2,1,0:T(8,128)S(1)}, u32[]{:S(2)}, u32[]{:S(2)}) collective-permute-start(f32[12,8,512]{2,1,0:T(8,128)S(1)} %get-tuple-element.107), channel_id=1, source_target_pairs={{0,2},{2,0},{4,6},{6,4},{1,3},{3,1},{5,7},{7,5},{8,10},{10,8},{12,... | collective-permute-start | bytes 589832 | tf_op jit(solution)/shard_map/ppermute | solution.py:894
  26.8 7.0 %collective-permute-start.39 = (f32[12,8,512]{2,1,0:T(8,128)S(1)}, f32[12,8,512]{2,1,0:T(8,128)S(1)}, u32[]{:S(2)}, u32[]{:S(2)}) collective-permute-start(f32[12,8,512]{2,1,0:T(8,128)S(1)} %get-tuple-element.108), channel_id=1, source_target_pairs={{2,4},{4,2},{3,5},{5,3},{10,12},{12,10},{11,13},{13,11},{18,20},{2... | collective-permute-start | bytes 589832 | tf_op jit(solution)/shard_map/ppermute | solution.py:895
  29.2 7.1 %collective-permute-start.40 = (f32[8,1920]{1,0:T(8,128)S(1)}, f32[8,1920]{1,0:T(8,128)S(1)}, u32[]{:S(2)}, u32[]{:S(2)}) collective-permute-start(f32[8,1920]{1,0:T(8,128)S(1)} %get-tuple-element.104), channel_id=1, source_target_pairs={{0,8},{8,0},{16,24},{24,16},{1,9},{9,1},{17,25},{25,17},{2,10},{10... | collective-permute-start | bytes 184328 | tf_op jit(solution)/shard_map/ppermute | solution.py:831
  36.3 4.6 %collective-permute-start.41 = (f32[8,1920]{1,0:T(8,128)S(1)}, f32[8,1920]{1,0:T(8,128)S(1)}, u32[]{:S(2)}, u32[]{:S(2)}) collective-permute-start(f32[8,1920]{1,0:T(8,128)S(1)} %add.3.mine_ref), channel_id=1, source_target_pairs={{0,1},{1,0},{2,3},{3,2},{4,5},{5,4},{6,7},{7,6},{8,9},{9,8},{10,11... | collective-permute-start | bytes 184328 | tf_op jit(solution)/shard_map/ppermute | solution.py:917
  40.9 6.8 %collective-permute-start.42 = (f32[24,1280]{1,0:T(8,128)S(1)}, f32[24,1280]{1,0:T(8,128)S(1)}, u32[]{:S(2)}, u32[]{:S(2)}) collective-permute-start(f32[24,1280]{1,0:T(8,128)S(1)} %get-tuple-element.122), channel_id=1, source_target_pairs={{0,1},{2,3},{4,5},{6,7},{8,9},{10,11},{12,13},{14,15},{16,17},{18,... | collective-permute-start | bytes 368648 | tf_op jit(solution)/shard_map/ppermute | solution.py:918

commit v3 on v0

--- a/solution.py
+++ b/solution.py
@@ -23,7 +23,7 @@
 ABOVE = 56
 SLABS = 11
 CORNERS = SLABS
-VMEM_BYTES = 24 * 1024 * 1024
+VMEM_BYTES = 16 * 1024 * 1024
 
 VMEM = pl.BlockSpec(memory_space=pltpu.VMEM)
 SMEM = pl.BlockSpec(memory_space=pltpu.SMEM)
@@ -278,12 +278,15 @@
     def _():
         within = partner_ref[0] & (LANES - 1)
         sub8, lane8 = iota((DEEP, LANES), 0), iota((DEEP, LANES), 1)
-        col = iota((DEEP, cols + LANES), 1)
-        for place, out_ref in ((cols + within, west_out_ref), (within + 1, east_out_ref)):
+        for out_ref in (west_out_ref, east_out_ref):
             line = jnp.zeros((DEEP, LANES), F32)
             for slab in (0, 2, 4, 6, 8, CORNERS):
-                line_there = jnp.concatenate([fold_ref[piece, slab] for piece in range(fold_ref.shape[0])], axis=1)
-                cell = jnp.sum(jnp.where(col == place, line_there, 0.0), axis=1, keepdims=True)
+                if out_ref is west_out_ref:
+                    cell = jnp.where(lane8 == within, fold_ref[fold_ref.shape[0] - 1, slab], 0.0)
+                else:
+                    cell = jnp.where(lane8 == within + 1, fold_ref[0, slab], 0.0)
+                    cell = jnp.where((lane8 == 0) & (within == LANES - 1), fold_ref[1, slab], cell)
+                cell = jnp.sum(cell, axis=1, keepdims=True)
                 here = (lane8 == ABOVE) & (sub8 == 3) if slab == CORNERS else lane8 == (slab // 2) * DEEP + sub8
                 line = jnp.where(here, -cell if slab < 4 else cell, line)
             out_ref[rows : rows + 1, :] = jnp.sum(line, axis=0, keepdims=True)
@@ -854,11 +857,6 @@
         return swap
 
     fold = lax.switch(hinge_piece, [folded(n) for n in range(n_lon * pieces)], top)
-    keep = after(keep, fold)
-    keep, send = merged(keep, got)
-    got = passed_on(send, stages[1])
-
-    west, east = after((west, east), send)
     side = shape(rows + DEEP, LANES)
     west, east = call(
         functools.partial(columns_kernel, n_lat),
@@ -869,6 +867,11 @@
     )
     from_west = lax.ppermute(east, "lon", [(i, (i + 1) % n_lon) for i in range(n_lon)])
     from_east = lax.ppermute(west, "lon", [((i + 1) % n_lon, i) for i in range(n_lon)])
+    keep = after(keep, (from_west, from_east))
+    keep, send = merged(keep, got)
+    got = passed_on(send, stages[1])
+
+    from_west, from_east = after((from_west, from_east), send)
     pair, cross = call(
         rows_kernel,
         (message, message),

time: 45.5 us -> 44.6 us (0.980); the launches traced: 45.4 us -> 44 us
  waiting for transfers between devices: 16.9 us -> 9.68 us
  starting transfers between devices: 14.2 us -> 19.9 us
    ppermute x3, waiting for transfers between devices: 6.99 us -> 0.87 us  [passed_on(): return lax.ppermute(send, axis, [(i, i ^ bit) for i in range(size)])]
    ppermute x1, starting transfers between devices: 0.18 us -> 5.25 us  [body(): from_pair = lax.ppermute(pair, 'lat', [(i, i ^ 1) for i in range(n_lat)])]
    ppermute x1, waiting for transfers between devices: 1.14 us -> 0.01 us  [body(): lax.ppermute(west, 'lon', [((i + 1) % n_lon, i) for i in range(n_lon)])]
    ppermute x3, starting transfers between devices: 4.02 us -> 4.86 us  [passed_on(): return lax.ppermute(send, axis, [(i, i ^ bit) for i in range(size)])]
  transfers between devices with their start and end apart: 13 -> 13, of which waited for: 8 -> 6; matrix products, arithmetic and copies ran while one was open for 1% -> 1% of each run, Pallas kernels for 19% -> 19%
where the time goes in v3:
time: 44.6 us; the launch traced here: 44 us
  starting transfers between devices  19.9 us (45%)
  Pallas kernels  12.9 us (29%)
  waiting for transfers between devices  9.68 us (22%)
  between operations  0.81 us (2%)
  local copies, waits for them, and re-layouts  0.56 us (1%)
    pallas_call x12, Pallas kernels, call(): pl.pallas_call(kernel, out_shape=out_shape, in_specs=in_specs, out_specs=...  12.9 us
    ppermute x1, starting transfers between devices, body(): from_pair = lax.ppermute(pair, 'lat', [(i, i ^ 1) for i in range(n_lat)])  5.25 us
    ppermute x3, starting transfers between devices, passed_on(): return lax.ppermute(send, axis, [(i, i ^ bit) for i in range(size)])  4.86 us
    ppermute x1, waiting for transfers between devices, body(): prefix = lax.ppermute(total, 'lev', [(0, 1)])  3.33 us
    ppermute x1, starting transfers between devices, body(): lax.ppermute(west, 'lon', [((i + 1) % n_lon, i) for i in range(n_lon)])  2.24 us
    ppermute x1, waiting for transfers between devices, body(): above = lax.ppermute(above, 'lev', [(0, 1)])  1.99 us
    ppermute x1, starting transfers between devices, body(): lax.ppermute(cross, 'lat', [(i, i + 1 if i % 2 else i - 1) for i in range...  1.91 us
    ppermute x1, waiting for transfers between devices, body(): lax.ppermute(east, 'lon', [(i, (i + 1) % n_lon) for i in range(n_lon)])  1.8 us
  transfers between devices with their start and end apart: 13, of which 6 were waited for; matrix products, arithmetic and copies ran while one was open for 1% of the time, Pallas kernels for 19%

profile of v3, /device:TPU:6, one launch (start us, length us, event | category | flops | bytes accessed | tf_op | source)
XLA Modules:
  0.0 44.0 jit_solution(8677438780912230407)
XLA Ops:
  0.0 2.5 %prepare.1 = (f32[64,1920]{1,0:T(8,128)S(1)}, f32[64,1920]{1,0:T(8,128)S(1)}, f32[16,128]{1,0:T(8,128)S(1)}, f32[16,128]{1,0:T(8,128)S(1)}, f32[16,512]{1,0:T(8,128)S(1)}) custom-call(f32[5,128,512]{2,1,0:T(8,128)} %bitcast.7, s32[128,512]{1,0:T(8,128)} %bitcast.12, f32[3,128,512]{2,1,0:T(8,128)} %bitcast.19, s32[1,128]{1,0:T(1,128)} %bitcast.20, ...), custom_call_target="tpu_custom_call" | custom-call | tf_op jit(solution)/shard_map/prepare/pallas_call | solution.py:43
  2.6 1.3 %collective-permute-start.32 = (f32[16,512]{1,0:T(8,128)S(1)}, f32[16,512]{1,0:T(8,128)S(1)}, u32[]{:S(2)}, u32[]{:S(2)}) collective-permute-start(f32[16,512]{1,0:T(8,128)S(1)} %get-tuple-element.77), channel_id=1, source_target_pairs={{0,1},{2,3},{4,5},{6,7},{8,9},{10,11},{12,13},{14,15},{16,17},{18,... | collective-permute-start | bytes 98312 | tf_op jit(solution)/shard_map/ppermute | solution.py:826
  5.1 3.3 %collective-permute-done.32.prefix_ref = f32[16,512]{1,0:T(8,128)S(1)} collective-permute-done((f32[16,512]{1,0:T(8,128)S(1)}, f32[16,512]{1,0:T(8,128)S(1)}, u32[]{:S(2)}, u32[]{:S(2)}) %collective-permute-start.32) | collective-permute-done | bytes 32800 | tf_op jit(solution)/shard_map/ppermute | solution.py:826
  9.1 1.5 %conditional.1 = (f32[5,12,8,128]{3,2,1,0:T(8,128)S(1)}) conditional(s32[]{:T(128)} %clamp.3, f32[4,12,8,128]{3,2,1,0:T(8,128)S(1)} %top_rows.1, f32[4,12,8,128]{3,2,1,0:T(8,128)S(1)} %top_rows.1, f32[4,12,8,128]{3,2,1,0:T(8,128)S(1)} %top_rows.1, f32[4,12,8,128]{3,2,1,0:T(8,128)S(1)} %top_rows.1, ...), branch_computations={%region_0.0_spmd, %region_1.0_spmd, %region_2.0_spmd, %region_3.0_... | conditional | flops 61440 | bytes 1966168 | solution.py:859
  9.2 0.7 %collective-permute-start.13 = (f32[3,12,8,128]{3,2,1,0:T(8,128)S(1)}, f32[3,12,8,128]{3,2,1,0:T(8,128)S(1)}, u32[]{:S(2)}, u32[]{:S(2)}) collective-permute-start(f32[3,12,8,128]{3,2,1,0:T(8,128)S(1)} %slice.60), channel_id=1, source_target_pairs={{6,14},{14,6},{22,30},{30,22},{7,15},{15,7},{23,31},{31,23}} | collective-permute-start | bytes 442376 | tf_op jit(solution)/shard_map/cond/branch_6_fun/ppermute | solution.py:853
  9.9 0.7 %collective-permute-start.12 = (f32[2,12,8,128]{3,2,1,0:T(8,128)S(1)}, f32[2,12,8,128]{3,2,1,0:T(8,128)S(1)}, u32[]{:S(2)}, u32[]{:S(2)}) collective-permute-start(f32[2,12,8,128]{3,2,1,0:T(8,128)S(1)} %slice.59), channel_id=1, source_target_pairs={{6,6},{14,30},{22,22},{30,14},{7,7},{15,31},{23,23},{31,15}} | collective-permute-start | bytes 294920 | tf_op jit(solution)/shard_map/cond/branch_6_fun/ppermute | solution.py:853
  10.6 0.7 %edge_columns.1 = (f32[24,128]{1,0:T(8,128)S(1)}, f32[24,128]{1,0:T(8,128)S(1)}) custom-call(f32[16,128]{1,0:T(8,128)S(1)} %get-tuple-element.81.west_ref, f32[16,128]{1,0:T(8,128)S(1)} %get-tuple-element.82.east_ref, f32[16,512]{1,0:T(8,128)S(1)} %collective-permute-done.32.prefix_ref, f32[5,12,8,128]{3,2,1,0:T(8,128)S(1)} %get-tuple-element.114.fold_ref, ...), custom_call_target="tpu_custom_call" | custom-call | tf_op jit(solution)/shard_map/edge_columns/pallas_call | solution.py:43
  11.4 1.6 %collective-permute-start.34 = (f32[24,128]{1,0:T(8,128)S(1)}, f32[24,128]{1,0:T(8,128)S(1)}, u32[]{:S(2)}, u32[]{:S(2)}) collective-permute-start(f32[24,128]{1,0:T(8,128)S(1)} %get-tuple-element.85.own_east_ref), channel_id=1, source_target_pairs={{0,8},{8,16},{16,24},{24,0},{1,9},{9,17},{17,25},{25,1},{2,10},{10... | collective-permute-start | bytes 36872 | tf_op jit(solution)/shard_map/ppermute | solution.py:868
  13.0 2.2 %collective-permute-start.35 = (f32[24,128]{1,0:T(8,128)S(1)}, f32[24,128]{1,0:T(8,128)S(1)}, u32[]{:S(2)}, u32[]{:S(2)}) collective-permute-start(f32[24,128]{1,0:T(8,128)S(1)} %get-tuple-element.86.own_west_ref), channel_id=1, source_target_pairs={{8,0},{16,8},{24,16},{0,24},{9,1},{17,9},{25,17},{1,25},{10,2},{18... | collective-permute-start | bytes 36872 | tf_op jit(solution)/shard_map/ppermute | solution.py:869
  15.2 1.8 %collective-permute-done.34.from_west_ref = f32[24,128]{1,0:T(8,128)S(1)} collective-permute-done((f32[24,128]{1,0:T(8,128)S(1)}, f32[24,128]{1,0:T(8,128)S(1)}, u32[]{:S(2)}, u32[]{:S(2)}) %collective-permute-start.34) | collective-permute-done | bytes 12320 | tf_op jit(solution)/shard_map/ppermute | solution.py:868
  17.0 2.3 %collective-permute-start.37 = (f32[16,1920]{1,0:T(8,128)S(1)}, f32[16,1920]{1,0:T(8,128)S(1)}, u32[]{:S(2)}, u32[]{:S(2)}) collective-permute-start(f32[16,1920]{1,0:T(8,128)S(1)} %get-tuple-element.89), channel_id=1, source_target_pairs={{0,16},{8,24},{16,0},{24,8},{1,17},{9,25},{17,1},{25,9},{2,18},{10... | collective-permute-start | bytes 368648 | tf_op jit(solution)/shard_map/ppermute | solution.py:834
  19.4 0.7 %edge_rows.1 = (f32[12,8,512]{2,1,0:T(8,128)S(1)}, f32[12,8,512]{2,1,0:T(8,128)S(1)}) custom-call(f32[5,128,512]{2,1,0:T(8,128)S(1)} %bitcast.9, s32[128,512]{1,0:T(8,128)S(1)} %bitcast.14, f32[16,512]{1,0:T(8,128)S(1)} %collective-permute-done.32.prefix_ref, f32[16]{0:T(128)S(1)} %copy-done.3, f32[24,128]{1,0:T(8,128)S(1)} %collective-permute-done.34.from_west_ref, ...), custom_call_target="tpu_custom_call" | custom-call | tf_op jit(solution)/shard_map/edge_rows/pallas_call | solution.py:43
  20.1 5.2 %collective-permute-start.38 = (f32[12,8,512]{2,1,0:T(8,128)S(1)}, f32[12,8,512]{2,1,0:T(8,128)S(1)}, u32[]{:S(2)}, u32[]{:S(2)}) collective-permute-start(f32[12,8,512]{2,1,0:T(8,128)S(1)} %get-tuple-element.92), channel_id=1, source_target_pairs={{0,2},{2,0},{4,6},{6,4},{1,3},{3,1},{5,7},{7,5},{8,10},{10,8},{12,... | collective-permute-start | bytes 589832 | tf_op jit(solution)/shard_map/ppermute | solution.py:882
  25.3 1.9 %collective-permute-start.39 = (f32[12,8,512]{2,1,0:T(8,128)S(1)}, f32[12,8,512]{2,1,0:T(8,128)S(1)}, u32[]{:S(2)}, u32[]{:S(2)}) collective-permute-start(f32[12,8,512]{2,1,0:T(8,128)S(1)} %get-tuple-element.93), channel_id=1, source_target_pairs={{2,4},{4,2},{3,5},{5,3},{10,12},{12,10},{11,13},{13,11},{18,20},{2... | collective-permute-start | bytes 589832 | tf_op jit(solution)/shard_map/ppermute | solution.py:883
  27.3 2.0 %collective-permute-start.40 = (f32[8,1920]{1,0:T(8,128)S(1)}, f32[8,1920]{1,0:T(8,128)S(1)}, u32[]{:S(2)}, u32[]{:S(2)}) collective-permute-start(f32[8,1920]{1,0:T(8,128)S(1)} %get-tuple-element.95), channel_id=1, source_target_pairs={{0,8},{8,0},{16,24},{24,16},{1,9},{9,1},{17,25},{25,17},{2,10},{10... | collective-permute-start | bytes 184328 | tf_op jit(solution)/shard_map/ppermute | solution.py:834
  29.3 1.6 %first_inside.1 = (f32[5,128,512]{2,1,0:T(8,128)S(1)}, f32[16,1024]{1,0:T(8,128)S(1)}) custom-call(f32[5,128,512]{2,1,0:T(8,128)S(1)} %bitcast.10, s32[128,512]{1,0:T(8,128)S(1)} %bitcast.15, f32[16,512]{1,0:T(8,128)S(1)} %collective-permute-done.32.prefix_ref, f32[16]{0:T(128)S(1)} %copy-done.3, f32[8]{0:T(128)S(1)} %copy-done.4), custom_call_target="tpu_custom_call" | custom-call | tf_op jit(solution)/shard_map/first_inside/pallas_call | solution.py:43
  30.9 0.9 %collective-permute-done.40 = f32[8,1920]{1,0:T(8,128)S(1)} collective-permute-done((f32[8,1920]{1,0:T(8,128)S(1)}, f32[8,1920]{1,0:T(8,128)S(1)}, u32[]{:S(2)}, u32[]{:S(2)}) %collective-permute-start.40) | collective-permute-done | bytes 61472 | tf_op jit(solution)/shard_map/ppermute | solution.py:834
  32.3 2.5 %first_rim.1 = (f32[2,6,8,512]{3,2,1,0:T(8,128)S(1)}, f32[2,16,128]{2,1,0:T(8,128)S(1)}, f32[2,5,8,512]{3,2,1,0:T(8,128)S(1)}, f32[2,16,128]{2,1,0:T(8,128)S(1)}, f32[24,1280]{1,0:T(8,128)S(1)}) custom-call(f32[5,128,512]{2,1,0:T(8,128)S(1)} %bitcast.11, s32[128,512]{1,0:T(8,128)S(1)} %bitcast.16, f32[16,512]{1,0:T(8,128)S(1)} %collective-permute-done.32.prefix_ref, ...), custom_call_target="tpu_custom_call" | custom-call | tf_op jit(solution)/shard_map/first_rim/pallas_call | solution.py:43
  34.8 1.2 %collective-permute-done.41.theirs_ref = f32[8,1920]{1,0:T(8,128)S(1)} collective-permute-done((f32[8,1920]{1,0:T(8,128)S(1)}, f32[8,1920]{1,0:T(8,128)S(1)}, u32[]{:S(2)}, u32[]{:S(2)}) %collective-permute-start.41) | collective-permute-done | bytes 61472 | tf_op jit(solution)/shard_map/ppermute | solution.py:899
  36.0 0.9 %flux_parts.1 = (f32[3,16,512]{2,1,0:T(8,128)S(1)}, f32[8,512]{1,0:T(8,128)S(1)}, f32[16,128]{1,0:T(8,128)S(1)}, f32[24,640]{1,0:T(8,128)S(1)}) custom-call(f32[24,1280]{1,0:T(8,128)S(1)} %get-tuple-element.107.sums_ref, f32[8,1920]{1,0:T(8,128)S(1)} %add.3.mine_ref, f32[8,1920]{1,0:T(8,128)S(1)} %collective-permute-done.41.theirs_ref, s32[2048]{0:T(1024)S(1)} %copy-done.2), custom_call_target="tpu_custom_call" | custom-call | tf_op jit(solution)/shard_map/flux_parts/pallas_call | solution.py:43
  36.9 1.3 %collective-permute-start.42 = (f32[24,640]{1,0:T(8,128)S(1)}, f32[24,640]{1,0:T(8,128)S(1)}, u32[]{:S(2)}, u32[]{:S(2)}) collective-permute-start(f32[24,640]{1,0:T(8,128)S(1)} %get-tuple-element.113), channel_id=1, source_target_pairs={{0,1},{2,3},{4,5},{6,7},{8,9},{10,11},{12,13},{14,15},{16,17},{18,... | collective-permute-start | bytes 184328 | tf_op jit(solution)/shard_map/ppermute | solution.py:927
  38.2 2.8 %second_substep.1 = (f32[5,128,512]{2,1,0:T(8,128)}, f32[2,128,512]{2,1,0:T(8,128)S(1)}) custom-call(f32[5,128,512]{2,1,0:T(8,128)S(1)} %get-tuple-element.98.state_ref, s32[128,512]{1,0:T(8,128)S(1)} %bitcast.17, f32[2,6,8,512]{3,2,1,0:T(8,128)S(1)} %get-tuple-element.103.ring_rows_ref, f32[2,16,128]{2,1,0:T(8,128)S(1)} %get-tuple-element.104.ring_cols_ref, ...), custom_call_target="tpu_custom_call" | custom-call | tf_op jit(solution)/shard_map/second_substep/pallas_call | solution.py:43
  41.0 2.0 %collective-permute-done.42.above_ref = f32[24,640]{1,0:T(8,128)S(1)} collective-permute-done((f32[24,640]{1,0:T(8,128)S(1)}, f32[24,640]{1,0:T(8,128)S(1)}, u32[]{:S(2)}, u32[]{:S(2)}) %collective-permute-start.42) | collective-permute-done | bytes 61472 | tf_op jit(solution)/shard_map/ppermute | solution.py:927
  43.0 1.0 %deeper_pressure.1 = f32[5,128,512]{2,1,0:T(8,128)} custom-call(f32[5,128,512]{2,1,0:T(8,128)} %get-tuple-element.111.out_in_hbm, f32[2,128,512]{2,1,0:T(8,128)S(1)} %get-tuple-element.112.flow_ref, s32[128,512]{1,0:T(8,128)S(1)} %bitcast.18, f32[24,640]{1,0:T(8,128)S(1)} %collective-permute-done.42.above_ref), custom_call_target="tpu_custom_call", output_to_operand_aliasing={{}: (0, {})} | custom-call | tf_op jit(solution)/shard_map/deeper_pressure/pallas_call | solution.py:43
  (30 shorter events, 1.9 us)
Async XLA Ops:
  0.0 3.9 %copy-start.2 = (s32[2048]{0:T(1024)S(1)}, s32[2048]{0:T(1024)}, u32[]{:S(2)}) copy-start(s32[2048]{0:T(1024)} %partner_ref.5) | copy-start | bytes 24580
  0.0 9.0 %copy-start = (f32[5,8,16,512]{3,2,1,0:T(8,128)S(1)}, f32[5,8,16,512]{3,2,1,0:T(8,128)}, u32[]{:S(2)}) copy-start(f32[5,8,16,512]{3,2,1,0:T(8,128)} %param.24) | copy-start | bytes 3932164
  0.0 9.0 %copy-start.1 = (s32[8,16,512]{2,1,0:T(8,128)S(1)}, s32[8,16,512]{2,1,0:T(8,128)}, u32[]{:S(2)}) copy-start(s32[8,16,512]{2,1,0:T(8,128)} %param.25) | copy-start | bytes 786436
  2.5 5.9 %collective-permute-start.33 = (f32[64,1920]{1,0:T(8,128)S(1)}, f32[64,1920]{1,0:T(8,128)S(1)}, u32[]{:S(2)}, u32[]{:S(2)}) collective-permute-start(f32[64,1920]{1,0:T(8,128)S(1)} %get-tuple-element.79), channel_id=1, source_target_pairs={{0,2},{2,0},{4,6},{6,4},{1,3},{3,1},{5,7},{7,5},{8,10},{10,8},{12,... | collective-permute-start | bytes 1474568 | tf_op jit(solution)/shard_map/ppermute | solution.py:825
  2.6 5.8 %collective-permute-start.32 = (f32[16,512]{1,0:T(8,128)S(1)}, f32[16,512]{1,0:T(8,128)S(1)}, u32[]{:S(2)}, u32[]{:S(2)}) collective-permute-start(f32[16,512]{1,0:T(8,128)S(1)} %get-tuple-element.77), channel_id=1, source_target_pairs={{0,1},{2,3},{4,5},{6,7},{8,9},{10,11},{12,13},{14,15},{16,17},{18,... | collective-permute-start | bytes 98312 | tf_op jit(solution)/shard_map/ppermute | solution.py:826
  8.5 8.6 %collective-permute-start.36 = (f32[32,1920]{1,0:T(8,128)S(1)}, f32[32,1920]{1,0:T(8,128)S(1)}, u32[]{:S(2)}, u32[]{:S(2)}) collective-permute-start(f32[32,1920]{1,0:T(8,128)S(1)} %get-tuple-element.83), channel_id=1, source_target_pairs={{0,4},{2,6},{4,0},{6,2},{1,5},{3,7},{5,1},{7,3},{8,12},{10,14},{12... | collective-permute-start | bytes 737288 | tf_op jit(solution)/shard_map/ppermute | solution.py:834
  9.1 10.2 %copy-start.3 = (f32[16]{0:T(128)S(1)}, f32[16]{0:T(128)}, u32[]{:S(2)}) copy-start(f32[16]{0:T(128)} %turn_ref.7) | copy-start | bytes 196
  9.2 1.4 %collective-permute-start.13 = (f32[3,12,8,128]{3,2,1,0:T(8,128)S(1)}, f32[3,12,8,128]{3,2,1,0:T(8,128)S(1)}, u32[]{:S(2)}, u32[]{:S(2)}) collective-permute-start(f32[3,12,8,128]{3,2,1,0:T(8,128)S(1)} %slice.60), channel_id=1, source_target_pairs={{6,14},{14,6},{22,30},{30,22},{7,15},{15,7},{23,31},{31,23}} | collective-permute-start | bytes 442376 | tf_op jit(solution)/shard_map/cond/branch_6_fun/ppermute | solution.py:853
  9.9 0.7 %collective-permute-start.12 = (f32[2,12,8,128]{3,2,1,0:T(8,128)S(1)}, f32[2,12,8,128]{3,2,1,0:T(8,128)S(1)}, u32[]{:S(2)}, u32[]{:S(2)}) collective-permute-start(f32[2,12,8,128]{3,2,1,0:T(8,128)S(1)} %slice.59), channel_id=1, source_target_pairs={{6,6},{14,30},{22,22},{30,14},{7,7},{15,31},{23,23},{31,15}} | collective-permute-start | bytes 294920 | tf_op jit(solution)/shard_map/cond/branch_6_fun/ppermute | solution.py:853
  10.6 18.6 %copy-start.4 = (f32[8]{0:T(128)S(1)}, f32[8]{0:T(128)}, u32[]{:S(2)}) copy-start(f32[8]{0:T(128)} %share_ref.5) | copy-start | bytes 100
  11.4 5.6 %collective-permute-start.34 = (f32[24,128]{1,0:T(8,128)S(1)}, f32[24,128]{1,0:T(8,128)S(1)}, u32[]{:S(2)}, u32[]{:S(2)}) collective-permute-start(f32[24,128]{1,0:T(8,128)S(1)} %get-tuple-element.85.own_east_ref), channel_id=1, source_target_pairs={{0,8},{8,16},{16,24},{24,0},{1,9},{9,17},{17,25},{25,1},{2,10},{10... | collective-permute-start | bytes 36872 | tf_op jit(solution)/shard_map/ppermute | solution.py:868
  13.0 4.0 %collective-permute-start.35 = (f32[24,128]{1,0:T(8,128)S(1)}, f32[24,128]{1,0:T(8,128)S(1)}, u32[]{:S(2)}, u32[]{:S(2)}) collective-permute-start(f32[24,128]{1,0:T(8,128)S(1)} %get-tuple-element.86.own_west_ref), channel_id=1, source_target_pairs={{8,0},{16,8},{24,16},{0,24},{9,1},{17,9},{25,17},{1,25},{10,2},{18... | collective-permute-start | bytes 36872 | tf_op jit(solution)/shard_map/ppermute | solution.py:869
  17.0 10.2 %collective-permute-start.37 = (f32[16,1920]{1,0:T(8,128)S(1)}, f32[16,1920]{1,0:T(8,128)S(1)}, u32[]{:S(2)}, u32[]{:S(2)}) collective-permute-start(f32[16,1920]{1,0:T(8,128)S(1)} %get-tuple-element.89), channel_id=1, source_target_pairs={{0,16},{8,24},{16,0},{24,8},{1,17},{9,25},{17,1},{25,9},{2,18},{10... | collective-permute-start | bytes 368648 | tf_op jit(solution)/shard_map/ppermute | solution.py:834
  20.1 11.8 %collective-permute-start.38 = (f32[12,8,512]{2,1,0:T(8,128)S(1)}, f32[12,8,512]{2,1,0:T(8,128)S(1)}, u32[]{:S(2)}, u32[]{:S(2)}) collective-permute-start(f32[12,8,512]{2,1,0:T(8,128)S(1)} %get-tuple-element.92), channel_id=1, source_target_pairs={{0,2},{2,0},{4,6},{6,4},{1,3},{3,1},{5,7},{7,5},{8,10},{10,8},{12,... | collective-permute-start | bytes 589832 | tf_op jit(solution)/shard_map/ppermute | solution.py:882
  25.3 7.0 %collective-permute-start.39 = (f32[12,8,512]{2,1,0:T(8,128)S(1)}, f32[12,8,512]{2,1,0:T(8,128)S(1)}, u32[]{:S(2)}, u32[]{:S(2)}) collective-permute-start(f32[12,8,512]{2,1,0:T(8,128)S(1)} %get-tuple-element.93), channel_id=1, source_target_pairs={{2,4},{4,2},{3,5},{5,3},{10,12},{12,10},{11,13},{13,11},{18,20},{2... | collective-permute-start | bytes 589832 | tf_op jit(solution)/shard_map/ppermute | solution.py:883
  27.3 4.5 %collective-permute-start.40 = (f32[8,1920]{1,0:T(8,128)S(1)}, f32[8,1920]{1,0:T(8,128)S(1)}, u32[]{:S(2)}, u32[]{:S(2)}) collective-permute-start(f32[8,1920]{1,0:T(8,128)S(1)} %get-tuple-element.95), channel_id=1, source_target_pairs={{0,8},{8,0},{16,24},{24,16},{1,9},{9,1},{17,25},{25,17},{2,10},{10... | collective-permute-start | bytes 184328 | tf_op jit(solution)/shard_map/ppermute | solution.py:834
  31.7 4.3 %collective-permute-start.41 = (f32[8,1920]{1,0:T(8,128)S(1)}, f32[8,1920]{1,0:T(8,128)S(1)}, u32[]{:S(2)}, u32[]{:S(2)}) collective-permute-start(f32[8,1920]{1,0:T(8,128)S(1)} %add.3.mine_ref), channel_id=1, source_target_pairs={{0,1},{1,0},{2,3},{3,2},{4,5},{5,4},{6,7},{7,6},{8,9},{9,8},{10,11... | collective-permute-start | bytes 184328 | tf_op jit(solution)/shard_map/ppermute | solution.py:899
  36.9 6.1 %collective-permute-start.42 = (f32[24,640]{1,0:T(8,128)S(1)}, f32[24,640]{1,0:T(8,128)S(1)}, u32[]{:S(2)}, u32[]{:S(2)}) collective-permute-start(f32[24,640]{1,0:T(8,128)S(1)} %get-tuple-element.113), channel_id=1, source_target_pairs={{0,1},{2,3},{4,5},{6,7},{8,9},{10,11},{12,13},{14,15},{16,17},{18,... | collective-permute-start | bytes 184328 | tf_op jit(solution)/shard_map/ppermute | solution.py:927

commit v4 on v3

--- a/solution.py
+++ b/solution.py
@@ -214,6 +214,15 @@
     )
 
 
+def cell(ref, n):
+    return ref[0:1, n : n + 1]
+
+
+def scalar_of(ref):
+    row = ref[0:1, 0:LANES].astype(F32)
+    return jnp.sum(jnp.where(iota(row.shape, 1) == 0, row, 0.0)).astype(I32)
+
+
 def level_rows(ref, row, rows):
     return jnp.concatenate([ref[k * rows + row : k * rows + row + 1, :] for k in range(DEEP)], axis=0)
 
@@ -276,24 +285,24 @@
 
     @pl.when(lax.axis_index("lat") == n_lat - 1)
     def _():
-        within = partner_ref[0] & (LANES - 1)
+        within = cell(partner_ref, 0) & (LANES - 1)
         sub8, lane8 = iota((DEEP, LANES), 0), iota((DEEP, LANES), 1)
         for out_ref in (west_out_ref, east_out_ref):
             line = jnp.zeros((DEEP, LANES), F32)
             for slab in (0, 2, 4, 6, 8, CORNERS):
                 if out_ref is west_out_ref:
-                    cell = jnp.where(lane8 == within, fold_ref[fold_ref.shape[0] - 1, slab], 0.0)
+                    found = jnp.where(lane8 == within, fold_ref[fold_ref.shape[0] - 1, slab], 0.0)
                 else:
-                    cell = jnp.where(lane8 == within + 1, fold_ref[0, slab], 0.0)
-                    cell = jnp.where((lane8 == 0) & (within == LANES - 1), fold_ref[1, slab], cell)
-                cell = jnp.sum(cell, axis=1, keepdims=True)
+                    found = jnp.where(lane8 == within + 1, fold_ref[0, slab], 0.0)
+                    found = jnp.where(jnp.where(lane8 == 0, within, 0) == LANES - 1, fold_ref[1, slab], found)
+                found = jnp.sum(found, axis=1, keepdims=True)
                 here = (lane8 == ABOVE) & (sub8 == 3) if slab == CORNERS else lane8 == (slab // 2) * DEEP + sub8
-                line = jnp.where(here, -cell if slab < 4 else cell, line)
+                line = jnp.where(here, -found if slab < 4 else found, line)
             out_ref[rows : rows + 1, :] = jnp.sum(line, axis=0, keepdims=True)
 
 
 def corner_slab(out_ref, prefix_ref, turn_ref, from_west_ref, from_east_ref, near, far):
-    out_ref[CORNERS] = jnp.full(out_ref.shape[1:], turn_ref[near], F32)
+    out_ref[CORNERS] = jnp.broadcast_to(cell(turn_ref, near), out_ref.shape[1:])
     out_ref[CORNERS, 0:1, 0:LANES] = from_west_ref[near : near + 1, :]
     out_ref[CORNERS, 1:2, 0:LANES] = from_east_ref[near : near + 1, :]
     out_ref[CORNERS, 3:4, :] = prefix_ref[near : near + 1, :]
@@ -388,7 +397,7 @@
     row = iota((rows, LANES), 0)
     column = jnp.zeros((rows, LANES), F32)
     for j in range(rows):
-        column = jnp.where(row == j, turn_ref[j], column)
+        column = jnp.where(row == j, cell(turn_ref, j), column)
     return column
 
 
@@ -458,7 +467,7 @@
                 above_x + slopes[0],
                 above_y + slopes[1],
                 total + buoyancy_of(new[2], new[3]),
-                absorbed + wet * share_ref[k],
+                absorbed + wet * cell(share_ref, k),
             ]
     for r, j in grid:
         for kind in range(2):
@@ -474,7 +483,7 @@
     rows, cols = prefix_ref.shape
     lat = lax.axis_index("lat")
     odd = lax.rem(lat, 2) == 1
-    within = partner_ref[0] & (LANES - 1)
+    within = scalar_of(partner_ref) & (LANES - 1)
     at_top = lat == n_lat - 1
 
     @pl.when(odd)
@@ -510,7 +519,7 @@
             north_ref[slab] = mirrored(row, cols)
         north_ref[CORNERS, 0:1, 0:LANES] = from_west_ref[rows : rows + 1, :]
         north_ref[CORNERS, 1:2, 0:LANES] = from_east_ref[rows : rows + 1, :]
-        north_ref[CORNERS, 2:3, :] = jnp.full((1, cols), turn_ref[rows - 1], F32)
+        north_ref[CORNERS, 2:3, :] = jnp.broadcast_to(cell(turn_ref, rows - 1), (1, cols))
 
     wide = cols + LANES
     sums_ref[rows:, :] = jnp.zeros((DEEP, 2 * wide), F32)
@@ -519,7 +528,7 @@
 
     share_down = jnp.zeros((DEEP, LANES), F32)
     for k in range(DEEP):
-        share_down = jnp.where(sub8 == k, share_ref[k], share_down)
+        share_down = jnp.where(sub8 == k, cell(share_ref, k), share_down)
 
     def down(line, f):
         return jnp.sum(jnp.where(lane8 == f * DEEP + sub8, line, 0.0), axis=1, keepdims=True)
@@ -563,7 +572,7 @@
         wet = level_rows(mask_ref, edge, rows).astype(F32)
         edge_line = slice(edge, edge + 1)
         new = row_step(
-            own, south, north, from_west_ref[edge_line, :], from_east_ref[edge_line, :], wet, turn_ref[edge],
+            own, south, north, from_west_ref[edge_line, :], from_east_ref[edge_line, :], wet, cell(turn_ref, edge),
             above_own, above_south, above_north,
         )
         for f in range(5):
@@ -579,7 +588,7 @@
     turn = turn_column(turn_ref, rows)
     share_lanes = jnp.zeros((rows, LANES), F32)
     for k in range(DEEP):
-        share_lanes = jnp.where((lane & 7) == k, share_ref[k], share_lanes)
+        share_lanes = jnp.where((lane & 7) == k, cell(share_ref, k), share_lanes)
 
     def column_step(near, east, west, north, south):
         dx, dy = 0.5 * (east - west), 0.5 * (north - south)
@@ -629,8 +638,7 @@
     first = lax.axis_index("lev") == 0
     halves = (jnp.where(first, mine, theirs), jnp.where(first, theirs, mine))
     at_top = lax.axis_index("lat") == n_lat - 1
-    hinge = partner_ref[0]
-    within = hinge - (hinge // cols) * cols
+    within = scalar_of(partner_ref) & (cols - 1)
 
     def extra(kind, c):
         found = []
@@ -693,8 +701,8 @@
     share_down = jnp.zeros((DEEP, LANES), F32)
     share_lanes = jnp.zeros((rows, LANES), F32)
     for k in range(DEEP):
-        share_down = jnp.where(sub8 == k, share_ref[k], share_down)
-        share_lanes = jnp.where((lane & 7) == k, share_ref[k], share_lanes)
+        share_down = jnp.where(sub8 == k, cell(share_ref, k), share_down)
+        share_lanes = jnp.where((lane & 7) == k, cell(share_ref, k), share_lanes)
 
     ring_rows, ring_cols = [], []
     for side in range(2):
@@ -726,7 +734,7 @@
         for r, j in grid:
             at = tile(r, j, k, rows)
             wet = mask_ref[at].astype(F32)
-            taken = wet * share_ref[k]
+            taken = wet * cell(share_ref, k)
             wets[r, j] = wet
             heats[r, j] = [taken * cut(flux_ref[c], r, j) for c in range(3)]
             for f in range(5):
@@ -811,6 +819,7 @@
     flat_state = state.reshape(fields, levels * rows, cols)
     flat_mask = mask.reshape(levels * rows, cols)
     last = n_lat - 1
+    turn, share, hinge = coriolis.reshape(1, -1), penetration.reshape(1, -1), fold_partner.reshape(1, -1)
 
     keep, send, west, east, total = prepare(
         flat_state, flat_mask, flux_tiles, flux_owner, flux_row, fold_partner, n_lon, n_lat
@@ -861,8 +870,8 @@
     west, east = call(
         functools.partial(columns_kernel, n_lat),
         (side, side),
-        [VMEM] * 4 + [SMEM],
-        (west, east, prefix, fold, fold_partner),
+        [VMEM] * 4 + [VMEM],
+        (west, east, prefix, fold, hinge),
         name="edge_columns",
     )
     from_west = lax.ppermute(east, "lon", [(i, (i + 1) % n_lon) for i in range(n_lon)])
@@ -875,8 +884,8 @@
     pair, cross = call(
         rows_kernel,
         (message, message),
-        [VMEM, VMEM, VMEM, SMEM, VMEM, VMEM],
-        (flat_state, flat_mask, prefix, coriolis, from_west, from_east),
+        [VMEM, VMEM, VMEM, VMEM, VMEM, VMEM],
+        (flat_state, flat_mask, prefix, turn, from_west, from_east),
         name="edge_rows",
     )
     from_pair = lax.ppermute(pair, "lat", [(i, i ^ 1) for i in range(n_lat)])
@@ -890,8 +899,8 @@
     new_state, inside = call(
         inside_kernel,
         (shape(fields, levels * rows, cols), shape(rows, 2 * cols)),
-        [VMEM, VMEM, VMEM, SMEM, SMEM],
-        (near_state, near_mask, prefix, coriolis, penetration),
+        [VMEM, VMEM, VMEM, VMEM, VMEM],
+        (near_state, near_mask, prefix, turn, share),
         name="first_inside",
     )
     keep = after(keep, inside)
@@ -909,9 +918,9 @@
             shape(2, rows, LANES),
             shape(rows + DEEP, 2 * wide),
         ),
-        [VMEM, VMEM, VMEM, SMEM, SMEM, SMEM] + [VMEM] * 8,
+        [VMEM, VMEM, VMEM, VMEM, VMEM, VMEM] + [VMEM] * 8,
         (
-            flat_state, flat_mask, prefix, coriolis, penetration, fold_partner, west, east, from_west, from_east, from_pair,
+            flat_state, flat_mask, prefix, turn, share, hinge, west, east, from_west, from_east, from_pair,
             from_cross, fold, inside,
         ),
         [pltpu.VMEM((SLABS + 1, DEEP, cols), F32), pltpu.VMEM((SLABS + 1, DEEP, cols), F32)],
@@ -920,8 +929,8 @@
     *flux, above = call(
         functools.partial(flux_kernel, n_lat),
         (shape(3, rows, cols), shape(DEEP, cols), shape(rows, LANES), shape(rows + DEEP, wide)),
-        [VMEM] * 3 + [SMEM],
-        (sums, mine, theirs, fold_partner),
+        [VMEM] * 3 + [VMEM],
+        (sums, mine, theirs, hinge),
         name="flux_parts",
     )
     above = lax.ppermute(above, "lev", [(0, 1)])
@@ -930,8 +939,8 @@
     result, flow = call(
         second_kernel,
         (out, shape(2, levels * rows, cols)),
-        [VMEM] * 9 + [SMEM] * 2,
-        (new_state, flat_mask, *ring, *flux, coriolis, penetration),
+        [VMEM] * 9 + [VMEM] * 2,
+        (new_state, flat_mask, *ring, *flux, turn, share),
         [pltpu.VMEM((3, levels * rows, cols), F32), pltpu.SemaphoreType.DMA((DEEP,))],
         name="second_substep",
         out_specs=(ANY, VMEM),

time: 44.6 us -> 43.3 us (0.971)
  Pallas kernels: 12.9 us -> 9.73 us
  waiting for transfers between devices: 9.68 us -> 11.5 us
    pallas_call x12, Pallas kernels: 12.9 us -> 9.73 us  [call(): pl.pallas_call(kernel, out_shape=out_shape, in_specs=in_specs, out_specs=...]
    ppermute x3, waiting for transfers between devices: 0.87 us -> 1.85 us  [passed_on(): return lax.ppermute(send, axis, [(i, i ^ bit) for i in range(size)])]
    ppermute x1, waiting for transfers between devices: 1.22 us -> 2.07 us  [body(): theirs = lax.ppermute(mine, 'lev', [(0, 1), (1, 0)])]
    ppermute x1, starting transfers between devices: 5.25 us -> 5.7 us  [body(): from_pair = lax.ppermute(pair, 'lat', [(i, i ^ 1) for i in range(n_lat)])]
  transfers between devices with their start and end apart: 13 -> 13, of which waited for: 6 -> 6; matrix products, arithmetic and copies ran while one was open for 1% -> 1% of each run, Pallas kernels for 19% -> 14%
where the time goes in v4:
time: 43.3 us; the launch traced here: 43 us
  starting transfers between devices  20.3 us (47%)
  waiting for transfers between devices  11.5 us (27%)
  Pallas kernels  9.73 us (22%)
  between operations  0.81 us (2%)
  local copies, waits for them, and re-layouts  0.56 us (1%)
    pallas_call x12, Pallas kernels, call(): pl.pallas_call(kernel, out_shape=out_shape, in_specs=in_specs, out_specs=...  9.73 us
    ppermute x1, starting transfers between devices, body(): from_pair = lax.ppermute(pair, 'lat', [(i, i ^ 1) for i in range(n_lat)])  5.7 us
    ppermute x3, starting transfers between devices, passed_on(): return lax.ppermute(send, axis, [(i, i ^ bit) for i in range(size)])  4.76 us
    ppermute x1, waiting for transfers between devices, body(): prefix = lax.ppermute(total, 'lev', [(0, 1)])  3.33 us
    ppermute x1, waiting for transfers between devices, body(): above = lax.ppermute(above, 'lev', [(0, 1)])  2.41 us
    ppermute x1, starting transfers between devices, body(): lax.ppermute(west, 'lon', [((i + 1) % n_lon, i) for i in range(n_lon)])  2.24 us
    ppermute x1, waiting for transfers between devices, body(): theirs = lax.ppermute(mine, 'lev', [(0, 1), (1, 0)])  2.07 us
    ppermute x1, starting transfers between devices, body(): lax.ppermute(cross, 'lat', [(i, i + 1 if i % 2 else i - 1) for i in range...  1.91 us
  transfers between devices with their start and end apart: 13, of which 6 were waited for; matrix products, arithmetic and copies ran while one was open for 1% of the time, Pallas kernels for 14%

profile of v4, /device:TPU:6, one launch (start us, length us, event | category | flops | bytes accessed | tf_op | source)
XLA Modules:
  0.0 43.0 jit_solution(14993907025442474934)
XLA Ops:
  0.0 2.5 %prepare.1 = (f32[64,1920]{1,0:T(8,128)S(1)}, f32[64,1920]{1,0:T(8,128)S(1)}, f32[16,128]{1,0:T(8,128)S(1)}, f32[16,128]{1,0:T(8,128)S(1)}, f32[16,512]{1,0:T(8,128)S(1)}) custom-call(f32[5,128,512]{2,1,0:T(8,128)} %bitcast.10, s32[128,512]{1,0:T(8,128)} %bitcast.15, f32[3,128,512]{2,1,0:T(8,128)} %bitcast.32, s32[1,128]{1,0:T(1,128)} %bitcast.33, ...), custom_call_target="tpu_custom_call" | custom-call | tf_op jit(solution)/shard_map/prepare/pallas_call | solution.py:43
  2.6 1.3 %collective-permute-start.32 = (f32[16,512]{1,0:T(8,128)S(1)}, f32[16,512]{1,0:T(8,128)S(1)}, u32[]{:S(2)}, u32[]{:S(2)}) collective-permute-start(f32[16,512]{1,0:T(8,128)S(1)} %get-tuple-element.77), channel_id=1, source_target_pairs={{0,1},{2,3},{4,5},{6,7},{8,9},{10,11},{12,13},{14,15},{16,17},{18,... | collective-permute-start | bytes 98312 | tf_op jit(solution)/shard_map/ppermute | solution.py:835
  3.9 0.5 %slice.75 = s32[1]{0:T(128)} slice(s32[2048]{0:T(1024)S(1)} %copy-done.2), slice={[0:1]} | slice | bytes 8 | tf_op jit(solution)/shard_map/slice | solution.py:846
  5.1 3.3 %collective-permute-done.32.prefix_ref = f32[16,512]{1,0:T(8,128)S(1)} collective-permute-done((f32[16,512]{1,0:T(8,128)S(1)}, f32[16,512]{1,0:T(8,128)S(1)}, u32[]{:S(2)}, u32[]{:S(2)}) %collective-permute-start.32) | collective-permute-done | bytes 32800 | tf_op jit(solution)/shard_map/ppermute | solution.py:835
  8.5 0.6 %collective-permute-start.36 = (f32[32,1920]{1,0:T(8,128)S(1)}, f32[32,1920]{1,0:T(8,128)S(1)}, u32[]{:S(2)}, u32[]{:S(2)}) collective-permute-start(f32[32,1920]{1,0:T(8,128)S(1)} %get-tuple-element.83), channel_id=1, source_target_pairs={{0,4},{2,6},{4,0},{6,2},{1,5},{3,7},{5,1},{7,3},{8,12},{10,14},{12... | collective-permute-start | bytes 737288 | tf_op jit(solution)/shard_map/ppermute | solution.py:843
  9.1 1.5 %conditional.1 = (f32[5,12,8,128]{3,2,1,0:T(8,128)S(1)}) conditional(s32[]{:T(128)} %clamp.3, f32[4,12,8,128]{3,2,1,0:T(8,128)S(1)} %top_rows.1, f32[4,12,8,128]{3,2,1,0:T(8,128)S(1)} %top_rows.1, f32[4,12,8,128]{3,2,1,0:T(8,128)S(1)} %top_rows.1, f32[4,12,8,128]{3,2,1,0:T(8,128)S(1)} %top_rows.1, ...), branch_computations={%region_0.0_spmd, %region_1.0_spmd, %region_2.0_spmd, %region_3.0_... | conditional | flops 61440 | bytes 1966168 | solution.py:868
  9.2 0.7 %collective-permute-start.5 = (f32[3,12,8,128]{3,2,1,0:T(8,128)S(1)}, f32[3,12,8,128]{3,2,1,0:T(8,128)S(1)}, u32[]{:S(2)}, u32[]{:S(2)}) collective-permute-start(f32[3,12,8,128]{3,2,1,0:T(8,128)S(1)} %slice.54), channel_id=1, source_target_pairs={{6,6},{14,30},{22,22},{30,14},{7,7},{15,31},{23,23},{31,15}} | collective-permute-start | bytes 442376 | tf_op jit(solution)/shard_map/cond/branch_2_fun/ppermute | solution.py:862
  9.9 0.7 %collective-permute-start.4 = (f32[2,12,8,128]{3,2,1,0:T(8,128)S(1)}, f32[2,12,8,128]{3,2,1,0:T(8,128)S(1)}, u32[]{:S(2)}, u32[]{:S(2)}) collective-permute-start(f32[2,12,8,128]{3,2,1,0:T(8,128)S(1)} %slice.53), channel_id=1, source_target_pairs={{6,30},{14,22},{22,14},{30,6},{7,31},{15,23},{23,15},{31,7}} | collective-permute-start | bytes 294920 | tf_op jit(solution)/shard_map/cond/branch_2_fun/ppermute | solution.py:862
  10.7 1.6 %collective-permute-start.34 = (f32[24,128]{1,0:T(8,128)S(1)}, f32[24,128]{1,0:T(8,128)S(1)}, u32[]{:S(2)}, u32[]{:S(2)}) collective-permute-start(f32[24,128]{1,0:T(8,128)S(1)} %get-tuple-element.85.own_east_ref), channel_id=1, source_target_pairs={{0,8},{8,16},{16,24},{24,0},{1,9},{9,17},{17,25},{25,1},{2,10},{10... | collective-permute-start | bytes 36872 | tf_op jit(solution)/shard_map/ppermute | solution.py:877
  12.3 2.2 %collective-permute-start.35 = (f32[24,128]{1,0:T(8,128)S(1)}, f32[24,128]{1,0:T(8,128)S(1)}, u32[]{:S(2)}, u32[]{:S(2)}) collective-permute-start(f32[24,128]{1,0:T(8,128)S(1)} %get-tuple-element.86.own_west_ref), channel_id=1, source_target_pairs={{8,0},{16,8},{24,16},{0,24},{9,1},{17,9},{25,17},{1,25},{10,2},{18... | collective-permute-start | bytes 36872 | tf_op jit(solution)/shard_map/ppermute | solution.py:878
  14.5 1.8 %collective-permute-done.34.from_west_ref = f32[24,128]{1,0:T(8,128)S(1)} collective-permute-done((f32[24,128]{1,0:T(8,128)S(1)}, f32[24,128]{1,0:T(8,128)S(1)}, u32[]{:S(2)}, u32[]{:S(2)}) %collective-permute-start.34) | collective-permute-done | bytes 12320 | tf_op jit(solution)/shard_map/ppermute | solution.py:877
  16.4 2.3 %collective-permute-start.37 = (f32[16,1920]{1,0:T(8,128)S(1)}, f32[16,1920]{1,0:T(8,128)S(1)}, u32[]{:S(2)}, u32[]{:S(2)}) collective-permute-start(f32[16,1920]{1,0:T(8,128)S(1)} %get-tuple-element.89), channel_id=1, source_target_pairs={{0,16},{8,24},{16,0},{24,8},{1,17},{9,25},{17,1},{25,9},{2,18},{10... | collective-permute-start | bytes 368648 | tf_op jit(solution)/shard_map/ppermute | solution.py:843
  18.8 5.7 %collective-permute-start.38 = (f32[12,8,512]{2,1,0:T(8,128)S(1)}, f32[12,8,512]{2,1,0:T(8,128)S(1)}, u32[]{:S(2)}, u32[]{:S(2)}) collective-permute-start(f32[12,8,512]{2,1,0:T(8,128)S(1)} %get-tuple-element.92), channel_id=1, source_target_pairs={{0,2},{2,0},{4,6},{6,4},{1,3},{3,1},{5,7},{7,5},{8,10},{10,8},{12,... | collective-permute-start | bytes 589832 | tf_op jit(solution)/shard_map/ppermute | solution.py:891
  24.5 1.9 %collective-permute-start.39 = (f32[12,8,512]{2,1,0:T(8,128)S(1)}, f32[12,8,512]{2,1,0:T(8,128)S(1)}, u32[]{:S(2)}, u32[]{:S(2)}) collective-permute-start(f32[12,8,512]{2,1,0:T(8,128)S(1)} %get-tuple-element.93), channel_id=1, source_target_pairs={{2,4},{4,2},{3,5},{5,3},{10,12},{12,10},{11,13},{13,11},{18,20},{2... | collective-permute-start | bytes 589832 | tf_op jit(solution)/shard_map/ppermute | solution.py:892
  26.5 1.9 %collective-permute-start.40 = (f32[8,1920]{1,0:T(8,128)S(1)}, f32[8,1920]{1,0:T(8,128)S(1)}, u32[]{:S(2)}, u32[]{:S(2)}) collective-permute-start(f32[8,1920]{1,0:T(8,128)S(1)} %get-tuple-element.95), channel_id=1, source_target_pairs={{0,8},{8,0},{16,24},{24,16},{1,9},{9,1},{17,25},{25,17},{2,10},{10... | collective-permute-start | bytes 184328 | tf_op jit(solution)/shard_map/ppermute | solution.py:843
  28.4 1.1 %first_inside.1 = (f32[5,128,512]{2,1,0:T(8,128)S(1)}, f32[16,1024]{1,0:T(8,128)S(1)}) custom-call(f32[5,128,512]{2,1,0:T(8,128)S(1)} %bitcast.13, s32[128,512]{1,0:T(8,128)S(1)} %bitcast.18, f32[16,512]{1,0:T(8,128)S(1)} %collective-permute-done.32.prefix_ref, f32[1,16]{1,0:T(1,128)S(1)} %bitcast.26, f32[1,8]{1,0:T(1,128)S(1)} %bitcast.29), custom_call_target="tpu_custom_call" | custom-call | tf_op jit(solution)/shard_map/first_inside/pallas_call | solution.py:43
  29.5 1.8 %collective-permute-done.40 = f32[8,1920]{1,0:T(8,128)S(1)} collective-permute-done((f32[8,1920]{1,0:T(8,128)S(1)}, f32[8,1920]{1,0:T(8,128)S(1)}, u32[]{:S(2)}, u32[]{:S(2)}) %collective-permute-start.40) | collective-permute-done | bytes 61472 | tf_op jit(solution)/shard_map/ppermute | solution.py:843
  31.5 2.1 %first_rim.1 = (f32[2,6,8,512]{3,2,1,0:T(8,128)S(1)}, f32[2,16,128]{2,1,0:T(8,128)S(1)}, f32[2,5,8,512]{3,2,1,0:T(8,128)S(1)}, f32[2,16,128]{2,1,0:T(8,128)S(1)}, f32[24,1280]{1,0:T(8,128)S(1)}) custom-call(f32[5,128,512]{2,1,0:T(8,128)S(1)} %bitcast.14, s32[128,512]{1,0:T(8,128)S(1)} %bitcast.19, f32[16,512]{1,0:T(8,128)S(1)} %collective-permute-done.32.prefix_ref, ...), custom_call_target="tpu_custom_call" | custom-call | tf_op jit(solution)/shard_map/first_rim/pallas_call | solution.py:43
  33.6 2.1 %collective-permute-done.41.theirs_ref = f32[8,1920]{1,0:T(8,128)S(1)} collective-permute-done((f32[8,1920]{1,0:T(8,128)S(1)}, f32[8,1920]{1,0:T(8,128)S(1)}, u32[]{:S(2)}, u32[]{:S(2)}) %collective-permute-start.41) | collective-permute-done | bytes 61472 | tf_op jit(solution)/shard_map/ppermute | solution.py:908
  35.6 0.3 flux_parts.1
  35.9 1.3 %collective-permute-start.42 = (f32[24,640]{1,0:T(8,128)S(1)}, f32[24,640]{1,0:T(8,128)S(1)}, u32[]{:S(2)}, u32[]{:S(2)}) collective-permute-start(f32[24,640]{1,0:T(8,128)S(1)} %get-tuple-element.113), channel_id=1, source_target_pairs={{0,1},{2,3},{4,5},{6,7},{8,9},{10,11},{12,13},{14,15},{16,17},{18,... | collective-permute-start | bytes 184328 | tf_op jit(solution)/shard_map/ppermute | solution.py:936
  37.2 2.4 %second_substep.1 = (f32[5,128,512]{2,1,0:T(8,128)}, f32[2,128,512]{2,1,0:T(8,128)S(1)}) custom-call(f32[5,128,512]{2,1,0:T(8,128)S(1)} %get-tuple-element.98.state_ref, s32[128,512]{1,0:T(8,128)S(1)} %bitcast.20, f32[2,6,8,512]{3,2,1,0:T(8,128)S(1)} %get-tuple-element.103.ring_rows_ref, f32[2,16,128]{2,1,0:T(8,128)S(1)} %get-tuple-element.104.ring_cols_ref, ...), custom_call_target="tpu_custom_call" | custom-call | tf_op jit(solution)/shard_map/second_substep/pallas_call | solution.py:43
  39.6 2.4 %collective-permute-done.42.above_ref = f32[24,640]{1,0:T(8,128)S(1)} collective-permute-done((f32[24,640]{1,0:T(8,128)S(1)}, f32[24,640]{1,0:T(8,128)S(1)}, u32[]{:S(2)}, u32[]{:S(2)}) %collective-permute-start.42) | collective-permute-done | bytes 61472 | tf_op jit(solution)/shard_map/ppermute | solution.py:936
  42.0 1.0 %deeper_pressure.1 = f32[5,128,512]{2,1,0:T(8,128)} custom-call(f32[5,128,512]{2,1,0:T(8,128)} %get-tuple-element.111.out_in_hbm, f32[2,128,512]{2,1,0:T(8,128)S(1)} %get-tuple-element.112.flow_ref, s32[128,512]{1,0:T(8,128)S(1)} %bitcast.21, f32[24,640]{1,0:T(8,128)S(1)} %collective-permute-done.42.above_ref), custom_call_target="tpu_custom_call", output_to_operand_aliasing={{}: (0, {})} | custom-call | tf_op jit(solution)/shard_map/deeper_pressure/pallas_call | solution.py:43
  (30 shorter events, 0.7 us)
Async XLA Ops:
  0.0 3.9 %copy-start.2 = (s32[2048]{0:T(1024)S(1)}, s32[2048]{0:T(1024)}, u32[]{:S(2)}) copy-start(s32[2048]{0:T(1024)} %partner_hbm.1) | copy-start | bytes 24580
  0.0 9.0 %copy-start = (f32[5,8,16,512]{3,2,1,0:T(8,128)S(1)}, f32[5,8,16,512]{3,2,1,0:T(8,128)}, u32[]{:S(2)}) copy-start(f32[5,8,16,512]{3,2,1,0:T(8,128)} %param.24) | copy-start | bytes 3932164
  0.0 9.0 %copy-start.1 = (s32[8,16,512]{2,1,0:T(8,128)S(1)}, s32[8,16,512]{2,1,0:T(8,128)}, u32[]{:S(2)}) copy-start(s32[8,16,512]{2,1,0:T(8,128)} %param.25) | copy-start | bytes 786436
  2.5 5.9 %collective-permute-start.33 = (f32[64,1920]{1,0:T(8,128)S(1)}, f32[64,1920]{1,0:T(8,128)S(1)}, u32[]{:S(2)}, u32[]{:S(2)}) collective-permute-start(f32[64,1920]{1,0:T(8,128)S(1)} %get-tuple-element.79), channel_id=1, source_target_pairs={{0,2},{2,0},{4,6},{6,4},{1,3},{3,1},{5,7},{7,5},{8,10},{10,8},{12,... | collective-permute-start | bytes 1474568 | tf_op jit(solution)/shard_map/ppermute | solution.py:834
  2.6 5.8 %collective-permute-start.32 = (f32[16,512]{1,0:T(8,128)S(1)}, f32[16,512]{1,0:T(8,128)S(1)}, u32[]{:S(2)}, u32[]{:S(2)}) collective-permute-start(f32[16,512]{1,0:T(8,128)S(1)} %get-tuple-element.77), channel_id=1, source_target_pairs={{0,1},{2,3},{4,5},{6,7},{8,9},{10,11},{12,13},{14,15},{16,17},{18,... | collective-permute-start | bytes 98312 | tf_op jit(solution)/shard_map/ppermute | solution.py:835
  8.5 7.9 %collective-permute-start.36 = (f32[32,1920]{1,0:T(8,128)S(1)}, f32[32,1920]{1,0:T(8,128)S(1)}, u32[]{:S(2)}, u32[]{:S(2)}) collective-permute-start(f32[32,1920]{1,0:T(8,128)S(1)} %get-tuple-element.83), channel_id=1, source_target_pairs={{0,4},{2,6},{4,0},{6,2},{1,5},{3,7},{5,1},{7,3},{8,12},{10,14},{12... | collective-permute-start | bytes 737288 | tf_op jit(solution)/shard_map/ppermute | solution.py:843
  9.1 9.6 %copy-start.3 = (f32[16]{0:T(128)S(1)}, f32[16]{0:T(128)}, u32[]{:S(2)}) copy-start(f32[16]{0:T(128)} %param.26) | copy-start | bytes 196
  9.2 1.4 %collective-permute-start.5 = (f32[3,12,8,128]{3,2,1,0:T(8,128)S(1)}, f32[3,12,8,128]{3,2,1,0:T(8,128)S(1)}, u32[]{:S(2)}, u32[]{:S(2)}) collective-permute-start(f32[3,12,8,128]{3,2,1,0:T(8,128)S(1)} %slice.54), channel_id=1, source_target_pairs={{6,6},{14,30},{22,22},{30,14},{7,7},{15,31},{23,23},{31,15}} | collective-permute-start | bytes 442376 | tf_op jit(solution)/shard_map/cond/branch_2_fun/ppermute | solution.py:862
  9.9 0.7 %collective-permute-start.4 = (f32[2,12,8,128]{3,2,1,0:T(8,128)S(1)}, f32[2,12,8,128]{3,2,1,0:T(8,128)S(1)}, u32[]{:S(2)}, u32[]{:S(2)}) collective-permute-start(f32[2,12,8,128]{3,2,1,0:T(8,128)S(1)} %slice.53), channel_id=1, source_target_pairs={{6,30},{14,22},{22,14},{30,6},{7,31},{15,23},{23,15},{31,7}} | collective-permute-start | bytes 294920 | tf_op jit(solution)/shard_map/cond/branch_2_fun/ppermute | solution.py:862
  10.6 17.8 %copy-start.4 = (f32[8]{0:T(128)S(1)}, f32[8]{0:T(128)}, u32[]{:S(2)}) copy-start(f32[8]{0:T(128)} %param.27) | copy-start | bytes 100
  10.7 5.6 %collective-permute-start.34 = (f32[24,128]{1,0:T(8,128)S(1)}, f32[24,128]{1,0:T(8,128)S(1)}, u32[]{:S(2)}, u32[]{:S(2)}) collective-permute-start(f32[24,128]{1,0:T(8,128)S(1)} %get-tuple-element.85.own_east_ref), channel_id=1, source_target_pairs={{0,8},{8,16},{16,24},{24,0},{1,9},{9,17},{17,25},{25,1},{2,10},{10... | collective-permute-start | bytes 36872 | tf_op jit(solution)/shard_map/ppermute | solution.py:877
  12.3 4.1 %collective-permute-start.35 = (f32[24,128]{1,0:T(8,128)S(1)}, f32[24,128]{1,0:T(8,128)S(1)}, u32[]{:S(2)}, u32[]{:S(2)}) collective-permute-start(f32[24,128]{1,0:T(8,128)S(1)} %get-tuple-element.86.own_west_ref), channel_id=1, source_target_pairs={{8,0},{16,8},{24,16},{0,24},{9,1},{17,9},{25,17},{1,25},{10,2},{18... | collective-permute-start | bytes 36872 | tf_op jit(solution)/shard_map/ppermute | solution.py:878
  16.4 10.1 %collective-permute-start.37 = (f32[16,1920]{1,0:T(8,128)S(1)}, f32[16,1920]{1,0:T(8,128)S(1)}, u32[]{:S(2)}, u32[]{:S(2)}) collective-permute-start(f32[16,1920]{1,0:T(8,128)S(1)} %get-tuple-element.89), channel_id=1, source_target_pairs={{0,16},{8,24},{16,0},{24,8},{1,17},{9,25},{17,1},{25,9},{2,18},{10... | collective-permute-start | bytes 368648 | tf_op jit(solution)/shard_map/ppermute | solution.py:843
  18.8 12.6 %collective-permute-start.38 = (f32[12,8,512]{2,1,0:T(8,128)S(1)}, f32[12,8,512]{2,1,0:T(8,128)S(1)}, u32[]{:S(2)}, u32[]{:S(2)}) collective-permute-start(f32[12,8,512]{2,1,0:T(8,128)S(1)} %get-tuple-element.92), channel_id=1, source_target_pairs={{0,2},{2,0},{4,6},{6,4},{1,3},{3,1},{5,7},{7,5},{8,10},{10,8},{12,... | collective-permute-start | bytes 589832 | tf_op jit(solution)/shard_map/ppermute | solution.py:891
  24.5 7.0 %collective-permute-start.39 = (f32[12,8,512]{2,1,0:T(8,128)S(1)}, f32[12,8,512]{2,1,0:T(8,128)S(1)}, u32[]{:S(2)}, u32[]{:S(2)}) collective-permute-start(f32[12,8,512]{2,1,0:T(8,128)S(1)} %get-tuple-element.93), channel_id=1, source_target_pairs={{2,4},{4,2},{3,5},{5,3},{10,12},{12,10},{11,13},{13,11},{18,20},{2... | collective-permute-start | bytes 589832 | tf_op jit(solution)/shard_map/ppermute | solution.py:892
  26.5 4.9 %collective-permute-start.40 = (f32[8,1920]{1,0:T(8,128)S(1)}, f32[8,1920]{1,0:T(8,128)S(1)}, u32[]{:S(2)}, u32[]{:S(2)}) collective-permute-start(f32[8,1920]{1,0:T(8,128)S(1)} %get-tuple-element.95), channel_id=1, source_target_pairs={{0,8},{8,0},{16,24},{24,16},{1,9},{9,1},{17,25},{25,17},{2,10},{10... | collective-permute-start | bytes 184328 | tf_op jit(solution)/shard_map/ppermute | solution.py:843
  31.4 4.3 %collective-permute-start.41 = (f32[8,1920]{1,0:T(8,128)S(1)}, f32[8,1920]{1,0:T(8,128)S(1)}, u32[]{:S(2)}, u32[]{:S(2)}) collective-permute-start(f32[8,1920]{1,0:T(8,128)S(1)} %add.3.mine_ref), channel_id=1, source_target_pairs={{0,1},{1,0},{2,3},{3,2},{4,5},{5,4},{6,7},{7,6},{8,9},{9,8},{10,11... | collective-permute-start | bytes 184328 | tf_op jit(solution)/shard_map/ppermute | solution.py:908
  35.9 6.1 %collective-permute-start.42 = (f32[24,640]{1,0:T(8,128)S(1)}, f32[24,640]{1,0:T(8,128)S(1)}, u32[]{:S(2)}, u32[]{:S(2)}) collective-permute-start(f32[24,640]{1,0:T(8,128)S(1)} %get-tuple-element.113), channel_id=1, source_target_pairs={{0,1},{2,3},{4,5},{6,7},{8,9},{10,11},{12,13},{14,15},{16,17},{18,... | collective-permute-start | bytes 184328 | tf_op jit(solution)/shard_map/ppermute | solution.py:936
